TPU v7x, 512 devices: a whole 4x8x8 slice. The times are simulated.
512 devices in a mesh: exp: 32 (over y_hi, z, core), pix: 16 (over x, y_lo).
Axes of the slice: x: 4, y: 8 (y_hi: 2, y_lo: 4; y = y_hi * 4 + y_lo), z: 8, core: 2. Of those that a mesh axis runs over, the one named last changes fastest.
Arguments:
- transmission: bfloat16 [16384, 24576], P('exp', 'pix'), may hold values from 0.29882812 to 1
- inverse_var: bfloat16 [16384, 24576], P('exp', 'pix'), may hold values from 0.25 to 4
- pixel_mask: int32 [16384, 192], P('exp', 'pix'), may hold values 0 or 1
- coef: bfloat16 [16384, 256], P('exp'), may hold values from -6 to 6
- basis: bfloat16 [256, 24576], P(None, 'pix'), may hold values from -6 to 6
- coef_tangent: bfloat16 [16384, 256], P('exp', 'pix'), may hold values from -0.375 to 0.375
- basis_tangent: bfloat16 [256, 24576], P('exp', 'pix'), may hold values from -0.375 to 0.375
Outputs:
- coef_grad: float32 [16384, 256], P('exp', 'pix')
- basis_grad: float32 [256, 24576], P('exp', 'pix')
All inputs are finite; a program needn't handle non-finite values. No bound on the sum of `pixel_mask` on one device may be relied on, other than what follows from the above.
Results may differ from a plain program's by a relative error of at most 0.0008.
Values may be sent and summed in bfloat16 or wider, within the bound.
No kernel may reach another device: no remote copies, remote signals or barrier semaphores. Data moves between devices by JAX's collectives and lax.ppermute only.
A program may use at most 64 MiB of HBM per device.

v0:
```python
import math

import jax
import jax.numpy as jnp
from jax import lax
from jax.sharding import PartitionSpec as P

TILE = 128


def laid_out(tiles, dim):
    tiles = jnp.moveaxis(tiles, 0, dim)
    dims = tiles.shape
    return tiles.reshape(*dims[:dim], dims[dim] * dims[dim + 1], *dims[dim + 2 :])


def sent_to_all(value, axis):
    size = lax.axis_size(axis)
    return lax.all_to_all(
        jnp.broadcast_to(value[None], (size, *value.shape)), axis, 0, 0, tiled=True
    )


def gathered_copies(value, axis, dim):
    return laid_out(sent_to_all(value, axis), dim)


def cut_along(value, dim, size):
    before, after = (value.shape[:dim], value.shape[dim + 1 :])
    return jnp.moveaxis(value.reshape(*before, size, -1, *after), dim, 0)


def summed_on_arrival(value, axis, dim):
    tiles = cut_along(value, dim, lax.axis_size(axis))
    arrived = lax.all_to_all(tiles, axis, split_axis=0, concat_axis=0, tiled=True)
    return arrived.sum(axis=0)


def body(transmission, inverse_var, pixel_mask, coef, basis, coef_tangent, basis_tangent):
    rows_here = transmission.shape[0]
    cols_here = transmission.shape[1]
    full_tangent = gathered_copies(coef_tangent, "pix", 1)
    moved = jnp.dot(full_tangent, basis, preferred_element_type=jnp.float32)
    full_basis = gathered_copies(basis_tangent, "exp", 0)
    moved = moved + jnp.dot(coef, full_basis, preferred_element_type=jnp.float32)
    spread = jnp.broadcast_to(
        pixel_mask.astype(jnp.float32)[:, :, None], (rows_here, cols_here // TILE, TILE)
    ).reshape(rows_here, cols_here)
    trans = transmission.astype(jnp.float32)
    weights = trans * trans * inverse_var.astype(jnp.float32) * spread
    weighted = (weights * moved).astype(jnp.bfloat16)
    coef_term = lax.dot_general(
        weighted, basis, (((1,), (1,)), ((), ())), preferred_element_type=jnp.float32
    )
    coef_grad = summed_on_arrival(coef_term, "pix", 1) / math.sqrt(cols_here * lax.axis_size("pix"))
    basis_term = lax.dot_general(
        coef, weighted, (((0,), (0,)), ((), ())), preferred_element_type=jnp.float32
    )
    summed = summed_on_arrival(basis_term, "exp", 0)
    basis_grad = summed / math.sqrt(rows_here * lax.axis_size("exp"))
    return (coef_grad, basis_grad)


def solution(mesh):
    placed = (
        P("exp", "pix"),
        P("exp", "pix"),
        P("exp", "pix"),
        P("exp", None),
        P(None, "pix"),
        P("exp", "pix"),
        P("exp", "pix"),
    )
    return jax.shard_map(
        body,
        mesh=mesh,
        in_specs=placed,
        out_specs=(P("exp", "pix"), P("exp", "pix")),
        check_vma=False,
    )
```

profile of v0, /device:TPU:6, one launch (start us, length us, event | category | flops | bytes accessed | tf_op | source)
XLA Modules:
  0.0 133.9 jit_solution(5703951620134578373)
XLA Ops:
  0.6 0.0 copy-start
  0.6 0.0 copy-start.2
  0.7 0.8 broadcast_in_dim.7
  1.5 16.2 %all_to_all.20 = bf16[16,512,16]{1,2,0:T(8,128)(2,1)S(1)} all-to-all(bf16[16,512,16]{1,2,0:T(8,128)(2,1)S(1)} %broadcast_in_dim.7), channel_id=1, replica_groups=mesh['exp'=32,'pix'=16] {'pix'}, dimensions={0} | all-to-all | bytes 524288 | tf_op jit(solution)/shard_map/all_to_all | solution.py:19
  17.7 1.7 %broadcast_in_dim.8 = bf16[32,8,1536]{2,1,0:T(8,128)(2,1)} broadcast(bf16[8,1536]{1,0:T(8,128)(2,1)} %param.13), dimensions={1,2} | broadcast | bytes 811008 | tf_op jit(solution)/shard_map/broadcast_in_dim | solution.py:20
  19.4 13.3 %all-to-all-start.1 = ((bf16[32,8,1536]{2,1,0:T(8,128)(2,1)}), bf16[32,8,1536]{2,1,0:T(8,128)(2,1)S(1)}, u32[]{:S(2)}, u32[]{:S(2)}) async-start(bf16[32,8,1536]{2,1,0:T(8,128)(2,1)} %broadcast_in_dim.8), calls=%async_computation.1 | async-start | bytes 1572864 | tf_op jit(solution)/shard_map/all_to_all | solution.py:19
  32.6 0.0 copy-done.2
  32.7 2.1 %broadcast_in_dim.6 = f32[512,12,128]{0,2,1:T(8,128)} broadcast(f32[512,12]{0,1:T(8,128)S(1)} %convert_element_type.14), dimensions={0,1} | broadcast | bytes 3170304 | tf_op jit(solution)/shard_map/broadcast_in_dim | solution.py:46
  34.7 3.5 %copy.11 = f32[512,1536]{1,0:T(8,128)} copy(f32[512,1536]{0,1:T(8,128)} %bitcast.21) | data formatting | bytes 6291456 | tf_op jit(solution)/shard_map/reshape | solution.py:48
  38.2 0.0 copy-done
  38.2 0.0 copy-start.1
  38.3 2.3 %fusion.3 = f32[512,1536]{1,0:T(8,128)} fusion(bf16[512,256]{0,1:T(8,128)(2,1)S(1)} %bitcast.22, bf16[256,1536]{1,0:T(8,128)(2,1)S(1)} %copy-done), kind=kOutput, calls=%fused_computation.7 | convolution fusion | flops 402653184 | bytes 4194304 | tf_op jit(solution)/shard_map/dot_general | solution.py:43
  40.5 15.7 %all-to-all-done.1 = bf16[32,8,1536]{2,1,0:T(8,128)(2,1)S(1)} async-done(((bf16[32,8,1536]{2,1,0:T(8,128)(2,1)}), bf16[32,8,1536]{2,1,0:T(8,128)(2,1)S(1)}, u32[]{:S(2)}, u32[]{:S(2)}) %all-to-all-start.1) | async-done | bytes 786464 | tf_op jit(solution)/shard_map/all_to_all | solution.py:19
  56.2 0.0 copy-done.1
  56.2 4.6 %fusion.1 = bf16[512,1536]{1,0:T(8,128)(2,1)S(1)} fusion(f32[512,1536]{1,0:T(8,128)} %fusion.3, bf16[512,256]{1,0:T(8,128)(2,1)S(1)} %copy-done.1, f32[512,1536]{1,0:T(8,128)} %copy.11, bf16[512,1536]{1,0:T(8,128)(2,1)} %param.8, bf16[512,1536]{1,0:T(8,128)(2,1)} %param.7, bf16[32,8,1536]{2,1,0:T(8,128)(2,1)S(1)} %all-to-all-done.1), kind=kOutput, calls=%fused_computation.2 | convolution fusion | flops 408944640 | bytes 12058624 | tf_op jit(solution)/shard_map/dot_general | solution.py:45
  60.9 1.4 %fusion.4 = f32[512,256]{0,1:T(8,128)} fusion(bf16[512,1536]{1,0:T(8,128)(2,1)S(1)} %fusion.1, bf16[256,1536]{1,0:T(8,128)(2,1)S(1)} %copy-done), kind=kOutput, calls=%fused_computation.8 | convolution fusion | flops 402653184 | bytes 2883584 | tf_op jit(solution)/shard_map/dot_general | solution.py:52
  62.3 9.6 %all-to-all-start.2 = ((f32[16,512,16]{1,2,0:T(8,128)}), f32[16,512,16]{1,2,0:T(8,128)S(1)}, u32[]{:S(2)}, u32[]{:S(2)}) async-start(f32[16,512,16]{1,2,0:T(8,128)} %bitcast.5), calls=%async_computation.2 | async-start | bytes 1048576 | tf_op jit(solution)/shard_map/all_to_all | solution.py:35
  71.9 1.8 %convolution_bitcast_fusion = f32[32,8,1536]{2,1,0:T(8,128)} fusion(bf16[512,1536]{1,0:T(8,128)(2,1)S(1)} %fusion.1, bf16[512,256]{1,0:T(8,128)(2,1)S(1)} %copy-done.1), kind=kOutput, calls=%fused_computation.3 | convolution fusion | flops 402653184 | bytes 3407872 | tf_op jit(solution)/shard_map/dot_general | solution.py:56
  73.6 11.4 %all-to-all-done.2 = f32[16,512,16]{1,2,0:T(8,128)S(1)} async-done(((f32[16,512,16]{1,2,0:T(8,128)}), f32[16,512,16]{1,2,0:T(8,128)S(1)}, u32[]{:S(2)}, u32[]{:S(2)}) %all-to-all-start.2) | async-done | bytes 524320 | tf_op jit(solution)/shard_map/all_to_all | solution.py:35
  85.0 4.9 %all-to-all-start.3 = ((f32[32,8,1536]{2,1,0:T(8,128)}), f32[32,8,1536]{2,1,0:T(8,128)S(1)}, u32[]{:S(2)}, u32[]{:S(2)}) async-start(f32[32,8,1536]{2,1,0:T(8,128)} %convolution_bitcast_fusion), calls=%async_computation.3 | async-start | bytes 3145728 | tf_op jit(solution)/shard_map/all_to_all | solution.py:35
  90.0 0.6 broadcast_multiply_fusion.1
  90.6 42.6 %all-to-all-done.3 = f32[32,8,1536]{2,1,0:T(8,128)S(1)} async-done(((f32[32,8,1536]{2,1,0:T(8,128)}), f32[32,8,1536]{2,1,0:T(8,128)S(1)}, u32[]{:S(2)}, u32[]{:S(2)}) %all-to-all-start.3) | async-done | bytes 1572896 | tf_op jit(solution)/shard_map/all_to_all | solution.py:35
  133.2 0.1 reduce_sum.19
  133.2 0.6 broadcast_multiply_fusion
  (2 shorter events, 0.0 us)
Async XLA Ops:
  0.6 37.6 %copy-start = (bf16[256,1536]{1,0:T(8,128)(2,1)S(1)}, bf16[256,1536]{1,0:T(8,128)(2,1)}, u32[]{:S(2)}) copy-start(bf16[256,1536]{1,0:T(8,128)(2,1)} %param.11) | copy-start | bytes 2359300
  0.6 32.0 %copy-start.2 = (s32[512,12]{0,1:T(8,128)S(1)}, s32[512,12]{0,1:T(8,128)}, u32[]{:S(2)}) copy-start(s32[512,12]{0,1:T(8,128)} %param.9) | copy-start | bytes 73732
  19.4 36.9 %all-to-all-start.1 = ((bf16[32,8,1536]{2,1,0:T(8,128)(2,1)}), bf16[32,8,1536]{2,1,0:T(8,128)(2,1)S(1)}, u32[]{:S(2)}, u32[]{:S(2)}) async-start(bf16[32,8,1536]{2,1,0:T(8,128)(2,1)} %broadcast_in_dim.8), calls=%async_computation.1 | async-start | bytes 1572864 | tf_op jit(solution)/shard_map/all_to_all | solution.py:19
  38.2 18.0 %copy-start.1 = (bf16[512,256]{1,0:T(8,128)(2,1)S(1)}, bf16[512,256]{1,0:T(8,128)(2,1)}, u32[]{:S(2)}) copy-start(bf16[512,256]{1,0:T(8,128)(2,1)} %param.10) | copy-start | bytes 786436
  62.3 22.8 %all-to-all-start.2 = ((f32[16,512,16]{1,2,0:T(8,128)}), f32[16,512,16]{1,2,0:T(8,128)S(1)}, u32[]{:S(2)}, u32[]{:S(2)}) async-start(f32[16,512,16]{1,2,0:T(8,128)} %bitcast.5), calls=%async_computation.2 | async-start | bytes 1048576 | tf_op jit(solution)/shard_map/all_to_all | solution.py:35
  85.0 48.1 %all-to-all-start.3 = ((f32[32,8,1536]{2,1,0:T(8,128)}), f32[32,8,1536]{2,1,0:T(8,128)S(1)}, u32[]{:S(2)}, u32[]{:S(2)}) async-start(f32[32,8,1536]{2,1,0:T(8,128)} %convolution_bitcast_fusion), calls=%async_computation.3 | async-start | bytes 3145728 | tf_op jit(solution)/shard_map/all_to_all | solution.py:35
where the time goes:
time: 136 us; the launch traced here: 134 us
  waiting for transfers between devices  69.7 us (51%)
  starting transfers between devices  27.8 us (20%)
  blocking collectives  16.2 us (12%)
  matrix products  10.1 us (7%)
  local copies, waits for them, and re-layouts  8.08 us (6%)
  other arithmetic  1.37 us (1%)
    all_to_all x2, waiting for transfers between devices, summed_on_arrival(): lax.all_to_all(tiles, axis, split_axis=0, concat_axis=0, tiled=True)  53.9 us
    all_to_all x1, blocking collectives, sent_to_all(): lax.all_to_all(jnp.broadcast_to(value[None], (size, *value.shape)), axis,...  16.2 us
    all_to_all x1, waiting for transfers between devices, sent_to_all(): lax.all_to_all(jnp.broadcast_to(value[None], (size, *value.shape)), axis,...  15.7 us
    all_to_all x2, starting transfers between devices, summed_on_arrival(): lax.all_to_all(tiles, axis, split_axis=0, concat_axis=0, tiled=True)  14.5 us
    all_to_all x1, starting transfers between devices, sent_to_all(): lax.all_to_all(jnp.broadcast_to(value[None], (size, *value.shape)), axis,...  13.3 us
    dot_general x1, matrix products, body(): jnp.dot(coef, full_basis, preferred_element_type=jnp.float32)  4.63 us
    reshape x1, local copies, waits for them, and re-layouts, body(): spread = jnp.broadcast_to(pixel_mask.astype(jnp.float32)[:, :, None], (ro...  3.53 us
  transfers between devices with their start and end apart: 3, of which 3 were waited for; matrix products, arithmetic and copies ran while one was open for 8% of the time, Pallas kernels for 0%

commit v1 on v0

v1 whole, which is shorter than its diff:
```python
import math

import jax
import jax.numpy as jnp
from jax import lax
from jax.experimental import pallas as pl
from jax.experimental.pallas import tpu as pltpu
from jax.sharding import Mesh
from jax.sharding import PartitionSpec as P

TILE = 128
BF16, F16, F32 = jnp.bfloat16, jnp.float16, jnp.float32
TOP, STEP, RUNGS = -14, 16, 8
STAGES = (("x", 2), ("yl", 2), ("x", 1), ("yl", 1))


def rung_of(amax):
    return sum(
        (amax < 2.0 ** (15 - TOP - STEP * i)).astype(F32) for i in range(1, RUNGS + 1)
    )


def scale_of(rung, sign):
    scale = jnp.full_like(rung, 2.0 ** (sign * TOP))
    for i in range(1, RUNGS + 1):
        scale = scale * jnp.where(rung >= i, F32(2.0 ** (sign * STEP)), F32(1.0))
    return scale


def partner(value, axis, bit):
    size = lax.axis_size(axis)
    return lax.ppermute(value, axis, [(i, i ^ bit) for i in range(size)])


def upper(axis, bit):
    return (lax.axis_index(axis) & bit) != 0


def in_stage_order(rows, count):
    shape = rows.shape
    cut = rows.reshape(2, 2, 2, 2, count, *shape[1:])
    return cut.transpose(3, 1, 2, 0, *range(4, cut.ndim)).reshape(shape)


def first_kernel(trans_ref, ivar_ref, mask_ref, tangent_ref, basis_ref, weights_ref, moved_ref):
    trans = trans_ref[...].astype(F32)
    weights = trans * trans * ivar_ref[...].astype(F32)
    step = pl.program_id(0)
    tiles = trans.shape[1] // TILE
    lanes = lax.broadcasted_iota(jnp.int32, mask_ref.shape, 1)
    for t in range(tiles):
        here = jnp.where(lanes == step * tiles + t, mask_ref[...], 0.0)
        column = jnp.sum(here, axis=1, keepdims=True)
        weights_ref[:, t * TILE : (t + 1) * TILE] = (
            weights[:, t * TILE : (t + 1) * TILE] * column
        )
    moved_ref[...] = lax.dot_general(
        tangent_ref[...], basis_ref[...], (((0,), (0,)), ((), ())), preferred_element_type=F32
    )


def second_kernel(weights_ref, moved_ref, coef_ref, coef_t_ref, full_ref, basis_ref, coef_out, own_out, other_out):
    moved = moved_ref[...] + jnp.dot(coef_ref[...], full_ref[...], preferred_element_type=F32)
    weighted = (weights_ref[...] * moved).astype(BF16)
    sums = jnp.dot(coef_t_ref[...], weighted, preferred_element_type=F32)
    half = own_out.shape[0]
    own_out[...] = sums[:half]
    other_out[...] = sums[half:]
    term = lax.dot_general(
        basis_ref[...], weighted, (((1,), (1,)), ((), ())), preferred_element_type=F32
    )

    @pl.when(pl.program_id(0) == 0)
    def _():
        coef_out[...] = term

    @pl.when(pl.program_id(0) > 0)
    def _():
        coef_out[...] += term


def pack_kernel(own_ref, other_ref, out_ref):
    total = own_ref[...] + other_ref[...]
    cols = total.shape[1]
    amax = jnp.max(jnp.max(jnp.abs(total), axis=0, keepdims=True), axis=1, keepdims=True)
    rung = rung_of(amax)
    out_ref[:, :cols] = total * scale_of(rung, 1)
    out_ref[:, cols:] = jnp.broadcast_to(rung, (total.shape[0], out_ref.shape[1] - cols))


def unpack_kernel(divisor, in_ref, out_ref):
    cols = out_ref.shape[1]
    total = jnp.zeros(out_ref.shape, F32)
    for i in range(in_ref.shape[0]):
        inverse = scale_of(in_ref[i, :, cols : cols + TILE], -1)
        for t in range(cols // TILE):
            part = slice(t * TILE, (t + 1) * TILE)
            out = in_ref[i, :, part] * inverse
            out_ref[:, part] = out if i == 0 else out_ref[:, part] + out
    out_ref[...] = out_ref[...] * (1.0 / divisor)


def body(transmission, inverse_var, pixel_mask, coef, basis, coef_tangent, basis_tangent):
    rows, cols = transmission.shape
    rank = basis.shape[0]
    mine = rank // 32
    exposures, pixels = rows * 32, cols * 16
    core = lax.axis_index("c")

    spread = jnp.broadcast_to(basis_tangent[None], (16, *basis_tangent.shape))
    arrived = lax.all_to_all(spread, ("yh", "z"), 0, 0, tiled=True)

    tangent = coef_tangent.T
    for axis, bit in STAGES:
        other = partner(tangent, axis, bit)
        up = upper(axis, bit)
        tangent = jnp.concatenate(
            [jnp.where(up, other, tangent), jnp.where(up, tangent, other)], axis=0
        )
    basis_p = in_stage_order(basis, rank // 16)
    coef_t = coef.T.reshape(16, 2, mine, rows).transpose(1, 0, 2, 3).reshape(rank, rows)
    coef_p = coef_t.T
    half = rank // 2
    coef_own = jnp.concatenate(
        [
            lax.dynamic_slice_in_dim(coef_t, core * half, half, 0),
            lax.dynamic_slice_in_dim(coef_t, (1 - core) * half, half, 0),
        ],
        axis=0,
    )

    width = 256
    steps = cols // width
    whole = lambda *shape: pl.BlockSpec(shape, lambda i: (0,) * len(shape))
    tall = lambda n: pl.BlockSpec((n, width), lambda i: (0, i))
    weights, moved = pl.pallas_call(
        first_kernel,
        grid=(steps,),
        in_specs=[tall(rows), tall(rows), whole(rows, cols // TILE), whole(rank, rows), tall(rank)],
        out_specs=[tall(rows), tall(rows)],
        out_shape=[jax.ShapeDtypeStruct((rows, cols), F32)] * 2,
        compiler_params=pltpu.CompilerParams(vmem_limit_bytes=24 << 20),
        cost_estimate=pl.CostEstimate(
            flops=2 * rows * cols * rank, bytes_accessed=12 * rows * cols, transcendentals=0
        ),
    )(transmission, inverse_var, pixel_mask.astype(F32), tangent, basis_p)

    full = lax.all_gather(arrived.reshape(half, cols), "c", axis=0, tiled=True)
    coef_term, own, other = pl.pallas_call(
        second_kernel,
        grid=(steps,),
        in_specs=[
            tall(rows), tall(rows), whole(rows, rank), whole(rank, rows), tall(rank), tall(rank),
        ],
        out_specs=[whole(rank, rows), tall(half), tall(half)],
        out_shape=[
            jax.ShapeDtypeStruct((rank, rows), F32),
            jax.ShapeDtypeStruct((half, cols), F32),
            jax.ShapeDtypeStruct((half, cols), F32),
        ],
        compiler_params=pltpu.CompilerParams(vmem_limit_bytes=24 << 20),
        cost_estimate=pl.CostEstimate(
            flops=6 * rows * cols * rank, bytes_accessed=10 * rows * cols, transcendentals=0
        ),
    )(weights, moved, coef_p, coef_own, full, basis_p)

    other = lax.ppermute(other, "c", [(0, 1), (1, 0)])
    packed = pl.pallas_call(
        pack_kernel, out_shape=jax.ShapeDtypeStruct((half, cols + TILE), F32)
    )(own, other)
    packed = packed.astype(F16).reshape(16, mine, cols + TILE)
    packed = lax.all_to_all(packed, ("yh", "z"), 0, 0, tiled=True).astype(F32)
    basis_grad = pl.pallas_call(
        lambda *refs: unpack_kernel(math.sqrt(exposures), *refs),
        out_shape=jax.ShapeDtypeStruct((mine, cols), F32),
    )(packed)

    for axis, bit in reversed(STAGES):
        up = upper(axis, bit)
        n = coef_term.shape[0] // 2
        low, high = coef_term[:n], coef_term[n:]
        came = partner(jnp.where(up, low, high), axis, bit)
        coef_term = jnp.where(up, high, low) + came
    coef_grad = coef_term.T / math.sqrt(pixels)
    return (coef_grad, basis_grad)


def solution(mesh):
    fine = Mesh(mesh.devices.reshape(2, 8, 2, 4, 4), ("yh", "z", "c", "x", "yl"))
    exp, pix = ("yh", "z", "c"), ("x", "yl")
    placed = (
        P(exp, pix),
        P(exp, pix),
        P(exp, pix),
        P(exp, None),
        P(None, pix),
        P(exp, pix),
        P(exp, pix),
    )
    return jax.shard_map(
        body,
        mesh=fine,
        in_specs=placed,
        out_specs=(P(exp, pix), P(exp, pix)),
        check_vma=False,
    )
```

time: 136 us -> 124 us (0.912)
  waiting for transfers between devices: 69.7 us -> 31.4 us
  starting transfers between devices: 27.8 us -> 54.7 us
  blocking collectives: 16.2 us -> 2.36 us
  Pallas kernels: 0 us -> 11.3 us
  matrix products: 10.1 us -> 0 us
  local copies, waits for them, and re-layouts: 8.08 us -> 14.3 us
  other arithmetic: 1.37 us -> 7.22 us
    all_to_all x3 -> x2, waiting for transfers between devices: 69.7 us -> 0.01 us  [the longest x1 0.01 us: body(): arrived = lax.all_to_all(spread, ('yh', 'z'), 0, 0, tiled=True)]
    ppermute x0 -> x9, waiting for transfers between devices: none -> 31.4 us  [the longest x8 31.4 us: partner(): return lax.ppermute(value, axis, [(i, i ^ bit) for i in range(size)])]
    ppermute x0 -> x9, starting transfers between devices: none -> 30.2 us  [the longest x8 28.2 us: partner(): return lax.ppermute(value, axis, [(i, i ^ bit) for i in range(size)])]
    all_to_all x1 -> x0, blocking collectives: 16.2 us -> none  [sent_to_all(): lax.all_to_all(jnp.broadcast_to(value[None], (size, *value.shape)), axis,...]
    pallas_call x0 -> x4, Pallas kernels: none -> 11.3 us  [the longest x1 4.23 us: body(): pl.pallas_call(second_kernel, grid=(steps,), in_specs=[tall(rows), tall(r...]
    unnamed x6 -> x23, local copies, waits for them, and re-layouts: 0.02 us -> 10.6 us
    dot_general x4 -> x0, matrix products: 10.1 us -> none  [the longest x1 4.63 us: body(): jnp.dot(coef, full_basis, preferred_element_type=jnp.float32)]
    all_to_all x3 -> x2, starting transfers between devices: 27.8 us -> 24.5 us  [the longest x1 13.7 us: body(): arrived = lax.all_to_all(spread, ('yh', 'z'), 0, 0, tiled=True)]
  transfers between devices with their start and end apart: 3 -> 11, of which waited for: 3 -> 7; matrix products, arithmetic and copies ran while one was open for 8% -> 7% of each run, Pallas kernels for 0% -> 2%
where the time goes in v1:
time: 124 us; the launch traced here: 122 us
  starting transfers between devices  54.7 us (44%)
  waiting for transfers between devices  31.4 us (25%)
  local copies, waits for them, and re-layouts  14.3 us (12%)
  Pallas kernels  11.3 us (9%)
  other arithmetic  7.22 us (6%)
  blocking collectives  2.36 us (2%)
    ppermute x8, waiting for transfers between devices, partner(): return lax.ppermute(value, axis, [(i, i ^ bit) for i in range(size)])  31.4 us
    ppermute x8, starting transfers between devices, partner(): return lax.ppermute(value, axis, [(i, i ^ bit) for i in range(size)])  28.2 us
    all_to_all x1, starting transfers between devices, body(): arrived = lax.all_to_all(spread, ('yh', 'z'), 0, 0, tiled=True)  13.7 us
    all_to_all x1, starting transfers between devices, body(): packed = lax.all_to_all(packed, ('yh', 'z'), 0, 0, tiled=True).astype(F32)  10.9 us
    unnamed x23, local copies, waits for them, and re-layouts  10.6 us
    pallas_call x1, Pallas kernels, body(): pl.pallas_call(second_kernel, grid=(steps,), in_specs=[tall(rows), tall(r...  4.23 us
    pallas_call x1, Pallas kernels, body(): pl.pallas_call(first_kernel, grid=(steps,), in_specs=[tall(rows), tall(ro...  2.62 us
    pallas_call x1, Pallas kernels, body(): pl.pallas_call(pack_kernel, out_shape=jax.ShapeDtypeStruct((half, cols +...  2.52 us
  transfers between devices with their start and end apart: 11, of which 7 were waited for; matrix products, arithmetic and copies ran while one was open for 7% of the time, Pallas kernels for 2%

profile of v1, /device:TPU:6, one launch (start us, length us, event | category | flops | bytes accessed | tf_op | source)
XLA Modules:
  0.0 122.3 jit_solution(3776065043215266096)
XLA Ops:
  0.6 3.3 %collective-permute-start = (bf16[16,512]{1,0:T(8,128)(2,1)}, bf16[16,512]{1,0:T(8,128)(2,1)S(1)}, u32[]{:S(2)}, u32[]{:S(2)}) collective-permute-start(bf16[16,512]{1,0:T(8,128)(2,1)} %bitcast.27), channel_id=1, source_target_pairs={{0,8},{4,12},{8,0},{12,4},{1,9},{5,13},{9,1},{13,5},{2,10},{6,14},... | collective-permute-start | bytes 49160 | tf_op jit(solution)/shard_map/ppermute | solution.py:32
  4.0 4.0 %collective-permute-done = bf16[16,512]{1,0:T(8,128)(2,1)S(1)} collective-permute-done((bf16[16,512]{1,0:T(8,128)(2,1)}, bf16[16,512]{1,0:T(8,128)(2,1)S(1)}, u32[]{:S(2)}, u32[]{:S(2)}) %collective-permute-start) | collective-permute-done | bytes 16416 | tf_op jit(solution)/shard_map/ppermute | solution.py:32
  8.7 4.5 %collective-permute-start.1 = (bf16[32,512]{1,0:T(8,128)(2,1)S(1)}, bf16[32,512]{1,0:T(8,128)(2,1)S(1)}, u32[]{:S(2)}, u32[]{:S(2)}) collective-permute-start(bf16[32,512]{1,0:T(8,128)(2,1)S(1)} %pad_maximum_fusion.4), channel_id=1, source_target_pairs={{0,2},{1,3},{2,0},{3,1},{4,6},{5,7},{6,4},{7,5},{8,10},{9,11},{10,... | collective-permute-start | bytes 98312 | tf_op jit(solution)/shard_map/ppermute | solution.py:32
  13.2 2.2 %collective-permute-done.1 = bf16[32,512]{1,0:T(8,128)(2,1)S(1)} collective-permute-done((bf16[32,512]{1,0:T(8,128)(2,1)S(1)}, bf16[32,512]{1,0:T(8,128)(2,1)S(1)}, u32[]{:S(2)}, u32[]{:S(2)}) %collective-permute-start.1) | collective-permute-done | bytes 32800 | tf_op jit(solution)/shard_map/ppermute | solution.py:32
  15.5 5.1 %collective-permute-start.2 = (bf16[64,512]{1,0:T(8,128)(2,1)S(1)}, bf16[64,512]{1,0:T(8,128)(2,1)S(1)}, u32[]{:S(2)}, u32[]{:S(2)}) collective-permute-start(bf16[64,512]{1,0:T(8,128)(2,1)S(1)} %pad_maximum_fusion.3), channel_id=1, source_target_pairs={{0,4},{4,0},{8,12},{12,8},{1,5},{5,1},{9,13},{13,9},{2,6},{6,2},{1... | collective-permute-start | bytes 196616 | tf_op jit(solution)/shard_map/ppermute | solution.py:32
  22.1 13.7 %all-to-all-start = ((bf16[16,8,1536]{2,1,0:T(8,128)(2,1)}), bf16[16,8,1536]{2,1,0:T(8,128)(2,1)S(1)}, u32[]{:S(2)}, u32[]{:S(2)}) async-start(bf16[16,8,1536]{2,1,0:T(8,128)(2,1)} %broadcast_in_dim.2), calls=%async_computation | async-start | bytes 786432 | tf_op jit(solution)/shard_map/all_to_all | solution.py:111
  37.8 2.3 %collective-permute-start.3 = (bf16[128,512]{1,0:T(8,128)(2,1)}, bf16[128,512]{1,0:T(8,128)(2,1)}, u32[]{:S(2)}, u32[]{:S(2)}) collective-permute-start(bf16[128,512]{1,0:T(8,128)(2,1)} %pad_maximum_fusion.2), channel_id=1, source_target_pairs={{0,1},{1,0},{2,3},{3,2},{4,5},{5,4},{6,7},{7,6},{8,9},{9,8},{10,11... | collective-permute-start | bytes 393224 | tf_op jit(solution)/shard_map/ppermute | solution.py:32
  43.3 2.3 %collective-permute-done.3 = bf16[128,512]{1,0:T(8,128)(2,1)} collective-permute-done((bf16[128,512]{1,0:T(8,128)(2,1)}, bf16[128,512]{1,0:T(8,128)(2,1)}, u32[]{:S(2)}, u32[]{:S(2)}) %collective-permute-start.3) | collective-permute-done | bytes 131104 | tf_op jit(solution)/shard_map/ppermute | solution.py:32
  48.1 2.6 %shard_map.86 = (f32[512,1536]{1,0:T(8,128)S(1)}, f32[512,1536]{1,0:T(8,128)S(1)}) custom-call(bf16[512,1536]{1,0:T(8,128)(2,1)S(1)} %copy-done.4, bf16[512,1536]{1,0:T(8,128)(2,1)S(1)} %copy-done.5, f32[512,12]{1,0:T(8,128)S(1)} %copy.19.mask_ref, bf16[256,512]{1,0:T(8,128)(2,1)S(1)} %pad_maximum_fusion.tangent_ref, bf16[256,1536]{1,0:T(8,128)(2,1)S(1)} %bitcast.20), custom_call_target="tpu_custom_call" | custom-call | flops 402653184 | bytes 9437184 | tf_op jit(solution)/shard_map/pallas_call | solution.py:136
  54.0 2.4 %all_gather.3.full_ref = bf16[256,1536]{1,0:T(8,128)(2,1)S(1)} all-gather(bf16[128,1536]{1,0:T(8,128)(2,1)S(1)} %bitcast.24), channel_id=1, replica_groups=mesh['yh'=2,'z'=8,'c'=2,'x'=4,'yl'=4] {'c'}, dimensions={0}, use_global_device_ids=true | all-gather | bytes 1179648 | tf_op jit(solution)/shard_map/all_gather | solution.py:148
  56.4 1.9 %copy-done.1 = f32[512,1536]{1,0:T(8,128)S(1)} copy-done((f32[512,1536]{1,0:T(8,128)S(1)}, f32[512,1536]{1,0:T(8,128)}, u32[]{:S(2)}) %copy-start.1) | copy-done | bytes 3145752
  60.1 4.2 %shard_map.87 = (f32[256,512]{1,0:T(8,128)S(1)}, f32[128,1536]{1,0:T(8,128)S(1)}, f32[128,1536]{1,0:T(8,128)S(1)}) custom-call(f32[512,1536]{1,0:T(8,128)S(1)} %copy-done.1, f32[512,1536]{1,0:T(8,128)S(1)} %copy-done.3, bf16[512,256]{1,0:T(8,128)(2,1)S(1)} %copy.22.coef_ref, bf16[256,512]{1,0:T(8,128)(2,1)S(1)} %pad_maximum_fusion.1.coef_t_ref, ...), custom_call_target="tpu_custom_call" | custom-call | flops 1207959552 | bytes 7864320 | tf_op jit(solution)/shard_map/pallas_call | solution.py:149
  64.4 4.4 %collective-permute-start.4 = (f32[128,512]{1,0:T(8,128)S(1)}, f32[128,512]{1,0:T(8,128)S(1)}, u32[]{:S(2)}, u32[]{:S(2)}) collective-permute-start(f32[128,512]{1,0:T(8,128)S(1)} %slice_select_fusion), channel_id=1, source_target_pairs={{0,1},{1,0},{2,3},{3,2},{4,5},{5,4},{6,7},{7,6},{8,9},{9,8},{10,11... | collective-permute-start | bytes 786440 | tf_op jit(solution)/shard_map/ppermute | solution.py:32
  68.8 1.9 %collective-permute-start.8 = (f32[128,1536]{1,0:T(8,128)S(1)}, f32[128,1536]{1,0:T(8,128)S(1)}, u32[]{:S(2)}, u32[]{:S(2)}) collective-permute-start(f32[128,1536]{1,0:T(8,128)S(1)} %get-tuple-element.11), channel_id=1, source_target_pairs={{0,16},{16,0},{1,17},{17,1},{2,18},{18,2},{3,19},{19,3},{4,20},{20... | collective-permute-start | bytes 2359304 | tf_op jit(solution)/shard_map/ppermute | solution.py:167
  70.8 4.7 %collective-permute-done.4 = f32[128,512]{1,0:T(8,128)S(1)} collective-permute-done((f32[128,512]{1,0:T(8,128)S(1)}, f32[128,512]{1,0:T(8,128)S(1)}, u32[]{:S(2)}, u32[]{:S(2)}) %collective-permute-start.4) | collective-permute-done | bytes 262176 | tf_op jit(solution)/shard_map/ppermute | solution.py:32
  75.5 3.1 %collective-permute-start.5 = (f32[64,512]{1,0:T(8,128)S(1)}, f32[64,512]{1,0:T(8,128)S(1)}, u32[]{:S(2)}, u32[]{:S(2)}) collective-permute-start(f32[64,512]{1,0:T(8,128)S(1)} %slice_select_fusion.1), channel_id=1, source_target_pairs={{0,4},{4,0},{8,12},{12,8},{1,5},{5,1},{9,13},{13,9},{2,6},{6,2},{1... | collective-permute-start | bytes 393224 | tf_op jit(solution)/shard_map/ppermute | solution.py:32
  78.6 3.8 %collective-permute-done.5 = f32[64,512]{1,0:T(8,128)S(1)} collective-permute-done((f32[64,512]{1,0:T(8,128)S(1)}, f32[64,512]{1,0:T(8,128)S(1)}, u32[]{:S(2)}, u32[]{:S(2)}) %collective-permute-start.5) | collective-permute-done | bytes 131104 | tf_op jit(solution)/shard_map/ppermute | solution.py:32
  83.4 2.5 %shard_map.88 = f32[128,1664]{1,0:T(8,128)} custom-call(f32[128,1536]{1,0:T(8,128)} %copy-done.6, f32[128,1536]{1,0:T(8,128)} %copy-done.7), custom_call_target="tpu_custom_call" | custom-call | tf_op jit(solution)/shard_map/pallas_call | solution.py:168
  85.9 2.0 %convert_bitcast_fusion = f16[16,8,1664]{2,1,0:T(8,128)(2,1)} fusion(f32[128,1664]{1,0:T(8,128)} %shard_map.88), kind=kLoop, calls=%fused_computation | loop fusion | flops 212992 | bytes 1277952 | tf_op jit(solution)/shard_map/reshape | solution.py:171
  87.9 10.9 %all-to-all-start.1 = ((f16[16,8,1664]{2,1,0:T(8,128)(2,1)}), f16[16,8,1664]{2,1,0:T(8,128)(2,1)S(1)}, u32[]{:S(2)}, u32[]{:S(2)}) async-start(f16[16,8,1664]{2,1,0:T(8,128)(2,1)} %convert_bitcast_fusion), calls=%async_computation.1 | async-start | bytes 851968 | tf_op jit(solution)/shard_map/all_to_all | solution.py:172
  98.8 2.5 %collective-permute-start.6 = (f32[32,512]{1,0:T(8,128)S(1)}, f32[32,512]{1,0:T(8,128)S(1)}, u32[]{:S(2)}, u32[]{:S(2)}) collective-permute-start(f32[32,512]{1,0:T(8,128)S(1)} %slice_select_fusion.2), channel_id=1, source_target_pairs={{0,2},{1,3},{2,0},{3,1},{4,6},{5,7},{6,4},{7,5},{8,10},{9,11},{10,... | collective-permute-start | bytes 196616 | tf_op jit(solution)/shard_map/ppermute | solution.py:32
  101.3 10.2 %collective-permute-done.6 = f32[32,512]{1,0:T(8,128)S(1)} collective-permute-done((f32[32,512]{1,0:T(8,128)S(1)}, f32[32,512]{1,0:T(8,128)S(1)}, u32[]{:S(2)}, u32[]{:S(2)}) %collective-permute-start.6) | collective-permute-done | bytes 65568 | tf_op jit(solution)/shard_map/ppermute | solution.py:32
  111.5 3.0 %collective-permute-start.7 = (f32[16,512]{1,0:T(8,128)S(1)}, f32[16,512]{1,0:T(8,128)S(1)}, u32[]{:S(2)}, u32[]{:S(2)}) collective-permute-start(f32[16,512]{1,0:T(8,128)S(1)} %slice_select_fusion.3), channel_id=1, source_target_pairs={{0,8},{4,12},{8,0},{12,4},{1,9},{5,13},{9,1},{13,5},{2,10},{6,14},... | collective-permute-start | bytes 98312 | tf_op jit(solution)/shard_map/ppermute | solution.py:32
  114.5 4.3 %collective-permute-done.7 = f32[16,512]{1,0:T(8,128)S(1)} collective-permute-done((f32[16,512]{1,0:T(8,128)S(1)}, f32[16,512]{1,0:T(8,128)S(1)}, u32[]{:S(2)}, u32[]{:S(2)}) %collective-permute-start.7) | collective-permute-done | bytes 32800 | tf_op jit(solution)/shard_map/ppermute | solution.py:32
  (52 shorter events, 19.6 us)
Async XLA Ops:
  0.6 40.2 %copy-start.10 = (s32[512,12]{0,1:T(8,128)S(1)}, s32[512,12]{0,1:T(8,128)}, u32[]{:S(2)}) copy-start(s32[512,12]{0,1:T(8,128)} %param.9) | copy-start | bytes 73732
  0.6 7.3 %collective-permute-start = (bf16[16,512]{1,0:T(8,128)(2,1)}, bf16[16,512]{1,0:T(8,128)(2,1)S(1)}, u32[]{:S(2)}, u32[]{:S(2)}) collective-permute-start(bf16[16,512]{1,0:T(8,128)(2,1)} %bitcast.27), channel_id=1, source_target_pairs={{0,8},{4,12},{8,0},{12,4},{1,9},{5,13},{9,1},{13,5},{2,10},{6,14},... | collective-permute-start | bytes 49160 | tf_op jit(solution)/shard_map/ppermute | solution.py:32
  8.7 6.7 %collective-permute-start.1 = (bf16[32,512]{1,0:T(8,128)(2,1)S(1)}, bf16[32,512]{1,0:T(8,128)(2,1)S(1)}, u32[]{:S(2)}, u32[]{:S(2)}) collective-permute-start(bf16[32,512]{1,0:T(8,128)(2,1)S(1)} %pad_maximum_fusion.4), channel_id=1, source_target_pairs={{0,2},{1,3},{2,0},{3,1},{4,6},{5,7},{6,4},{7,5},{8,10},{9,11},{10,... | collective-permute-start | bytes 98312 | tf_op jit(solution)/shard_map/ppermute | solution.py:32
  15.5 21.6 %collective-permute-start.2 = (bf16[64,512]{1,0:T(8,128)(2,1)S(1)}, bf16[64,512]{1,0:T(8,128)(2,1)S(1)}, u32[]{:S(2)}, u32[]{:S(2)}) collective-permute-start(bf16[64,512]{1,0:T(8,128)(2,1)S(1)} %pad_maximum_fusion.3), channel_id=1, source_target_pairs={{0,4},{4,0},{8,12},{12,8},{1,5},{5,1},{9,13},{13,9},{2,6},{6,2},{1... | collective-permute-start | bytes 196616 | tf_op jit(solution)/shard_map/ppermute | solution.py:32
  22.1 31.9 %all-to-all-start = ((bf16[16,8,1536]{2,1,0:T(8,128)(2,1)}), bf16[16,8,1536]{2,1,0:T(8,128)(2,1)S(1)}, u32[]{:S(2)}, u32[]{:S(2)}) async-start(bf16[16,8,1536]{2,1,0:T(8,128)(2,1)} %broadcast_in_dim.2), calls=%async_computation | async-start | bytes 786432 | tf_op jit(solution)/shard_map/all_to_all | solution.py:111
  35.8 10.9 %copy-start.4 = (bf16[512,1536]{1,0:T(8,128)(2,1)S(1)}, bf16[512,1536]{1,0:T(8,128)(2,1)}, u32[]{:S(2)}) copy-start(bf16[512,1536]{1,0:T(8,128)(2,1)} %trans_ref.1) | copy-start | bytes 4718596
  37.1 3.9 %copy-start.8 = (bf16[64,512]{1,0:T(8,128)(2,1)}, bf16[64,512]{1,0:T(8,128)(2,1)S(1)}, u32[]{:S(2)}) copy-start(bf16[64,512]{1,0:T(8,128)(2,1)S(1)} %get-tuple-element.16) | copy-start | bytes 196612
  37.1 3.9 %copy-start.9 = (bf16[64,512]{1,0:T(8,128)(2,1)}, bf16[64,512]{1,0:T(8,128)(2,1)S(1)}, u32[]{:S(2)}) copy-start(bf16[64,512]{1,0:T(8,128)(2,1)S(1)} %get-tuple-element.17) | copy-start | bytes 196612
  37.8 7.9 %collective-permute-start.3 = (bf16[128,512]{1,0:T(8,128)(2,1)}, bf16[128,512]{1,0:T(8,128)(2,1)}, u32[]{:S(2)}, u32[]{:S(2)}) collective-permute-start(bf16[128,512]{1,0:T(8,128)(2,1)} %pad_maximum_fusion.2), channel_id=1, source_target_pairs={{0,1},{1,0},{2,3},{3,2},{4,5},{5,4},{6,7},{7,6},{8,9},{9,8},{10,11... | collective-permute-start | bytes 393224 | tf_op jit(solution)/shard_map/ppermute | solution.py:32
  46.7 1.4 %copy-start.5 = (bf16[512,1536]{1,0:T(8,128)(2,1)S(1)}, bf16[512,1536]{1,0:T(8,128)(2,1)}, u32[]{:S(2)}) copy-start(bf16[512,1536]{1,0:T(8,128)(2,1)} %ivar_ref.1) | copy-start | bytes 4718596
  50.7 1.6 %copy-start = (f32[512,1536]{1,0:T(8,128)}, f32[512,1536]{1,0:T(8,128)S(1)}, u32[]{:S(2)}) copy-start(f32[512,1536]{1,0:T(8,128)S(1)} %get-tuple-element.7.weights_ref) | copy-start | bytes 9437188
  52.3 1.7 %copy-start.2 = (f32[512,1536]{1,0:T(8,128)}, f32[512,1536]{1,0:T(8,128)S(1)}, u32[]{:S(2)}) copy-start(f32[512,1536]{1,0:T(8,128)S(1)} %get-tuple-element.8.moved_ref) | copy-start | bytes 9437188
  56.4 1.9 %copy-start.1 = (f32[512,1536]{1,0:T(8,128)S(1)}, f32[512,1536]{1,0:T(8,128)}, u32[]{:S(2)}) copy-start(f32[512,1536]{1,0:T(8,128)} %copy-done) | copy-start | bytes 9437188
  58.3 1.9 %copy-start.3 = (f32[512,1536]{1,0:T(8,128)S(1)}, f32[512,1536]{1,0:T(8,128)}, u32[]{:S(2)}) copy-start(f32[512,1536]{1,0:T(8,128)} %copy-done.2) | copy-start | bytes 9437188
  64.4 11.1 %copy-start.6 = (f32[128,1536]{1,0:T(8,128)}, f32[128,1536]{1,0:T(8,128)S(1)}, u32[]{:S(2)}) copy-start(f32[128,1536]{1,0:T(8,128)S(1)} %get-tuple-element.10.own_ref) | copy-start | bytes 2359300
  64.4 11.0 %collective-permute-start.4 = (f32[128,512]{1,0:T(8,128)S(1)}, f32[128,512]{1,0:T(8,128)S(1)}, u32[]{:S(2)}, u32[]{:S(2)}) collective-permute-start(f32[128,512]{1,0:T(8,128)S(1)} %slice_select_fusion), channel_id=1, source_target_pairs={{0,1},{1,0},{2,3},{3,2},{4,5},{5,4},{6,7},{7,6},{8,9},{9,8},{10,11... | collective-permute-start | bytes 786440 | tf_op jit(solution)/shard_map/ppermute | solution.py:32
  68.8 13.6 %collective-permute-start.8 = (f32[128,1536]{1,0:T(8,128)S(1)}, f32[128,1536]{1,0:T(8,128)S(1)}, u32[]{:S(2)}, u32[]{:S(2)}) collective-permute-start(f32[128,1536]{1,0:T(8,128)S(1)} %get-tuple-element.11), channel_id=1, source_target_pairs={{0,16},{16,0},{1,17},{17,1},{2,18},{18,2},{3,19},{19,3},{4,20},{20... | collective-permute-start | bytes 2359304 | tf_op jit(solution)/shard_map/ppermute | solution.py:167
  75.5 6.9 %collective-permute-start.5 = (f32[64,512]{1,0:T(8,128)S(1)}, f32[64,512]{1,0:T(8,128)S(1)}, u32[]{:S(2)}, u32[]{:S(2)}) collective-permute-start(f32[64,512]{1,0:T(8,128)S(1)} %slice_select_fusion.1), channel_id=1, source_target_pairs={{0,4},{4,0},{8,12},{12,8},{1,5},{5,1},{9,13},{13,9},{2,6},{6,2},{1... | collective-permute-start | bytes 393224 | tf_op jit(solution)/shard_map/ppermute | solution.py:32
  82.5 0.9 copy-start.7
  87.9 31.5 %all-to-all-start.1 = ((f16[16,8,1664]{2,1,0:T(8,128)(2,1)}), f16[16,8,1664]{2,1,0:T(8,128)(2,1)S(1)}, u32[]{:S(2)}, u32[]{:S(2)}) async-start(f16[16,8,1664]{2,1,0:T(8,128)(2,1)} %convert_bitcast_fusion), calls=%async_computation.1 | async-start | bytes 851968 | tf_op jit(solution)/shard_map/all_to_all | solution.py:172
  98.8 12.7 %collective-permute-start.6 = (f32[32,512]{1,0:T(8,128)S(1)}, f32[32,512]{1,0:T(8,128)S(1)}, u32[]{:S(2)}, u32[]{:S(2)}) collective-permute-start(f32[32,512]{1,0:T(8,128)S(1)} %slice_select_fusion.2), channel_id=1, source_target_pairs={{0,2},{1,3},{2,0},{3,1},{4,6},{5,7},{6,4},{7,5},{8,10},{9,11},{10,... | collective-permute-start | bytes 196616 | tf_op jit(solution)/shard_map/ppermute | solution.py:32
  111.5 7.3 %collective-permute-start.7 = (f32[16,512]{1,0:T(8,128)S(1)}, f32[16,512]{1,0:T(8,128)S(1)}, u32[]{:S(2)}, u32[]{:S(2)}) collective-permute-start(f32[16,512]{1,0:T(8,128)S(1)} %slice_select_fusion.3), channel_id=1, source_target_pairs={{0,8},{4,12},{8,0},{12,4},{1,9},{5,13},{9,1},{13,5},{2,10},{6,14},... | collective-permute-start | bytes 98312 | tf_op jit(solution)/shard_map/ppermute | solution.py:32

commit v2 on v0

v2 whole, which is shorter than its diff:
```python
import math

import jax
import jax.numpy as jnp
from jax import lax
from jax.experimental import pallas as pl
from jax.experimental.pallas import tpu as pltpu
from jax.sharding import Mesh
from jax.sharding import PartitionSpec as P

TILE = 128
BF16, F32, I16, I32 = jnp.bfloat16, jnp.float32, jnp.int16, jnp.int32
FOUR = range(4)
BASE, RUNG_BITS, LARGEST = 14, (64, 32, 16, 8, 4, 2, 1), 32767.0


def partner(value, axis, flip):
    if flip == 0:
        return value
    return lax.ppermute(value, axis, [(i, i ^ flip) for i in range(lax.axis_size(axis))])


def fused_kernel(
    trans_ref, ivar_ref, mask_ref, tangent_ref, coef_ref, coef_t_ref, full_ref, basis_ref,
    own_ref, other_ref, *coef_outs,
):
    step = pl.program_id(0)
    width = trans_ref.shape[1]
    x, y = lax.axis_index("x"), lax.axis_index("yl")
    count = basis_ref.shape[0] // 16
    basis = jnp.concatenate(
        [
            basis_ref[pl.ds(pl.multiple_of(((x ^ i) * 4 + (y ^ j)) * count, count), count), :]
            for i in FOUR
            for j in FOUR
        ],
        axis=0,
    )
    moved = lax.dot_general(
        tangent_ref[...], basis, (((0,), (0,)), ((), ())), preferred_element_type=F32
    ) + jnp.dot(coef_ref[...], full_ref[...], preferred_element_type=F32)
    lanes = lax.broadcasted_iota(I32, mask_ref.shape, 1)
    parts = []
    for t in range(width // TILE):
        part = slice(t * TILE, (t + 1) * TILE)
        here = jnp.where(lanes == step * (width // TILE) + t, mask_ref[...].astype(F32), 0.0)
        column = jnp.sum(here, axis=1, keepdims=True)
        trans = trans_ref[:, part].astype(F32)
        weights = trans * trans * ivar_ref[:, part].astype(F32) * column
        parts.append((weights * moved[:, part]).astype(BF16))
    weighted = jnp.concatenate(parts, axis=1)
    sums = jnp.dot(coef_t_ref[...], weighted, preferred_element_type=F32)
    half = own_ref.shape[0]
    own_ref[...] = sums[:half]
    other_ref[...] = sums[half:]
    term = lax.dot_general(
        basis, weighted, (((1,), (1,)), ((), ())), preferred_element_type=F32
    )
    rows = coef_outs[0].shape[0]

    @pl.when(step == 0)
    def _():
        for i, out in enumerate(coef_outs):
            out[...] = term[i * rows : (i + 1) * rows]

    @pl.when(step > 0)
    def _():
        for i, out in enumerate(coef_outs):
            out[...] += term[i * rows : (i + 1) * rows]


def pack_kernel(own_ref, other_ref, out_ref):
    total = own_ref[...] + other_ref[...]
    cols = total.shape[1]
    largest = jnp.max(jnp.abs(total), axis=1, keepdims=True) * 2.0**-BASE
    scale = jnp.full_like(largest, 2.0**-BASE)
    rung = jnp.zeros_like(largest)
    for bit in RUNG_BITS:
        fits = largest * 2.0**bit <= LARGEST
        largest = jnp.where(fits, largest * 2.0**bit, largest)
        scale = jnp.where(fits, scale * 2.0**bit, scale)
        rung = jnp.where(fits, rung + bit, rung)
    codes = jnp.round(total * scale).astype(I32).astype(I16)
    out_ref[:, :, :cols] = codes.reshape(*out_ref.shape[:2], cols)
    rungs = jnp.broadcast_to(rung, (total.shape[0], TILE)).astype(I32).astype(I16)
    out_ref[:, :, cols:] = rungs.reshape(*out_ref.shape[:2], TILE)


def unpack_kernel(divisor, in_ref, out_ref):
    cols = out_ref.shape[1]
    total = [None] * (cols // TILE)
    for i in range(in_ref.shape[0]):
        rung = in_ref[i, :, cols : cols + TILE].astype(I32)
        inverse = jnp.full(rung.shape, 2.0**BASE, F32)
        for bit in RUNG_BITS:
            inverse = inverse * jnp.where((rung & bit) != 0, F32(2.0**-bit), F32(1.0))
        for t in range(cols // TILE):
            term = in_ref[i, :, t * TILE : (t + 1) * TILE].astype(I32).astype(F32) * inverse
            total[t] = term if i == 0 else total[t] + term
    for t in range(cols // TILE):
        out_ref[:, t * TILE : (t + 1) * TILE] = total[t] * (1.0 / divisor)


def body(transmission, inverse_var, pixel_mask, coef, basis, coef_tangent, basis_tangent):
    rows, cols = transmission.shape
    rank = basis.shape[0]
    half, mine, ours = rank // 2, rank // 32, rank // 16
    exposures, pixels = rows * 32, cols * 16
    core = lax.axis_index("c")

    spread = jnp.broadcast_to(basis_tangent[None], (16, mine, cols))
    arrived = lax.all_to_all(spread, ("yh", "z"), 0, 0, tiled=True)

    tangent = coef_tangent.T
    tangent = jnp.concatenate([partner(tangent, "yl", j) for j in FOUR], axis=0)
    tangent = jnp.concatenate([partner(tangent, "x", i) for i in FOUR], axis=0)

    coef_t = coef.T.reshape(16, 2, mine, rows).transpose(1, 0, 2, 3).reshape(rank, rows)
    coef_p = coef_t.T
    coef_own = jnp.concatenate(
        [
            lax.dynamic_slice_in_dim(coef_t, core * half, half, 0),
            lax.dynamic_slice_in_dim(coef_t, (1 - core) * half, half, 0),
        ],
        axis=0,
    )

    full = lax.all_gather(arrived.reshape(half, cols), "c", axis=0, tiled=True)
    width = 256
    whole = lambda *shape: pl.BlockSpec(shape, lambda i: (0,) * len(shape))
    tall = lambda n: pl.BlockSpec((n, width), lambda i: (0, i))
    own, other, *terms = pl.pallas_call(
        fused_kernel,
        grid=(cols // width,),
        in_specs=[
            tall(rows), tall(rows), whole(rows, cols // TILE), whole(rank, rows),
            whole(rows, rank), whole(rank, rows), tall(rank), tall(rank),
        ],
        out_specs=[tall(half), tall(half)] + [whole(rank // 4, rows)] * 4,
        out_shape=[jax.ShapeDtypeStruct((half, cols), F32)] * 2
        + [jax.ShapeDtypeStruct((rank // 4, rows), F32)] * 4,
        compiler_params=pltpu.CompilerParams(vmem_limit_bytes=24 << 20),
        cost_estimate=pl.CostEstimate(
            flops=8 * rows * cols * rank, bytes_accessed=6 * rows * cols, transcendentals=0
        ),
    )(transmission, inverse_var, pixel_mask, tangent, coef_p, coef_own, full, basis)

    other = lax.ppermute(other, "c", [(0, 1), (1, 0)])
    packed = pl.pallas_call(
        pack_kernel, out_shape=jax.ShapeDtypeStruct((16, mine, cols + TILE), I16)
    )(own, other)
    packed = lax.all_to_all(packed, ("yh", "z"), 0, 0, tiled=True)
    basis_grad = pl.pallas_call(
        lambda *refs: unpack_kernel(math.sqrt(exposures), *refs),
        out_shape=jax.ShapeDtypeStruct((mine, cols), F32),
    )(packed)

    term = sum(partner(terms[i], "x", i) for i in FOUR)
    term = sum(partner(term[j * ours : (j + 1) * ours], "yl", j) for j in FOUR)
    coef_grad = term.T / math.sqrt(pixels)
    return (coef_grad, basis_grad)


def solution(mesh):
    fine = Mesh(mesh.devices.reshape(2, 8, 2, 4, 4), ("yh", "z", "c", "x", "yl"))
    exp, pix = ("yh", "z", "c"), ("x", "yl")
    placed = (
        P(exp, pix),
        P(exp, pix),
        P(exp, pix),
        P(exp, None),
        P(None, pix),
        P(exp, pix),
        P(exp, pix),
    )
    return jax.shard_map(
        body,
        mesh=fine,
        in_specs=placed,
        out_specs=(P(exp, pix), P(exp, pix)),
        check_vma=False,
    )
```

time: 136 us -> 105 us (0.77)
  the two profiles are of different devices: /device:TPU:6 before, /device:TPU:8 now
where the time goes in v2:
time: 105 us; the launch traced here: 104 us
  starting transfers between devices  68.8 us (66%)
  waiting for transfers between devices  11.8 us (11%)
  Pallas kernels  10.4 us (10%)
  local copies, waits for them, and re-layouts  9.28 us (9%)
  blocking collectives  2.57 us (2%)
    ppermute x12, starting transfers between devices, partner(): lax.ppermute(value, axis, [(i, i ^ flip) for i in range(lax.axis_size(axi...  44.3 us
    all_to_all x1, starting transfers between devices, body(): packed = lax.all_to_all(packed, ('yh', 'z'), 0, 0, tiled=True)  12 us
    all_to_all x1, starting transfers between devices, body(): arrived = lax.all_to_all(spread, ('yh', 'z'), 0, 0, tiled=True)  10.5 us
    ppermute x12, waiting for transfers between devices, partner(): lax.ppermute(value, axis, [(i, i ^ flip) for i in range(lax.axis_size(axi...  6.73 us
    unnamed x26, local copies, waits for them, and re-layouts  6.51 us
    pallas_call x1, Pallas kernels, body(): pl.pallas_call(fused_kernel, grid=(cols // width,), in_specs=[tall(rows),...  6.17 us
    all_to_all x1, waiting for transfers between devices, body(): packed = lax.all_to_all(packed, ('yh', 'z'), 0, 0, tiled=True)  4.99 us
    all_gather x1, blocking collectives, body(): full = lax.all_gather(arrived.reshape(half, cols), 'c', axis=0, tiled=True)  2.57 us
  transfers between devices with their start and end apart: 15, of which 5 were waited for; matrix products, arithmetic and copies ran while one was open for 5% of the time, Pallas kernels for 2%

profile of v2, /device:TPU:8, one launch (start us, length us, event | category | flops | bytes accessed | tf_op | source)
XLA Modules:
  0.0 104.5 jit_solution(5374849934102968637)
XLA Ops:
  0.6 3.5 %collective-permute-start.2 = (bf16[16,512]{1,0:T(8,128)(2,1)}, bf16[16,512]{1,0:T(8,128)(2,1)S(1)}, u32[]{:S(2)}, u32[]{:S(2)}) collective-permute-start(bf16[16,512]{1,0:T(8,128)(2,1)} %bitcast.16), channel_id=1, source_target_pairs={{0,3},{1,2},{2,1},{3,0},{4,7},{5,6},{6,5},{7,4},{8,11},{9,10},{10,... | collective-permute-start | bytes 49160 | tf_op jit(solution)/shard_map/ppermute | solution.py:20
  4.1 8.5 %collective-permute-start.1 = (bf16[16,512]{1,0:T(8,128)(2,1)}, bf16[16,512]{1,0:T(8,128)(2,1)S(1)}, u32[]{:S(2)}, u32[]{:S(2)}) collective-permute-start(bf16[16,512]{1,0:T(8,128)(2,1)} %bitcast.17), channel_id=1, source_target_pairs={{0,2},{1,3},{2,0},{3,1},{4,6},{5,7},{6,4},{7,5},{8,10},{9,11},{10,... | collective-permute-start | bytes 49160 | tf_op jit(solution)/shard_map/ppermute | solution.py:20
  12.7 1.9 %collective-permute-start = (bf16[16,512]{1,0:T(8,128)(2,1)}, bf16[16,512]{1,0:T(8,128)(2,1)S(1)}, u32[]{:S(2)}, u32[]{:S(2)}) collective-permute-start(bf16[16,512]{1,0:T(8,128)(2,1)} %bitcast.18), channel_id=1, source_target_pairs={{0,1},{1,0},{2,3},{3,2},{4,5},{5,4},{6,7},{7,6},{8,9},{9,8},{10,11... | collective-permute-start | bytes 49160 | tf_op jit(solution)/shard_map/ppermute | solution.py:20
  14.6 1.5 %broadcast_in_dim.2 = bf16[16,8,1536]{2,1,0:T(8,128)(2,1)} broadcast(bf16[8,1536]{1,0:T(8,128)(2,1)} %param.13), dimensions={1,2} | broadcast | bytes 417792 | tf_op jit(solution)/shard_map/broadcast_in_dim | solution.py:111
  16.1 10.5 %all-to-all-start = ((bf16[16,8,1536]{2,1,0:T(8,128)(2,1)}), bf16[16,8,1536]{2,1,0:T(8,128)(2,1)}, u32[]{:S(2)}, u32[]{:S(2)}) async-start(bf16[16,8,1536]{2,1,0:T(8,128)(2,1)} %broadcast_in_dim.2), calls=%async_computation | async-start | bytes 786432 | tf_op jit(solution)/shard_map/all_to_all | solution.py:112
  30.5 4.7 %collective-permute-start.5 = (bf16[64,512]{1,0:T(8,128)(2,1)S(1)}, bf16[64,512]{1,0:T(8,128)(2,1)S(1)}, u32[]{:S(2)}, u32[]{:S(2)}) collective-permute-start(bf16[64,512]{1,0:T(8,128)(2,1)S(1)} %pad_maximum_fusion.1), channel_id=1, source_target_pairs={{0,12},{4,8},{8,4},{12,0},{1,13},{5,9},{9,5},{13,1},{2,14},{6,10},... | collective-permute-start | bytes 196616 | tf_op jit(solution)/shard_map/ppermute | solution.py:20
  35.2 2.7 %collective-permute-start.4 = (bf16[64,512]{1,0:T(8,128)(2,1)S(1)}, bf16[64,512]{1,0:T(8,128)(2,1)S(1)}, u32[]{:S(2)}, u32[]{:S(2)}) collective-permute-start(bf16[64,512]{1,0:T(8,128)(2,1)S(1)} %pad_maximum_fusion.1), channel_id=1, source_target_pairs={{0,8},{4,12},{8,0},{12,4},{1,9},{5,13},{9,1},{13,5},{2,10},{6,14},... | collective-permute-start | bytes 196616 | tf_op jit(solution)/shard_map/ppermute | solution.py:20
  37.9 2.4 %collective-permute-start.3 = (bf16[64,512]{1,0:T(8,128)(2,1)S(1)}, bf16[64,512]{1,0:T(8,128)(2,1)S(1)}, u32[]{:S(2)}, u32[]{:S(2)}) collective-permute-start(bf16[64,512]{1,0:T(8,128)(2,1)S(1)} %pad_maximum_fusion.1), channel_id=1, source_target_pairs={{0,4},{4,0},{8,12},{12,8},{1,5},{5,1},{9,13},{13,9},{2,6},{6,2},{1... | collective-permute-start | bytes 196616 | tf_op jit(solution)/shard_map/ppermute | solution.py:20
  40.4 3.7 %collective-permute-done.3 = bf16[64,512]{1,0:T(8,128)(2,1)S(1)} collective-permute-done((bf16[64,512]{1,0:T(8,128)(2,1)S(1)}, bf16[64,512]{1,0:T(8,128)(2,1)S(1)}, u32[]{:S(2)}, u32[]{:S(2)}) %collective-permute-start.3) | collective-permute-done | bytes 65568 | tf_op jit(solution)/shard_map/ppermute | solution.py:20
  44.1 2.6 %all_gather.3.full_ref = bf16[256,1536]{1,0:T(8,128)(2,1)S(1)} all-gather(bf16[128,1536]{1,0:T(8,128)(2,1)} %bitcast.6), channel_id=1, replica_groups=mesh['yh'=2,'z'=8,'c'=2,'x'=4,'yl'=4] {'c'}, dimensions={0}, use_global_device_ids=true | all-gather | bytes 1179648 | tf_op jit(solution)/shard_map/all_gather | solution.py:128
  46.7 1.4 %copy-done.2 = bf16[512,1536]{1,0:T(8,128)(2,1)S(1)} copy-done((bf16[512,1536]{1,0:T(8,128)(2,1)S(1)}, bf16[512,1536]{1,0:T(8,128)(2,1)}, u32[]{:S(2)}) %copy-start.2) | copy-done | bytes 1572888
  48.1 6.2 %shard_map.86 = (f32[128,1536]{1,0:T(8,128)S(1)}, f32[128,1536]{1,0:T(8,128)S(1)}, f32[64,512]{1,0:T(8,128)S(1)}, f32[64,512]{1,0:T(8,128)}, f32[64,512]{1,0:T(8,128)}, /*index=5*/f32[64,512]{1,0:T(8,128)}) custom-call(bf16[512,1536]{1,0:T(8,128)(2,1)S(1)} %copy-done.1, bf16[512,1536]{1,0:T(8,128)(2,1)S(1)} %copy-done.2, s32[512,12]{1,0:T(8,128)S(1)} %copy.14.mask_ref, ...), custom_call_target="tpu_custom_call" | custom-call | flops 1610612736 | bytes 4718592 | tf_op jit(solution)/shard_map/pallas_call | solution.py:132
  55.2 2.0 %collective-permute-start.12 = (f32[128,1536]{1,0:T(8,128)S(1)}, f32[128,1536]{1,0:T(8,128)S(1)}, u32[]{:S(2)}, u32[]{:S(2)}) collective-permute-start(f32[128,1536]{1,0:T(8,128)S(1)} %get-tuple-element.13), channel_id=1, source_target_pairs={{0,16},{16,0},{1,17},{17,1},{2,18},{18,2},{3,19},{19,3},{4,20},{20... | collective-permute-start | bytes 2359304 | tf_op jit(solution)/shard_map/ppermute | solution.py:148
  57.2 3.4 %collective-permute-start.6 = (f32[64,512]{1,0:T(8,128)}, f32[64,512]{1,0:T(8,128)S(1)}, u32[]{:S(2)}, u32[]{:S(2)}) collective-permute-start(f32[64,512]{1,0:T(8,128)} %get-tuple-element.9), channel_id=1, source_target_pairs={{0,4},{4,0},{8,12},{12,8},{1,5},{5,1},{9,13},{13,9},{2,6},{6,2},{1... | collective-permute-start | bytes 393224 | tf_op jit(solution)/shard_map/ppermute | solution.py:20
  60.6 4.6 %collective-permute-start.7 = (f32[64,512]{1,0:T(8,128)}, f32[64,512]{1,0:T(8,128)S(1)}, u32[]{:S(2)}, u32[]{:S(2)}) collective-permute-start(f32[64,512]{1,0:T(8,128)} %get-tuple-element.10), channel_id=1, source_target_pairs={{0,8},{4,12},{8,0},{12,4},{1,9},{5,13},{9,1},{13,5},{2,10},{6,14},... | collective-permute-start | bytes 393224 | tf_op jit(solution)/shard_map/ppermute | solution.py:20
  65.3 2.4 %collective-permute-start.8 = (f32[64,512]{1,0:T(8,128)}, f32[64,512]{1,0:T(8,128)S(1)}, u32[]{:S(2)}, u32[]{:S(2)}) collective-permute-start(f32[64,512]{1,0:T(8,128)} %get-tuple-element.11), channel_id=1, source_target_pairs={{0,12},{4,8},{8,4},{12,0},{1,13},{5,9},{9,5},{13,1},{2,14},{6,10},... | collective-permute-start | bytes 393224 | tf_op jit(solution)/shard_map/ppermute | solution.py:20
  68.6 2.4 %shard_map.87 = s16[16,8,1664]{2,1,0:T(8,128)(2,1)} custom-call(f32[128,1536]{1,0:T(8,128)} %copy-done, f32[128,1536]{1,0:T(8,128)} %copy-done.6), custom_call_target="tpu_custom_call" | custom-call | tf_op jit(solution)/shard_map/pallas_call | solution.py:149
  71.0 12.0 %all-to-all-start.1 = ((s16[16,8,1664]{2,1,0:T(8,128)(2,1)}), s16[16,8,1664]{2,1,0:T(8,128)(2,1)S(1)}, u32[]{:S(2)}, u32[]{:S(2)}) async-start(s16[16,8,1664]{2,1,0:T(8,128)(2,1)} %shard_map.87), calls=%async_computation.1 | async-start | bytes 851968 | tf_op jit(solution)/shard_map/all_to_all | solution.py:152
  83.1 3.9 %collective-permute-start.9 = (f32[16,512]{1,0:T(8,128)S(1)}, f32[16,512]{1,0:T(8,128)S(1)}, u32[]{:S(2)}, u32[]{:S(2)}) collective-permute-start(f32[16,512]{1,0:T(8,128)S(1)} %get-tuple-element.16), channel_id=1, source_target_pairs={{0,1},{1,0},{2,3},{3,2},{4,5},{5,4},{6,7},{7,6},{8,9},{9,8},{10,11... | collective-permute-start | bytes 98312 | tf_op jit(solution)/shard_map/ppermute | solution.py:20
  87.0 1.9 %collective-permute-start.11 = (f32[16,512]{1,0:T(8,128)S(1)}, f32[16,512]{1,0:T(8,128)S(1)}, u32[]{:S(2)}, u32[]{:S(2)}) collective-permute-start(f32[16,512]{1,0:T(8,128)S(1)} %get-tuple-element.17), channel_id=1, source_target_pairs={{0,3},{1,2},{2,1},{3,0},{4,7},{5,6},{6,5},{7,4},{8,11},{9,10},{10,... | collective-permute-start | bytes 98312 | tf_op jit(solution)/shard_map/ppermute | solution.py:20
  89.0 4.3 %collective-permute-start.10 = (f32[16,512]{1,0:T(8,128)S(1)}, f32[16,512]{1,0:T(8,128)S(1)}, u32[]{:S(2)}, u32[]{:S(2)}) collective-permute-start(f32[16,512]{1,0:T(8,128)S(1)} %get-tuple-element.18), channel_id=1, source_target_pairs={{0,2},{1,3},{2,0},{3,1},{4,6},{5,7},{6,4},{7,5},{8,10},{9,11},{10,... | collective-permute-start | bytes 98312 | tf_op jit(solution)/shard_map/ppermute | solution.py:20
  93.8 1.3 %collective-permute-done.11 = f32[16,512]{1,0:T(8,128)S(1)} collective-permute-done((f32[16,512]{1,0:T(8,128)S(1)}, f32[16,512]{1,0:T(8,128)S(1)}, u32[]{:S(2)}, u32[]{:S(2)}) %collective-permute-start.11) | collective-permute-done | bytes 32800 | tf_op jit(solution)/shard_map/ppermute | solution.py:20
  96.9 5.0 %all-to-all-done.1.refs_0_ = s16[16,8,1664]{2,1,0:T(8,128)(2,1)S(1)} async-done(((s16[16,8,1664]{2,1,0:T(8,128)(2,1)}), s16[16,8,1664]{2,1,0:T(8,128)(2,1)S(1)}, u32[]{:S(2)}, u32[]{:S(2)}) %all-to-all-start.1) | async-done | bytes 426016 | tf_op jit(solution)/shard_map/all_to_all | solution.py:152
  102.7 1.8 %shard_map.88 = f32[8,1536]{1,0:T(8,128)} custom-call(s16[16,8,1664]{2,1,0:T(8,128)(2,1)} %copy-done.5), custom_call_target="tpu_custom_call" | custom-call | tf_op jit(solution)/shard_map/pallas_call | solution.py:153
  (46 shorter events, 8.8 us)
Async XLA Ops:
  0.6 29.8 %collective-permute-start.2 = (bf16[16,512]{1,0:T(8,128)(2,1)}, bf16[16,512]{1,0:T(8,128)(2,1)S(1)}, u32[]{:S(2)}, u32[]{:S(2)}) collective-permute-start(bf16[16,512]{1,0:T(8,128)(2,1)} %bitcast.16), channel_id=1, source_target_pairs={{0,3},{1,2},{2,1},{3,0},{4,7},{5,6},{6,5},{7,4},{8,11},{9,10},{10,... | collective-permute-start | bytes 49160 | tf_op jit(solution)/shard_map/ppermute | solution.py:20
  4.1 26.3 %collective-permute-start.1 = (bf16[16,512]{1,0:T(8,128)(2,1)}, bf16[16,512]{1,0:T(8,128)(2,1)S(1)}, u32[]{:S(2)}, u32[]{:S(2)}) collective-permute-start(bf16[16,512]{1,0:T(8,128)(2,1)} %bitcast.17), channel_id=1, source_target_pairs={{0,2},{1,3},{2,0},{3,1},{4,6},{5,7},{6,4},{7,5},{8,10},{9,11},{10,... | collective-permute-start | bytes 49160 | tf_op jit(solution)/shard_map/ppermute | solution.py:20
  12.7 17.8 %collective-permute-start = (bf16[16,512]{1,0:T(8,128)(2,1)}, bf16[16,512]{1,0:T(8,128)(2,1)S(1)}, u32[]{:S(2)}, u32[]{:S(2)}) collective-permute-start(bf16[16,512]{1,0:T(8,128)(2,1)} %bitcast.18), channel_id=1, source_target_pairs={{0,1},{1,0},{2,3},{3,2},{4,5},{5,4},{6,7},{7,6},{8,9},{9,8},{10,11... | collective-permute-start | bytes 49160 | tf_op jit(solution)/shard_map/ppermute | solution.py:20
  16.1 12.5 %copy-start.8 = (s32[512,12]{0,1:T(8,128)S(1)}, s32[512,12]{0,1:T(8,128)}, u32[]{:S(2)}) copy-start(s32[512,12]{0,1:T(8,128)} %param.9) | copy-start | bytes 73732
  16.1 28.0 %all-to-all-start = ((bf16[16,8,1536]{2,1,0:T(8,128)(2,1)}), bf16[16,8,1536]{2,1,0:T(8,128)(2,1)}, u32[]{:S(2)}, u32[]{:S(2)}) async-start(bf16[16,8,1536]{2,1,0:T(8,128)(2,1)} %broadcast_in_dim.2), calls=%async_computation | async-start | bytes 786432 | tf_op jit(solution)/shard_map/all_to_all | solution.py:112
  26.6 3.9 %copy-start.7 = (bf16[512,16]{0,1:T(8,128)(2,1)S(1)}, bf16[512,16]{0,1:T(8,128)(2,1)}, u32[]{:S(2)}) copy-start(bf16[512,16]{0,1:T(8,128)(2,1)} %param.12) | copy-start | bytes 49156
  28.5 0.7 copy-start.4
  28.6 18.1 %copy-start.1 = (bf16[512,1536]{1,0:T(8,128)(2,1)S(1)}, bf16[512,1536]{1,0:T(8,128)(2,1)}, u32[]{:S(2)}) copy-start(bf16[512,1536]{1,0:T(8,128)(2,1)} %trans_ref.1) | copy-start | bytes 4718596
  28.6 18.1 %copy-start.3 = (bf16[256,1536]{1,0:T(8,128)(2,1)S(1)}, bf16[256,1536]{1,0:T(8,128)(2,1)}, u32[]{:S(2)}) copy-start(bf16[256,1536]{1,0:T(8,128)(2,1)} %basis_ref.1) | copy-start | bytes 2359300
  30.5 13.6 %collective-permute-start.5 = (bf16[64,512]{1,0:T(8,128)(2,1)S(1)}, bf16[64,512]{1,0:T(8,128)(2,1)S(1)}, u32[]{:S(2)}, u32[]{:S(2)}) collective-permute-start(bf16[64,512]{1,0:T(8,128)(2,1)S(1)} %pad_maximum_fusion.1), channel_id=1, source_target_pairs={{0,12},{4,8},{8,4},{12,0},{1,13},{5,9},{9,5},{13,1},{2,14},{6,10},... | collective-permute-start | bytes 196616 | tf_op jit(solution)/shard_map/ppermute | solution.py:20
  35.2 8.9 %collective-permute-start.4 = (bf16[64,512]{1,0:T(8,128)(2,1)S(1)}, bf16[64,512]{1,0:T(8,128)(2,1)S(1)}, u32[]{:S(2)}, u32[]{:S(2)}) collective-permute-start(bf16[64,512]{1,0:T(8,128)(2,1)S(1)} %pad_maximum_fusion.1), channel_id=1, source_target_pairs={{0,8},{4,12},{8,0},{12,4},{1,9},{5,13},{9,1},{13,5},{2,10},{6,14},... | collective-permute-start | bytes 196616 | tf_op jit(solution)/shard_map/ppermute | solution.py:20
  37.9 6.2 %collective-permute-start.3 = (bf16[64,512]{1,0:T(8,128)(2,1)S(1)}, bf16[64,512]{1,0:T(8,128)(2,1)S(1)}, u32[]{:S(2)}, u32[]{:S(2)}) collective-permute-start(bf16[64,512]{1,0:T(8,128)(2,1)S(1)} %pad_maximum_fusion.1), channel_id=1, source_target_pairs={{0,4},{4,0},{8,12},{12,8},{1,5},{5,1},{9,13},{13,9},{2,6},{6,2},{1... | collective-permute-start | bytes 196616 | tf_op jit(solution)/shard_map/ppermute | solution.py:20
  46.7 1.4 %copy-start.2 = (bf16[512,1536]{1,0:T(8,128)(2,1)S(1)}, bf16[512,1536]{1,0:T(8,128)(2,1)}, u32[]{:S(2)}) copy-start(bf16[512,1536]{1,0:T(8,128)(2,1)} %ivar_ref.1) | copy-start | bytes 4718596
  54.3 0.9 copy-start
  55.2 12.5 %collective-permute-start.12 = (f32[128,1536]{1,0:T(8,128)S(1)}, f32[128,1536]{1,0:T(8,128)S(1)}, u32[]{:S(2)}, u32[]{:S(2)}) collective-permute-start(f32[128,1536]{1,0:T(8,128)S(1)} %get-tuple-element.13), channel_id=1, source_target_pairs={{0,16},{16,0},{1,17},{17,1},{2,18},{18,2},{3,19},{19,3},{4,20},{20... | collective-permute-start | bytes 2359304 | tf_op jit(solution)/shard_map/ppermute | solution.py:148
  57.2 25.8 %collective-permute-start.6 = (f32[64,512]{1,0:T(8,128)}, f32[64,512]{1,0:T(8,128)S(1)}, u32[]{:S(2)}, u32[]{:S(2)}) collective-permute-start(f32[64,512]{1,0:T(8,128)} %get-tuple-element.9), channel_id=1, source_target_pairs={{0,4},{4,0},{8,12},{12,8},{1,5},{5,1},{9,13},{13,9},{2,6},{6,2},{1... | collective-permute-start | bytes 393224 | tf_op jit(solution)/shard_map/ppermute | solution.py:20
  60.6 22.4 %collective-permute-start.7 = (f32[64,512]{1,0:T(8,128)}, f32[64,512]{1,0:T(8,128)S(1)}, u32[]{:S(2)}, u32[]{:S(2)}) collective-permute-start(f32[64,512]{1,0:T(8,128)} %get-tuple-element.10), channel_id=1, source_target_pairs={{0,8},{4,12},{8,0},{12,4},{1,9},{5,13},{9,1},{13,5},{2,10},{6,14},... | collective-permute-start | bytes 393224 | tf_op jit(solution)/shard_map/ppermute | solution.py:20
  65.3 17.7 %collective-permute-start.8 = (f32[64,512]{1,0:T(8,128)}, f32[64,512]{1,0:T(8,128)S(1)}, u32[]{:S(2)}, u32[]{:S(2)}) collective-permute-start(f32[64,512]{1,0:T(8,128)} %get-tuple-element.11), channel_id=1, source_target_pairs={{0,12},{4,8},{8,4},{12,0},{1,13},{5,9},{9,5},{13,1},{2,14},{6,10},... | collective-permute-start | bytes 393224 | tf_op jit(solution)/shard_map/ppermute | solution.py:20
  67.7 0.9 copy-start.6
  71.0 30.9 %all-to-all-start.1 = ((s16[16,8,1664]{2,1,0:T(8,128)(2,1)}), s16[16,8,1664]{2,1,0:T(8,128)(2,1)S(1)}, u32[]{:S(2)}, u32[]{:S(2)}) async-start(s16[16,8,1664]{2,1,0:T(8,128)(2,1)} %shard_map.87), calls=%async_computation.1 | async-start | bytes 851968 | tf_op jit(solution)/shard_map/all_to_all | solution.py:152
  83.1 10.7 %collective-permute-start.9 = (f32[16,512]{1,0:T(8,128)S(1)}, f32[16,512]{1,0:T(8,128)S(1)}, u32[]{:S(2)}, u32[]{:S(2)}) collective-permute-start(f32[16,512]{1,0:T(8,128)S(1)} %get-tuple-element.16), channel_id=1, source_target_pairs={{0,1},{1,0},{2,3},{3,2},{4,5},{5,4},{6,7},{7,6},{8,9},{9,8},{10,11... | collective-permute-start | bytes 98312 | tf_op jit(solution)/shard_map/ppermute | solution.py:20
  87.0 8.1 %collective-permute-start.11 = (f32[16,512]{1,0:T(8,128)S(1)}, f32[16,512]{1,0:T(8,128)S(1)}, u32[]{:S(2)}, u32[]{:S(2)}) collective-permute-start(f32[16,512]{1,0:T(8,128)S(1)} %get-tuple-element.17), channel_id=1, source_target_pairs={{0,3},{1,2},{2,1},{3,0},{4,7},{5,6},{6,5},{7,4},{8,11},{9,10},{10,... | collective-permute-start | bytes 98312 | tf_op jit(solution)/shard_map/ppermute | solution.py:20
  89.0 7.3 %collective-permute-start.10 = (f32[16,512]{1,0:T(8,128)S(1)}, f32[16,512]{1,0:T(8,128)S(1)}, u32[]{:S(2)}, u32[]{:S(2)}) collective-permute-start(f32[16,512]{1,0:T(8,128)S(1)} %get-tuple-element.18), channel_id=1, source_target_pairs={{0,2},{1,3},{2,0},{3,1},{4,6},{5,7},{6,4},{7,5},{8,10},{9,11},{10,... | collective-permute-start | bytes 98312 | tf_op jit(solution)/shard_map/ppermute | solution.py:20
  101.9 0.8 copy-start.5

commit v3 on v2

v3 whole, which is shorter than its diff:
```python
import math

import jax
import jax.numpy as jnp
from jax import lax
from jax.experimental import pallas as pl
from jax.experimental.pallas import tpu as pltpu
from jax.sharding import Mesh
from jax.sharding import PartitionSpec as P

TILE = 128
BF16, F32, I16, I32 = jnp.bfloat16, jnp.float32, jnp.int16, jnp.int32
BASE, RUNG_BITS, LARGEST = 14, (64, 32, 16, 8, 4, 2, 1), 32767.0


def partner(value, axis, flip):
    return lax.ppermute(value, axis, [(i, i ^ flip) for i in range(lax.axis_size(axis))])


def first_kernel(trans_ref, ivar_ref, mask_ref, tangent_ref, basis_ref, weights_ref, moved_ref):
    step = pl.program_id(0)
    tiles = trans_ref.shape[1] // TILE
    lanes = lax.broadcasted_iota(I32, mask_ref.shape, 1)
    mask = mask_ref[...].astype(F32)
    for t in range(tiles):
        part = slice(t * TILE, (t + 1) * TILE)
        column = jnp.sum(jnp.where(lanes == step * tiles + t, mask, 0.0), axis=1, keepdims=True)
        trans = trans_ref[:, part].astype(F32)
        weights_ref[:, part] = trans * trans * ivar_ref[:, part].astype(F32) * column
    moved_ref[...] = lax.dot_general(
        tangent_ref[...], basis_ref[...], (((0,), (0,)), ((), ())), preferred_element_type=F32
    )


def second_kernel(
    weights_ref, moved_ref, coef_ref, coef_t_ref, full_ref, basis_ref,
    own_ref, other_ref, kept_ref, given_ref,
):
    moved = moved_ref[...] + jnp.dot(coef_ref[...], full_ref[...], preferred_element_type=F32)
    weighted = (weights_ref[...] * moved).astype(BF16)
    half = own_ref.shape[0]
    core = lax.axis_index("c")
    for out, which in ((own_ref, core), (other_ref, 1 - core)):
        rows = pl.ds(pl.multiple_of(which * half, half), half)
        out[...] = jnp.dot(coef_t_ref[rows, :], weighted, preferred_element_type=F32)
    x, y = lax.axis_index("x"), lax.axis_index("yl")
    count = basis_ref.shape[0] // 16
    for out, a in ((kept_ref, 0), (given_ref, 1)):
        basis = jnp.concatenate(
            [
                basis_ref[
                    pl.ds(pl.multiple_of(((x ^ (a + 2 * c)) * 4 + (y ^ (b + 2 * d))) * count, count), count), :
                ]
                for b in (0, 1)
                for c in (0, 1)
                for d in (0, 1)
            ],
            axis=0,
        )
        term = lax.dot_general(
            basis, weighted, (((1,), (1,)), ((), ())), preferred_element_type=F32
        )

        @pl.when(pl.program_id(0) == 0)
        def _():
            out[...] = term

        @pl.when(pl.program_id(0) > 0)
        def _():
            out[...] += term


def pack_kernel(own_ref, other_ref, out_ref):
    total = own_ref[...] + other_ref[...]
    cols = total.shape[1]
    largest = jnp.max(jnp.abs(total), axis=1, keepdims=True) * 2.0**-BASE
    scale = jnp.full_like(largest, 2.0**-BASE)
    rung = jnp.zeros_like(largest)
    for bit in RUNG_BITS:
        fits = largest * 2.0**bit <= LARGEST
        largest = jnp.where(fits, largest * 2.0**bit, largest)
        scale = jnp.where(fits, scale * 2.0**bit, scale)
        rung = jnp.where(fits, rung + bit, rung)
    codes = jnp.round(total * scale).astype(I32).astype(I16)
    out_ref[:, :, :cols] = codes.reshape(*out_ref.shape[:2], cols)
    rungs = jnp.broadcast_to(rung, (total.shape[0], TILE)).astype(I32).astype(I16)
    out_ref[:, :, cols:] = rungs.reshape(*out_ref.shape[:2], TILE)


def unpack_kernel(in_ref, own_ref, other_ref):
    count, cols = own_ref.shape
    first = lax.axis_index("yh") == 0
    total = [None] * (cols // TILE)
    for i in range(in_ref.shape[0]):
        rung = in_ref[i, :, cols : cols + TILE].astype(I32)
        inverse = jnp.full(rung.shape, 2.0**BASE, F32)
        for bit in RUNG_BITS:
            inverse = inverse * jnp.where((rung & bit) != 0, F32(2.0**-bit), F32(1.0))
        for t in range(cols // TILE):
            term = in_ref[i, :, t * TILE : (t + 1) * TILE].astype(I32).astype(F32) * inverse
            total[t] = term if i == 0 else total[t] + term
    for t in range(cols // TILE):
        part = slice(t * TILE, (t + 1) * TILE)
        low, high = total[t][:count], total[t][count:]
        own_ref[:, part] = jnp.where(first, low, high)
        other_ref[:, part] = jnp.where(first, high, low)


def body(transmission, inverse_var, pixel_mask, coef, basis, coef_tangent, basis_tangent):
    rows, cols = transmission.shape
    rank = basis.shape[0]
    half, mine, ours = rank // 2, rank // 32, rank // 16
    exposures, pixels = rows * 32, cols * 16

    across = partner(basis_tangent, "yh", 1)
    tangent = jnp.broadcast_to(coef_tangent.T[None], (16, ours, rows))
    tangent = lax.all_to_all(tangent, ("x", "yl"), 0, 0, tiled=True).reshape(rank, rows)
    across, tangent = lax.optimization_barrier((across, tangent))

    first = lax.axis_index("yh") == 0
    pair = jnp.stack(
        [jnp.where(first, basis_tangent, across), jnp.where(first, across, basis_tangent)]
    ).reshape(1, 2 * mine, cols)
    arrived = lax.all_to_all(jnp.broadcast_to(pair, (8, 2 * mine, cols)), "z", 0, 0, tiled=True)
    full = lax.all_gather(arrived.reshape(half, cols), "c", axis=0, tiled=True)
    coef_t = coef.T.reshape(2, 8, 2, mine, rows).transpose(2, 1, 0, 3, 4).reshape(rank, rows)
    coef_p = coef_t.T

    width = 256
    whole = lambda *shape: pl.BlockSpec(shape, lambda i: (0,) * len(shape))
    tall = lambda n: pl.BlockSpec((n, width), lambda i: (0, i))
    params = pltpu.CompilerParams(vmem_limit_bytes=24 << 20)
    weights, moved = pl.pallas_call(
        first_kernel,
        grid=(cols // width,),
        in_specs=[tall(rows), tall(rows), whole(rows, cols // TILE), whole(rank, rows), tall(rank)],
        out_specs=[tall(rows), tall(rows)],
        out_shape=[pltpu.HBM((rows, cols), F32)] * 2,
        compiler_params=params,
        cost_estimate=pl.CostEstimate(
            flops=2 * rows * cols * rank, bytes_accessed=12 * rows * cols, transcendentals=0
        ),
    )(transmission, inverse_var, pixel_mask, tangent, basis)
    own, other, kept, given = pl.pallas_call(
        second_kernel,
        grid=(cols // width,),
        in_specs=[
            tall(rows), tall(rows), whole(rows, rank), whole(rank, rows), tall(rank), tall(rank),
        ],
        out_specs=[tall(half), tall(half), whole(half, rows), whole(half, rows)],
        out_shape=[jax.ShapeDtypeStruct((half, cols), F32)] * 2
        + [jax.ShapeDtypeStruct((half, rows), F32)] * 2,
        compiler_params=params,
        cost_estimate=pl.CostEstimate(
            flops=6 * rows * cols * rank, bytes_accessed=8 * rows * cols, transcendentals=0
        ),
    )(weights, moved, coef_p, coef_t, full, basis)

    small = pltpu.CompilerParams(vmem_limit_bytes=8 << 20)
    other = partner(other, "c", 1)
    packed = pl.pallas_call(
        pack_kernel,
        out_shape=jax.ShapeDtypeStruct((8, 2 * mine, cols + TILE), I16),
        compiler_params=small,
    )(own, other)
    packed = lax.all_to_all(packed, "z", 0, 0, tiled=True)
    own, other = pl.pallas_call(
        unpack_kernel,
        out_shape=[jax.ShapeDtypeStruct((mine, cols), F32)] * 2,
        compiler_params=small,
    )(packed)
    basis_grad = (own + partner(other, "yh", 1)) * (1.0 / math.sqrt(exposures))

    for axis, flip in (("x", 1), ("yl", 1), ("x", 2), ("yl", 2)):
        total = kept + partner(given, axis, flip)
        n = total.shape[0] // 2
        kept, given = total[:n], total[n:]
    coef_grad = total.T / math.sqrt(pixels)
    return (coef_grad, basis_grad)


def solution(mesh):
    fine = Mesh(mesh.devices.reshape(2, 8, 2, 4, 4), ("yh", "z", "c", "x", "yl"))
    exp, pix = ("yh", "z", "c"), ("x", "yl")
    placed = (
        P(exp, pix),
        P(exp, pix),
        P(exp, pix),
        P(exp, None),
        P(None, pix),
        P(exp, pix),
        P(exp, pix),
    )
    return jax.shard_map(
        body,
        mesh=fine,
        in_specs=placed,
        out_specs=(P(exp, pix), P(exp, pix)),
        check_vma=False,
    )
```

time: 105 us -> 100 us (0.952)
  the two profiles are of different devices: /device:TPU:8 before, /device:TPU:6 now
where the time goes in v3:
time: 100 us; the launch traced here: 99.5 us
  starting transfers between devices  46.6 us (47%)
  waiting for transfers between devices  26 us (26%)
  Pallas kernels  11.6 us (12%)
  local copies, waits for them, and re-layouts  9.73 us (10%)
  blocking collectives  2.57 us (3%)
  other arithmetic  2.07 us (2%)
    ppermute x7, starting transfers between devices, partner(): lax.ppermute(value, axis, [(i, i ^ flip) for i in range(lax.axis_size(axi...  25.1 us
    ppermute x7, waiting for transfers between devices, partner(): lax.ppermute(value, axis, [(i, i ^ flip) for i in range(lax.axis_size(axi...  21.1 us
    all_to_all x1, starting transfers between devices, body(): lax.all_to_all(tangent, ('x', 'yl'), 0, 0, tiled=True).reshape(rank, rows)  9.25 us
    all_to_all x1, starting transfers between devices, body(): lax.all_to_all(jnp.broadcast_to(pair, (8, 2 * mine, cols)), 'z', 0, 0, ti...  8.78 us
    unnamed x12, local copies, waits for them, and re-layouts  7.17 us
    pallas_call x1, Pallas kernels, body(): pl.pallas_call(second_kernel, grid=(cols // width,), in_specs=[tall(rows)...  5.82 us
    all_to_all x1, waiting for transfers between devices, body(): lax.all_to_all(jnp.broadcast_to(pair, (8, 2 * mine, cols)), 'z', 0, 0, ti...  4.94 us
    pallas_call x1, Pallas kernels, body(): pl.pallas_call(first_kernel, grid=(cols // width,), in_specs=[tall(rows),...  4.55 us
  transfers between devices with their start and end apart: 10, of which 6 were waited for; matrix products, arithmetic and copies ran while one was open for 3% of the time, Pallas kernels for 6%

profile of v3, /device:TPU:6, one launch (start us, length us, event | category | flops | bytes accessed | tf_op | source)
XLA Modules:
  0.0 99.5 jit_solution(10560089475688521729)
XLA Ops:
  0.6 1.6 %broadcast_in_dim.6 = bf16[16,16,512]{2,1,0:T(8,128)(2,1)} broadcast(bf16[16,512]{1,0:T(8,128)(2,1)} %bitcast.23), dimensions={1,2} | broadcast | bytes 278528 | tf_op jit(solution)/shard_map/broadcast_in_dim | solution.py:116
  2.2 9.2 %all-to-all-start = ((bf16[16,16,512]{2,1,0:T(8,128)(2,1)}), bf16[16,16,512]{2,1,0:T(8,128)(2,1)S(1)}, u32[]{:S(2)}, u32[]{:S(2)}) async-start(bf16[16,16,512]{2,1,0:T(8,128)(2,1)} %broadcast_in_dim.6), calls=%async_computation | async-start | bytes 524288 | tf_op jit(solution)/shard_map/all_to_all | solution.py:117
  11.5 3.6 %collective-permute-start = (bf16[8,1536]{1,0:T(8,128)(2,1)}, bf16[8,1536]{1,0:T(8,128)(2,1)S(1)}, u32[]{:S(2)}, u32[]{:S(2)}) collective-permute-start(bf16[8,1536]{1,0:T(8,128)(2,1)} %param.13), channel_id=1, source_target_pairs={{0,256},{256,0},{1,257},{257,1},{2,258},{258,2},{3,259},{259,3},{4... | collective-permute-start | bytes 73736 | tf_op jit(solution)/shard_map/ppermute | solution.py:17
  15.1 6.3 %collective-permute-done = bf16[8,1536]{1,0:T(8,128)(2,1)S(1)} collective-permute-done((bf16[8,1536]{1,0:T(8,128)(2,1)}, bf16[8,1536]{1,0:T(8,128)(2,1)S(1)}, u32[]{:S(2)}, u32[]{:S(2)}) %collective-permute-start) | collective-permute-done | bytes 24608 | tf_op jit(solution)/shard_map/ppermute | solution.py:17
  23.0 8.8 %all-to-all-start.1 = ((bf16[8,16,1536]{2,1,0:T(8,128)(2,1)}), bf16[8,16,1536]{2,1,0:T(8,128)(2,1)}, u32[]{:S(2)}, u32[]{:S(2)}) async-start(bf16[8,16,1536]{2,1,0:T(8,128)(2,1)} %broadcast_in_dim.15), calls=%async_computation.1 | async-start | bytes 786432 | tf_op jit(solution)/shard_map/all_to_all | solution.py:124
  32.7 1.1 %copy.13 = bf16[512,256]{0,1:T(8,128)(2,1)S(1)} copy(bf16[512,256]{1,0:T(8,128)(2,1)} %param.10) | data formatting | bytes 524288 | tf_op args[3]
  34.0 1.4 %copy-done.4 = bf16[512,1536]{1,0:T(8,128)(2,1)S(1)} copy-done((bf16[512,1536]{1,0:T(8,128)(2,1)S(1)}, bf16[512,1536]{1,0:T(8,128)(2,1)}, u32[]{:S(2)}) %copy-start.4) | copy-done | bytes 1572888
  35.4 4.6 %shard_map.86 = (f32[512,1536]{1,0:T(8,128)}, f32[512,1536]{1,0:T(8,128)}) custom-call(bf16[512,1536]{1,0:T(8,128)(2,1)S(1)} %copy-done.3, bf16[512,1536]{1,0:T(8,128)(2,1)S(1)} %copy-done.4, s32[512,12]{1,0:T(8,128)S(1)} %copy.12.mask_ref, bf16[256,512]{1,0:T(8,128)(2,1)S(1)} %bitcast.21, bf16[256,1536]{1,0:T(8,128)(2,1)S(1)} %copy-done.2), custom_call_target="tpu_custom_call" | custom-call | flops 402653184 | bytes 9437184 | tf_op jit(solution)/shard_map/pallas_call | solution.py:133
  39.9 4.9 %all-to-all-done.1 = bf16[8,16,1536]{2,1,0:T(8,128)(2,1)} async-done(((bf16[8,16,1536]{2,1,0:T(8,128)(2,1)}), bf16[8,16,1536]{2,1,0:T(8,128)(2,1)}, u32[]{:S(2)}, u32[]{:S(2)}) %all-to-all-start.1) | async-done | bytes 393248 | tf_op jit(solution)/shard_map/all_to_all | solution.py:124
  44.9 2.6 %all_gather.3.full_ref = bf16[256,1536]{1,0:T(8,128)(2,1)S(1)} all-gather(bf16[128,1536]{1,0:T(8,128)(2,1)} %bitcast.10), channel_id=1, replica_groups=mesh['yh'=2,'z'=8,'c'=2,'x'=4,'yl'=4] {'c'}, dimensions={0}, use_global_device_ids=true | all-gather | bytes 1179648 | tf_op jit(solution)/shard_map/all_gather | solution.py:125
  47.4 1.9 %copy-done = f32[512,1536]{1,0:T(8,128)S(1)} copy-done((f32[512,1536]{1,0:T(8,128)S(1)}, f32[512,1536]{1,0:T(8,128)}, u32[]{:S(2)}) %copy-start) | copy-done | bytes 3145752
  49.3 1.9 %copy-done.1 = f32[512,1536]{1,0:T(8,128)S(1)} copy-done((f32[512,1536]{1,0:T(8,128)S(1)}, f32[512,1536]{1,0:T(8,128)}, u32[]{:S(2)}) %copy-start.1) | copy-done | bytes 3145752
  51.2 5.8 %shard_map.87 = (f32[128,1536]{1,0:T(8,128)S(1)}, f32[128,1536]{1,0:T(8,128)S(1)}, f32[128,512]{1,0:T(8,128)S(1)}, f32[128,512]{1,0:T(8,128)S(1)}) custom-call(f32[512,1536]{1,0:T(8,128)S(1)} %copy-done, f32[512,1536]{1,0:T(8,128)S(1)} %copy-done.1, bf16[512,256]{1,0:T(8,128)(2,1)S(1)} %copy.15.coef_ref, bf16[256,512]{1,0:T(8,128)(2,1)S(1)} %bitcast.20, ...), custom_call_target="tpu_custom_call" | custom-call | flops 1207959552 | bytes 6291456 | tf_op jit(solution)/shard_map/pallas_call | solution.py:144
  57.0 2.0 %collective-permute-start.5 = (f32[128,1536]{1,0:T(8,128)S(1)}, f32[128,1536]{1,0:T(8,128)S(1)}, u32[]{:S(2)}, u32[]{:S(2)}) collective-permute-start(f32[128,1536]{1,0:T(8,128)S(1)} %get-tuple-element.19), channel_id=1, source_target_pairs={{0,16},{16,0},{1,17},{17,1},{2,18},{18,2},{3,19},{19,3},{4,20},{20... | collective-permute-start | bytes 2359304 | tf_op jit(solution)/shard_map/ppermute | solution.py:17
  59.1 2.8 %collective-permute-start.1 = (f32[128,512]{1,0:T(8,128)S(1)}, f32[128,512]{1,0:T(8,128)S(1)}, u32[]{:S(2)}, u32[]{:S(2)}) collective-permute-start(f32[128,512]{1,0:T(8,128)S(1)} %get-tuple-element.17), channel_id=1, source_target_pairs={{0,4},{4,0},{8,12},{12,8},{1,5},{5,1},{9,13},{13,9},{2,6},{6,2},{1... | collective-permute-start | bytes 786440 | tf_op jit(solution)/shard_map/ppermute | solution.py:17
  62.9 3.5 %all-to-all-start.2 = ((s16[8,16,1664]{2,1,0:T(8,128)(2,1)}), s16[8,16,1664]{2,1,0:T(8,128)(2,1)S(1)}, u32[]{:S(2)}, u32[]{:S(2)}) async-start(s16[8,16,1664]{2,1,0:T(8,128)(2,1)} %shard_map.88), calls=%async_computation.2 | async-start | bytes 851968 | tf_op jit(solution)/shard_map/all_to_all | solution.py:166
  66.4 3.2 %collective-permute-done.1 = f32[128,512]{1,0:T(8,128)S(1)} collective-permute-done((f32[128,512]{1,0:T(8,128)S(1)}, f32[128,512]{1,0:T(8,128)S(1)}, u32[]{:S(2)}, u32[]{:S(2)}) %collective-permute-start.1) | collective-permute-done | bytes 262176 | tf_op jit(solution)/shard_map/ppermute | solution.py:17
  69.6 4.2 %collective-permute-start.2 = (f32[64,512]{1,0:T(8,128)S(1)}, f32[64,512]{1,0:T(8,128)S(1)}, u32[]{:S(2)}, u32[]{:S(2)}) collective-permute-start(f32[64,512]{1,0:T(8,128)S(1)} %slice.25), channel_id=1, source_target_pairs={{0,1},{1,0},{2,3},{3,2},{4,5},{5,4},{6,7},{7,6},{8,9},{9,8},{10,11... | collective-permute-start | bytes 393224 | tf_op jit(solution)/shard_map/ppermute | solution.py:17
  73.8 3.2 %collective-permute-done.2 = f32[64,512]{1,0:T(8,128)S(1)} collective-permute-done((f32[64,512]{1,0:T(8,128)S(1)}, f32[64,512]{1,0:T(8,128)S(1)}, u32[]{:S(2)}, u32[]{:S(2)}) %collective-permute-start.2) | collective-permute-done | bytes 131104 | tf_op jit(solution)/shard_map/ppermute | solution.py:17
  77.1 3.4 %collective-permute-start.3 = (f32[32,512]{1,0:T(8,128)S(1)}, f32[32,512]{1,0:T(8,128)S(1)}, u32[]{:S(2)}, u32[]{:S(2)}) collective-permute-start(f32[32,512]{1,0:T(8,128)S(1)} %slice.27), channel_id=1, source_target_pairs={{0,8},{4,12},{8,0},{12,4},{1,9},{5,13},{9,1},{13,5},{2,10},{6,14},... | collective-permute-start | bytes 196616 | tf_op jit(solution)/shard_map/ppermute | solution.py:17
  80.4 4.3 %collective-permute-done.3 = f32[32,512]{1,0:T(8,128)S(1)} collective-permute-done((f32[32,512]{1,0:T(8,128)S(1)}, f32[32,512]{1,0:T(8,128)S(1)}, u32[]{:S(2)}, u32[]{:S(2)}) %collective-permute-start.3) | collective-permute-done | bytes 65568 | tf_op jit(solution)/shard_map/ppermute | solution.py:17
  84.7 4.0 %collective-permute-start.4 = (f32[16,512]{1,0:T(8,128)S(1)}, f32[16,512]{1,0:T(8,128)S(1)}, u32[]{:S(2)}, u32[]{:S(2)}) collective-permute-start(f32[16,512]{1,0:T(8,128)S(1)} %slice.29), channel_id=1, source_target_pairs={{0,2},{1,3},{2,0},{3,1},{4,6},{5,7},{6,4},{7,5},{8,10},{9,11},{10,... | collective-permute-start | bytes 98312 | tf_op jit(solution)/shard_map/ppermute | solution.py:17
  88.9 5.2 %collective-permute-start.6 = (f32[8,1536]{1,0:T(8,128)S(1)}, f32[8,1536]{1,0:T(8,128)S(1)}, u32[]{:S(2)}, u32[]{:S(2)}) collective-permute-start(f32[8,1536]{1,0:T(8,128)S(1)} %get-tuple-element.21), channel_id=1, source_target_pairs={{0,256},{256,0},{1,257},{257,1},{2,258},{258,2},{3,259},{259,3},{4... | collective-permute-start | bytes 147464 | tf_op jit(solution)/shard_map/ppermute | solution.py:17
  94.8 4.1 %collective-permute-done.6 = f32[8,1536]{1,0:T(8,128)S(1)} collective-permute-done((f32[8,1536]{1,0:T(8,128)S(1)}, f32[8,1536]{1,0:T(8,128)S(1)}, u32[]{:S(2)}, u32[]{:S(2)}) %collective-permute-start.6) | collective-permute-done | bytes 49184 | tf_op jit(solution)/shard_map/ppermute | solution.py:17
  (27 shorter events, 5.2 us)
Async XLA Ops:
  0.6 33.3 %copy-start.2 = (bf16[256,1536]{1,0:T(8,128)(2,1)S(1)}, bf16[256,1536]{1,0:T(8,128)(2,1)}, u32[]{:S(2)}) copy-start(bf16[256,1536]{1,0:T(8,128)(2,1)} %basis_ref.3) | copy-start | bytes 2359300
  0.6 33.3 %copy-start.3 = (bf16[512,1536]{1,0:T(8,128)(2,1)S(1)}, bf16[512,1536]{1,0:T(8,128)(2,1)}, u32[]{:S(2)}) copy-start(bf16[512,1536]{1,0:T(8,128)(2,1)} %trans_ref.1) | copy-start | bytes 4718596
  2.2 19.2 %all-to-all-start = ((bf16[16,16,512]{2,1,0:T(8,128)(2,1)}), bf16[16,16,512]{2,1,0:T(8,128)(2,1)S(1)}, u32[]{:S(2)}, u32[]{:S(2)}) async-start(bf16[16,16,512]{2,1,0:T(8,128)(2,1)} %broadcast_in_dim.6), calls=%async_computation | async-start | bytes 524288 | tf_op jit(solution)/shard_map/all_to_all | solution.py:117
  11.5 10.0 %collective-permute-start = (bf16[8,1536]{1,0:T(8,128)(2,1)}, bf16[8,1536]{1,0:T(8,128)(2,1)S(1)}, u32[]{:S(2)}, u32[]{:S(2)}) collective-permute-start(bf16[8,1536]{1,0:T(8,128)(2,1)} %param.13), channel_id=1, source_target_pairs={{0,256},{256,0},{1,257},{257,1},{2,258},{258,2},{3,259},{259,3},{4... | collective-permute-start | bytes 73736 | tf_op jit(solution)/shard_map/ppermute | solution.py:17
  23.0 21.9 %all-to-all-start.1 = ((bf16[8,16,1536]{2,1,0:T(8,128)(2,1)}), bf16[8,16,1536]{2,1,0:T(8,128)(2,1)}, u32[]{:S(2)}, u32[]{:S(2)}) async-start(bf16[8,16,1536]{2,1,0:T(8,128)(2,1)} %broadcast_in_dim.15), calls=%async_computation.1 | async-start | bytes 786432 | tf_op jit(solution)/shard_map/all_to_all | solution.py:124
  34.0 1.4 %copy-start.4 = (bf16[512,1536]{1,0:T(8,128)(2,1)S(1)}, bf16[512,1536]{1,0:T(8,128)(2,1)}, u32[]{:S(2)}) copy-start(bf16[512,1536]{1,0:T(8,128)(2,1)} %ivar_ref.1) | copy-start | bytes 4718596
  47.4 1.9 %copy-start = (f32[512,1536]{1,0:T(8,128)S(1)}, f32[512,1536]{1,0:T(8,128)}, u32[]{:S(2)}) copy-start(f32[512,1536]{1,0:T(8,128)} %get-tuple-element.13.weights_ref) | copy-start | bytes 9437188
  49.3 1.9 %copy-start.1 = (f32[512,1536]{1,0:T(8,128)S(1)}, f32[512,1536]{1,0:T(8,128)}, u32[]{:S(2)}) copy-start(f32[512,1536]{1,0:T(8,128)} %get-tuple-element.14.moved_ref) | copy-start | bytes 9437188
  57.0 4.8 %collective-permute-start.5 = (f32[128,1536]{1,0:T(8,128)S(1)}, f32[128,1536]{1,0:T(8,128)S(1)}, u32[]{:S(2)}, u32[]{:S(2)}) collective-permute-start(f32[128,1536]{1,0:T(8,128)S(1)} %get-tuple-element.19), channel_id=1, source_target_pairs={{0,16},{16,0},{1,17},{17,1},{2,18},{18,2},{3,19},{19,3},{4,20},{20... | collective-permute-start | bytes 2359304 | tf_op jit(solution)/shard_map/ppermute | solution.py:17
  59.1 10.5 %collective-permute-start.1 = (f32[128,512]{1,0:T(8,128)S(1)}, f32[128,512]{1,0:T(8,128)S(1)}, u32[]{:S(2)}, u32[]{:S(2)}) collective-permute-start(f32[128,512]{1,0:T(8,128)S(1)} %get-tuple-element.17), channel_id=1, source_target_pairs={{0,4},{4,0},{8,12},{12,8},{1,5},{5,1},{9,13},{13,9},{2,6},{6,2},{1... | collective-permute-start | bytes 786440 | tf_op jit(solution)/shard_map/ppermute | solution.py:17
  62.9 25.8 %all-to-all-start.2 = ((s16[8,16,1664]{2,1,0:T(8,128)(2,1)}), s16[8,16,1664]{2,1,0:T(8,128)(2,1)S(1)}, u32[]{:S(2)}, u32[]{:S(2)}) async-start(s16[8,16,1664]{2,1,0:T(8,128)(2,1)} %shard_map.88), calls=%async_computation.2 | async-start | bytes 851968 | tf_op jit(solution)/shard_map/all_to_all | solution.py:166
  69.6 7.4 %collective-permute-start.2 = (f32[64,512]{1,0:T(8,128)S(1)}, f32[64,512]{1,0:T(8,128)S(1)}, u32[]{:S(2)}, u32[]{:S(2)}) collective-permute-start(f32[64,512]{1,0:T(8,128)S(1)} %slice.25), channel_id=1, source_target_pairs={{0,1},{1,0},{2,3},{3,2},{4,5},{5,4},{6,7},{7,6},{8,9},{9,8},{10,11... | collective-permute-start | bytes 393224 | tf_op jit(solution)/shard_map/ppermute | solution.py:17
  77.1 7.7 %collective-permute-start.3 = (f32[32,512]{1,0:T(8,128)S(1)}, f32[32,512]{1,0:T(8,128)S(1)}, u32[]{:S(2)}, u32[]{:S(2)}) collective-permute-start(f32[32,512]{1,0:T(8,128)S(1)} %slice.27), channel_id=1, source_target_pairs={{0,8},{4,12},{8,0},{12,4},{1,9},{5,13},{9,1},{13,5},{2,10},{6,14},... | collective-permute-start | bytes 196616 | tf_op jit(solution)/shard_map/ppermute | solution.py:17
  84.7 9.4 %collective-permute-start.4 = (f32[16,512]{1,0:T(8,128)S(1)}, f32[16,512]{1,0:T(8,128)S(1)}, u32[]{:S(2)}, u32[]{:S(2)}) collective-permute-start(f32[16,512]{1,0:T(8,128)S(1)} %slice.29), channel_id=1, source_target_pairs={{0,2},{1,3},{2,0},{3,1},{4,6},{5,7},{6,4},{7,5},{8,10},{9,11},{10,... | collective-permute-start | bytes 98312 | tf_op jit(solution)/shard_map/ppermute | solution.py:17
  88.9 9.9 %collective-permute-start.6 = (f32[8,1536]{1,0:T(8,128)S(1)}, f32[8,1536]{1,0:T(8,128)S(1)}, u32[]{:S(2)}, u32[]{:S(2)}) collective-permute-start(f32[8,1536]{1,0:T(8,128)S(1)} %get-tuple-element.21), channel_id=1, source_target_pairs={{0,256},{256,0},{1,257},{257,1},{2,258},{258,2},{3,259},{259,3},{4... | collective-permute-start | bytes 147464 | tf_op jit(solution)/shard_map/ppermute | solution.py:17

commit v4 on v3

v4 whole, which is shorter than its diff:
```python
import functools
import math

import jax
import jax.numpy as jnp
from jax import lax
from jax.experimental import pallas as pl
from jax.experimental.pallas import tpu as pltpu
from jax.sharding import Mesh
from jax.sharding import PartitionSpec as P

TILE = 128
BF16, F32, I16, I32 = jnp.bfloat16, jnp.float32, jnp.int16, jnp.int32
BASE, RUNG_BITS, LARGEST = 14, (64, 32, 16, 8, 4, 2, 1), 32767.0


def partner(value, axis, flip):
    return lax.ppermute(value, axis, [(i, i ^ flip) for i in range(lax.axis_size(axis))])


def in_hbm(value):
    return pltpu.with_memory_space_constraint(value, pltpu.HBM)


def block_of(ref, which, count):
    return ref[pl.ds(pl.multiple_of(which * count, count), count), :]


def fused_kernel(
    trans_ref, ivar_ref, mask_ref, tangent_ref, coef_t_ref, full_ref, basis_ref,
    own_ref, other_ref, kept_ref, given_ref,
):
    step = pl.program_id(0)
    tiles = trans_ref.shape[1] // TILE
    moved = lax.dot_general(
        tangent_ref[...], basis_ref[...], (((0,), (0,)), ((), ())), preferred_element_type=F32
    ) + lax.dot_general(
        coef_t_ref[...], full_ref[...], (((0,), (0,)), ((), ())), preferred_element_type=F32
    )
    mask = mask_ref[...].astype(F32).T
    lanes = lax.broadcasted_iota(I32, mask.shape, 1)
    parts = []
    for t in range(tiles):
        part = slice(t * TILE, (t + 1) * TILE)
        column = jnp.sum(jnp.where(lanes == step * tiles + t, mask, 0.0), axis=1, keepdims=True)
        trans = trans_ref[:, part].astype(F32)
        weights = trans * trans * ivar_ref[:, part].astype(F32) * column
        parts.append((weights * moved[:, part]).astype(BF16))
    weighted = jnp.concatenate(parts, axis=1)

    count = basis_ref.shape[0] // 16
    core, z = lax.axis_index("c"), lax.axis_index("z")
    for out, which in ((own_ref, core), (other_ref, 1 - core)):
        rows = [
            block_of(coef_t_ref, which * 8 + (z ^ (a + 2 * b + 4 * c)), count)
            for a in (0, 1)
            for b in (0, 1)
            for c in (0, 1)
        ]
        out[...] = jnp.dot(jnp.concatenate(rows, axis=0), weighted, preferred_element_type=F32)
    x, y = lax.axis_index("x"), lax.axis_index("yl")
    for out, a in ((kept_ref, 0), (given_ref, 1)):
        rows = [
            block_of(basis_ref, (x ^ (a + 2 * c)) * 4 + (y ^ (b + 2 * d)), count)
            for b in (0, 1)
            for c in (0, 1)
            for d in (0, 1)
        ]
        term = lax.dot_general(
            jnp.concatenate(rows, axis=0), weighted, (((1,), (1,)), ((), ())),
            preferred_element_type=F32,
        )

        @pl.when(step == 0)
        def _():
            out[...] = term

        @pl.when(step > 0)
        def _():
            out[...] += term


def encode(total, out_ref):
    cols = total.shape[1]
    largest = jnp.max(jnp.abs(total), axis=1, keepdims=True) * 2.0**-BASE
    scale = jnp.full_like(largest, 2.0**-BASE)
    rung = jnp.zeros_like(largest)
    for bit in RUNG_BITS:
        fits = largest * 2.0**bit <= LARGEST
        largest = jnp.where(fits, largest * 2.0**bit, largest)
        scale = jnp.where(fits, scale * 2.0**bit, scale)
        rung = jnp.where(fits, rung + bit, rung)
    out_ref[:, :cols] = jnp.round(total * scale).astype(I32).astype(I16)
    rungs = jnp.broadcast_to(rung, (total.shape[0], TILE))
    out_ref[:, cols:] = rungs.astype(I32).astype(I16)


def decode(code_ref):
    cols = code_ref.shape[1] - TILE
    rung = code_ref[:, cols:].astype(I32)
    inverse = jnp.full(rung.shape, 2.0**BASE, F32)
    for bit in RUNG_BITS:
        inverse = inverse * jnp.where((rung & bit) != 0, F32(2.0**-bit), F32(1.0))
    return jnp.concatenate(
        [
            code_ref[:, t * TILE : (t + 1) * TILE].astype(I32).astype(F32) * inverse
            for t in range(cols // TILE)
        ],
        axis=1,
    )


def halve_kernel(coded, by_y, mine_ref, came_ref, keep_ref, give_ref):
    total = mine_ref[...] + (decode(came_ref) if coded else came_ref[...])
    n = keep_ref.shape[0]
    keep, give = total[:n], total[n:]
    if by_y:
        first = lax.axis_index("yh") == 0
        keep, give = jnp.where(first, keep, give), jnp.where(first, give, keep)
    keep_ref[...] = keep
    encode(give, give_ref)


def last_kernel(divisor, mine_ref, came_ref, out_ref):
    out_ref[...] = (mine_ref[...] + decode(came_ref)) * (1.0 / divisor)


def body(transmission, inverse_var, pixel_mask, coef, basis, coef_tangent, basis_tangent):
    rows, cols = transmission.shape
    rank = basis.shape[0]
    half, mine, ours = rank // 2, rank // 32, rank // 16
    exposures, pixels = rows * 32, cols * 16

    across = partner(basis_tangent, "yh", 1)
    tangent = jnp.broadcast_to(coef_tangent.T[None], (16, ours, rows))
    tangent = lax.all_to_all(tangent, ("x", "yl"), 0, 0, tiled=True).reshape(rank, rows)
    coef_t = coef.T.reshape(2, 8, 2, mine, rows).transpose(2, 1, 0, 3, 4).reshape(rank, rows)
    across, tangent, coef_t = lax.optimization_barrier((across, tangent, coef_t))

    first = lax.axis_index("yh") == 0
    pair = jnp.stack(
        [jnp.where(first, basis_tangent, across), jnp.where(first, across, basis_tangent)]
    ).reshape(1, 2 * mine, cols)
    arrived = lax.all_to_all(jnp.broadcast_to(pair, (8, 2 * mine, cols)), "z", 0, 0, tiled=True)
    full = lax.all_gather(arrived.reshape(half, cols), "c", axis=0, tiled=True)

    width = cols // 2
    whole = lambda *shape: pl.BlockSpec(shape, lambda i: (0,) * len(shape))
    tall = lambda n: pl.BlockSpec((n, width), lambda i: (0, i))
    own, other, kept, given = pl.pallas_call(
        fused_kernel,
        grid=(cols // width,),
        in_specs=[
            tall(rows), tall(rows), whole(cols // TILE, rows), whole(rank, rows),
            whole(rank, rows), tall(rank), tall(rank),
        ],
        out_specs=[tall(half), tall(half), whole(half, rows), whole(half, rows)],
        out_shape=[jax.ShapeDtypeStruct((half, cols), F32)] * 2
        + [jax.ShapeDtypeStruct((half, rows), F32)] * 2,
        compiler_params=pltpu.CompilerParams(vmem_limit_bytes=32 << 20),
        cost_estimate=pl.CostEstimate(
            flops=8 * rows * cols * rank, bytes_accessed=6 * rows * cols, transcendentals=0
        ),
    )(*map(in_hbm, (transmission, inverse_var)), pixel_mask.T, tangent, coef_t, full, basis)

    small = pltpu.CompilerParams(vmem_limit_bytes=8 << 20)
    came = partner(other, "c", 1)
    for coded, (axis, flip) in enumerate((("z", 1), ("z", 2), ("z", 4), ("yh", 1))):
        n = own.shape[0] // 2
        own, give = pl.pallas_call(
            functools.partial(halve_kernel, coded > 0, axis == "yh"),
            out_shape=[
                jax.ShapeDtypeStruct((n, cols), F32),
                jax.ShapeDtypeStruct((n, cols + TILE), I16),
            ],
            compiler_params=small,
        )(own, came)
        came = partner(give, axis, flip)
    basis_grad = pl.pallas_call(
        functools.partial(last_kernel, math.sqrt(exposures)),
        out_shape=jax.ShapeDtypeStruct((mine, cols), F32),
        compiler_params=small,
    )(own, came)

    for axis, flip in (("x", 1), ("yl", 1), ("x", 2), ("yl", 2)):
        total = kept + partner(given, axis, flip)
        n = total.shape[0] // 2
        kept, given = total[:n], total[n:]
    coef_grad = total.T / math.sqrt(pixels)
    return (coef_grad, basis_grad)


def solution(mesh):
    fine = Mesh(mesh.devices.reshape(2, 8, 2, 4, 4), ("yh", "z", "c", "x", "yl"))
    exp, pix = ("yh", "z", "c"), ("x", "yl")
    placed = (
        P(exp, pix),
        P(exp, pix),
        P(exp, pix),
        P(exp, None),
        P(None, pix),
        P(exp, pix),
        P(exp, pix),
    )
    return jax.shard_map(
        body,
        mesh=fine,
        in_specs=placed,
        out_specs=(P(exp, pix), P(exp, pix)),
        check_vma=False,
    )
```

time: 100 us -> 97.7 us (0.977)
  blocking collectives: 2.57 us -> 23.9 us
  local copies, waits for them, and re-layouts: 9.73 us -> 2.63 us
  starting transfers between devices: 46.6 us -> 40.6 us
  Pallas kernels: 11.6 us -> 6.32 us
  waiting for transfers between devices: 26 us -> 21.9 us
  other arithmetic: 2.07 us -> 0.71 us
    all_to_all x0 -> x1, blocking collectives: none -> 21.6 us  [body(): lax.all_to_all(jnp.broadcast_to(pair, (8, 2 * mine, cols)), 'z', 0, 0, ti...]
    all_to_all x2 -> x0, starting transfers between devices: 12.2 us -> none  [the longest x1 8.78 us: body(): lax.all_to_all(jnp.broadcast_to(pair, (8, 2 * mine, cols)), 'z', 0, 0, ti...]
    ppermute x7 -> x10, starting transfers between devices: 25.1 us -> 31.3 us  [partner(): lax.ppermute(value, axis, [(i, i ^ flip) for i in range(lax.axis_size(axi...]
    unnamed x12 -> x7, local copies, waits for them, and re-layouts: 7.17 us -> 1.11 us
    pallas_call x4 -> x6, Pallas kernels: 11.6 us -> 6.32 us  [the longest x1 4.97 us: body(): pl.pallas_call(fused_kernel, grid=(cols // width,), in_specs=[tall(rows),...]
    all_to_all x2 -> x0, waiting for transfers between devices: 4.94 us -> none  [the longest x1 4.94 us: body(): lax.all_to_all(jnp.broadcast_to(pair, (8, 2 * mine, cols)), 'z', 0, 0, ti...]
    ppermute x7 -> x10, waiting for transfers between devices: 21.1 us -> 21.9 us  [partner(): lax.ppermute(value, axis, [(i, i ^ flip) for i in range(lax.axis_size(axi...]
  transfers between devices with their start and end apart: 10 -> 11, of which waited for: 6 -> 6; matrix products, arithmetic and copies ran while one was open for 3% -> 2% of each run, Pallas kernels for 6% -> 1%
where the time goes in v4:
time: 97.7 us; the launch traced here: 97 us
  starting transfers between devices  40.6 us (42%)
  blocking collectives  23.9 us (24%)
  waiting for transfers between devices  21.9 us (22%)
  Pallas kernels  6.32 us (6%)
  local copies, waits for them, and re-layouts  2.63 us (3%)
    ppermute x10, starting transfers between devices, partner(): lax.ppermute(value, axis, [(i, i ^ flip) for i in range(lax.axis_size(axi...  31.3 us
    ppermute x10, waiting for transfers between devices, partner(): lax.ppermute(value, axis, [(i, i ^ flip) for i in range(lax.axis_size(axi...  21.9 us
    all_to_all x1, blocking collectives, body(): lax.all_to_all(jnp.broadcast_to(pair, (8, 2 * mine, cols)), 'z', 0, 0, ti...  21.6 us
    all_to_all x1, starting transfers between devices, body(): lax.all_to_all(tangent, ('x', 'yl'), 0, 0, tiled=True).reshape(rank, rows)  9.25 us
    pallas_call x1, Pallas kernels, body(): pl.pallas_call(fused_kernel, grid=(cols // width,), in_specs=[tall(rows),...  4.97 us
    all_gather x1, blocking collectives, body(): full = lax.all_gather(arrived.reshape(half, cols), 'c', axis=0, tiled=True)  2.36 us
  transfers between devices with their start and end apart: 11, of which 6 were waited for; matrix products, arithmetic and copies ran while one was open for 2% of the time, Pallas kernels for 1%

profile of v4, /device:TPU:6, one launch (start us, length us, event | category | flops | bytes accessed | tf_op | source)
XLA Modules:
  0.0 97.0 jit_solution(2825913753890618686)
XLA Ops:
  0.6 1.4 %broadcast_in_dim.6 = bf16[16,16,512]{2,1,0:T(8,128)(2,1)} broadcast(bf16[16,512]{1,0:T(8,128)(2,1)} %bitcast.23), dimensions={1,2} | broadcast | bytes 278528 | tf_op jit(solution)/shard_map/broadcast_in_dim | solution.py:135
  2.1 9.2 %all-to-all-start = ((bf16[16,16,512]{2,1,0:T(8,128)(2,1)}), bf16[16,16,512]{2,1,0:T(8,128)(2,1)S(1)}, u32[]{:S(2)}, u32[]{:S(2)}) async-start(bf16[16,16,512]{2,1,0:T(8,128)(2,1)} %broadcast_in_dim.6), calls=%async_computation | async-start | bytes 524288 | tf_op jit(solution)/shard_map/all_to_all | solution.py:136
  11.3 3.6 %collective-permute-start = (bf16[8,1536]{1,0:T(8,128)(2,1)}, bf16[8,1536]{1,0:T(8,128)(2,1)S(1)}, u32[]{:S(2)}, u32[]{:S(2)}) collective-permute-start(bf16[8,1536]{1,0:T(8,128)(2,1)} %param.13), channel_id=1, source_target_pairs={{0,256},{256,0},{1,257},{257,1},{2,258},{258,2},{3,259},{259,3},{4... | collective-permute-start | bytes 73736 | tf_op jit(solution)/shard_map/ppermute | solution.py:18
  15.0 1.1 %copy.10 = bf16[512,256]{0,1:T(8,128)(2,1)S(1)} copy(bf16[512,256]{1,0:T(8,128)(2,1)} %param.10) | data formatting | bytes 524288 | tf_op args[3]
  16.1 5.2 %collective-permute-done = bf16[8,1536]{1,0:T(8,128)(2,1)S(1)} collective-permute-done((bf16[8,1536]{1,0:T(8,128)(2,1)}, bf16[8,1536]{1,0:T(8,128)(2,1)S(1)}, u32[]{:S(2)}, u32[]{:S(2)}) %collective-permute-start) | collective-permute-done | bytes 24608 | tf_op jit(solution)/shard_map/ppermute | solution.py:18
  21.4 21.6 %all_to_all.10 = bf16[8,16,1536]{2,1,0:T(8,128)(2,1)S(1)} all-to-all(bf16[8,16,1536]{2,1,0:T(8,128)(2,1)S(1)} %broadcast_in_dim.15), channel_id=1, replica_groups=mesh['yh'=2,'z'=8,'c'=2,'x'=4,'yl'=4] {'z'}, dimensions={0} | all-to-all | bytes 786432 | tf_op jit(solution)/shard_map/all_to_all | solution.py:144
  42.9 2.4 %all_gather.3.full_ref = bf16[256,1536]{1,0:T(8,128)(2,1)S(1)} all-gather(bf16[128,1536]{1,0:T(8,128)(2,1)S(1)} %bitcast.21), channel_id=1, replica_groups=mesh['yh'=2,'z'=8,'c'=2,'x'=4,'yl'=4] {'c'}, dimensions={0}, use_global_device_ids=true | all-gather | bytes 1179648 | tf_op jit(solution)/shard_map/all_gather | solution.py:145
  45.3 5.0 %shard_map.86 = (f32[128,1536]{1,0:T(8,128)S(1)}, f32[128,1536]{1,0:T(8,128)S(1)}, f32[128,512]{1,0:T(8,128)S(1)}, f32[128,512]{1,0:T(8,128)S(1)}) custom-call(bf16[512,1536]{1,0:T(8,128)(2,1)} %trans_ref.1, bf16[512,1536]{1,0:T(8,128)(2,1)} %ivar_ref.1, s32[12,512]{1,0:T(8,128)S(1)} %bitcast.20, bf16[256,512]{1,0:T(8,128)(2,1)S(1)} %bitcast.18, ...), custom_call_target="tpu_custom_call" | custom-call | flops 1610612736 | bytes 4718592 | tf_op jit(solution)/shard_map/pallas_call | solution.py:150
  50.3 2.0 %collective-permute-start.5 = (f32[128,1536]{1,0:T(8,128)S(1)}, f32[128,1536]{1,0:T(8,128)S(1)}, u32[]{:S(2)}, u32[]{:S(2)}) collective-permute-start(f32[128,1536]{1,0:T(8,128)S(1)} %get-tuple-element.23), channel_id=1, source_target_pairs={{0,16},{16,0},{1,17},{17,1},{2,18},{18,2},{3,19},{19,3},{4,20},{20... | collective-permute-start | bytes 2359304 | tf_op jit(solution)/shard_map/ppermute | solution.py:18
  52.3 2.8 %collective-permute-start.1 = (f32[128,512]{1,0:T(8,128)S(1)}, f32[128,512]{1,0:T(8,128)S(1)}, u32[]{:S(2)}, u32[]{:S(2)}) collective-permute-start(f32[128,512]{1,0:T(8,128)S(1)} %get-tuple-element.21), channel_id=1, source_target_pairs={{0,4},{4,0},{8,12},{12,8},{1,5},{5,1},{9,13},{13,9},{2,6},{6,2},{1... | collective-permute-start | bytes 786440 | tf_op jit(solution)/shard_map/ppermute | solution.py:18
  55.3 2.5 %collective-permute-start.6 = (s16[64,1664]{1,0:T(8,128)(2,1)S(1)}, s16[64,1664]{1,0:T(8,128)(2,1)S(1)}, u32[]{:S(2)}, u32[]{:S(2)}) collective-permute-start(s16[64,1664]{1,0:T(8,128)(2,1)S(1)} %get-tuple-element.25), channel_id=1, source_target_pairs={{0,32},{32,0},{64,96},{96,64},{128,160},{160,128},{192,224},{224,1... | collective-permute-start | bytes 638984 | tf_op jit(solution)/shard_map/ppermute | solution.py:18
  57.8 5.0 %collective-permute-done.1 = f32[128,512]{1,0:T(8,128)S(1)} collective-permute-done((f32[128,512]{1,0:T(8,128)S(1)}, f32[128,512]{1,0:T(8,128)S(1)}, u32[]{:S(2)}, u32[]{:S(2)}) %collective-permute-start.1) | collective-permute-done | bytes 262176 | tf_op jit(solution)/shard_map/ppermute | solution.py:18
  62.8 4.2 %collective-permute-start.2 = (f32[64,512]{1,0:T(8,128)S(1)}, f32[64,512]{1,0:T(8,128)S(1)}, u32[]{:S(2)}, u32[]{:S(2)}) collective-permute-start(f32[64,512]{1,0:T(8,128)S(1)} %slice.25), channel_id=1, source_target_pairs={{0,1},{1,0},{2,3},{3,2},{4,5},{5,4},{6,7},{7,6},{8,9},{9,8},{10,11... | collective-permute-start | bytes 393224 | tf_op jit(solution)/shard_map/ppermute | solution.py:18
  67.2 1.9 %collective-permute-start.7 = (s16[32,1664]{1,0:T(8,128)(2,1)S(1)}, s16[32,1664]{1,0:T(8,128)(2,1)S(1)}, u32[]{:S(2)}, u32[]{:S(2)}) collective-permute-start(s16[32,1664]{1,0:T(8,128)(2,1)S(1)} %get-tuple-element.27), channel_id=1, source_target_pairs={{0,64},{32,96},{64,0},{96,32},{128,192},{160,224},{192,128},{224,1... | collective-permute-start | bytes 319496 | tf_op jit(solution)/shard_map/ppermute | solution.py:18
  69.2 1.1 %collective-permute-done.2 = f32[64,512]{1,0:T(8,128)S(1)} collective-permute-done((f32[64,512]{1,0:T(8,128)S(1)}, f32[64,512]{1,0:T(8,128)S(1)}, u32[]{:S(2)}, u32[]{:S(2)}) %collective-permute-start.2) | collective-permute-done | bytes 131104 | tf_op jit(solution)/shard_map/ppermute | solution.py:18
  70.3 3.4 %collective-permute-start.3 = (f32[32,512]{1,0:T(8,128)S(1)}, f32[32,512]{1,0:T(8,128)S(1)}, u32[]{:S(2)}, u32[]{:S(2)}) collective-permute-start(f32[32,512]{1,0:T(8,128)S(1)} %slice.27), channel_id=1, source_target_pairs={{0,8},{4,12},{8,0},{12,4},{1,9},{5,13},{9,1},{13,5},{2,10},{6,14},... | collective-permute-start | bytes 196616 | tf_op jit(solution)/shard_map/ppermute | solution.py:18
  73.6 2.8 %collective-permute-done.7.came_ref = s16[32,1664]{1,0:T(8,128)(2,1)S(1)} collective-permute-done((s16[32,1664]{1,0:T(8,128)(2,1)S(1)}, s16[32,1664]{1,0:T(8,128)(2,1)S(1)}, u32[]{:S(2)}, u32[]{:S(2)}) %collective-permute-start.7) | collective-permute-done | bytes 106528 | tf_op jit(solution)/shard_map/ppermute | solution.py:18
  76.6 2.5 %collective-permute-start.8 = (s16[16,1664]{1,0:T(8,128)(2,1)S(1)}, s16[16,1664]{1,0:T(8,128)(2,1)S(1)}, u32[]{:S(2)}, u32[]{:S(2)}) collective-permute-start(s16[16,1664]{1,0:T(8,128)(2,1)S(1)} %get-tuple-element.29), channel_id=1, source_target_pairs={{0,128},{32,160},{64,192},{96,224},{128,0},{160,32},{192,64},{224,... | collective-permute-start | bytes 159752 | tf_op jit(solution)/shard_map/ppermute | solution.py:18
  79.1 3.6 %collective-permute-start.4 = (f32[16,512]{1,0:T(8,128)S(1)}, f32[16,512]{1,0:T(8,128)S(1)}, u32[]{:S(2)}, u32[]{:S(2)}) collective-permute-start(f32[16,512]{1,0:T(8,128)S(1)} %slice.29), channel_id=1, source_target_pairs={{0,2},{1,3},{2,0},{3,1},{4,6},{5,7},{6,4},{7,5},{8,10},{9,11},{10,... | collective-permute-start | bytes 98312 | tf_op jit(solution)/shard_map/ppermute | solution.py:18
  82.7 3.8 %collective-permute-done.8.came_ref = s16[16,1664]{1,0:T(8,128)(2,1)S(1)} collective-permute-done((s16[16,1664]{1,0:T(8,128)(2,1)S(1)}, s16[16,1664]{1,0:T(8,128)(2,1)S(1)}, u32[]{:S(2)}, u32[]{:S(2)}) %collective-permute-start.8) | collective-permute-done | bytes 53280 | tf_op jit(solution)/shard_map/ppermute | solution.py:18
  86.7 5.0 %collective-permute-start.9 = (s16[8,1664]{1,0:T(8,128)(2,1)S(1)}, s16[8,1664]{1,0:T(8,128)(2,1)S(1)}, u32[]{:S(2)}, u32[]{:S(2)}) collective-permute-start(s16[8,1664]{1,0:T(8,128)(2,1)S(1)} %get-tuple-element.31), channel_id=1, source_target_pairs={{0,256},{256,0},{1,257},{257,1},{2,258},{258,2},{3,259},{259,3},{4... | collective-permute-start | bytes 79880 | tf_op jit(solution)/shard_map/ppermute | solution.py:18
  91.7 0.6 fusion.1
  92.3 4.1 %collective-permute-done.9.came_ref = s16[8,1664]{1,0:T(8,128)(2,1)S(1)} collective-permute-done((s16[8,1664]{1,0:T(8,128)(2,1)S(1)}, s16[8,1664]{1,0:T(8,128)(2,1)S(1)}, u32[]{:S(2)}, u32[]{:S(2)}) %collective-permute-start.9) | collective-permute-done | bytes 26656 | tf_op jit(solution)/shard_map/ppermute | solution.py:18
  96.3 0.6 shard_map.91
  (25 shorter events, 0.9 us)
Async XLA Ops:
  0.6 20.7 %copy-start.2 = (bf16[8,1536]{1,0:T(8,128)(2,1)S(1)}, bf16[8,1536]{1,0:T(8,128)(2,1)}, u32[]{:S(2)}) copy-start(bf16[8,1536]{1,0:T(8,128)(2,1)} %param.13) | copy-start | bytes 73732
  2.1 19.2 %all-to-all-start = ((bf16[16,16,512]{2,1,0:T(8,128)(2,1)}), bf16[16,16,512]{2,1,0:T(8,128)(2,1)S(1)}, u32[]{:S(2)}, u32[]{:S(2)}) async-start(bf16[16,16,512]{2,1,0:T(8,128)(2,1)} %broadcast_in_dim.6), calls=%async_computation | async-start | bytes 524288 | tf_op jit(solution)/shard_map/all_to_all | solution.py:136
  11.3 10.0 %collective-permute-start = (bf16[8,1536]{1,0:T(8,128)(2,1)}, bf16[8,1536]{1,0:T(8,128)(2,1)S(1)}, u32[]{:S(2)}, u32[]{:S(2)}) collective-permute-start(bf16[8,1536]{1,0:T(8,128)(2,1)} %param.13), channel_id=1, source_target_pairs={{0,256},{256,0},{1,257},{257,1},{2,258},{258,2},{3,259},{259,3},{4... | collective-permute-start | bytes 73736 | tf_op jit(solution)/shard_map/ppermute | solution.py:18
  16.1 29.2 %copy-start = (bf16[256,1536]{1,0:T(8,128)(2,1)S(1)}, bf16[256,1536]{1,0:T(8,128)(2,1)}, u32[]{:S(2)}) copy-start(bf16[256,1536]{1,0:T(8,128)(2,1)} %basis_ref.1) | copy-start | bytes 2359300
  16.1 29.2 %copy-start.1 = (s32[512,12]{0,1:T(8,128)S(1)}, s32[512,12]{0,1:T(8,128)}, u32[]{:S(2)}) copy-start(s32[512,12]{0,1:T(8,128)} %param.9) | copy-start | bytes 73732
  50.3 4.8 %collective-permute-start.5 = (f32[128,1536]{1,0:T(8,128)S(1)}, f32[128,1536]{1,0:T(8,128)S(1)}, u32[]{:S(2)}, u32[]{:S(2)}) collective-permute-start(f32[128,1536]{1,0:T(8,128)S(1)} %get-tuple-element.23), channel_id=1, source_target_pairs={{0,16},{16,0},{1,17},{17,1},{2,18},{18,2},{3,19},{19,3},{4,20},{20... | collective-permute-start | bytes 2359304 | tf_op jit(solution)/shard_map/ppermute | solution.py:18
  52.3 10.5 %collective-permute-start.1 = (f32[128,512]{1,0:T(8,128)S(1)}, f32[128,512]{1,0:T(8,128)S(1)}, u32[]{:S(2)}, u32[]{:S(2)}) collective-permute-start(f32[128,512]{1,0:T(8,128)S(1)} %get-tuple-element.21), channel_id=1, source_target_pairs={{0,4},{4,0},{8,12},{12,8},{1,5},{5,1},{9,13},{13,9},{2,6},{6,2},{1... | collective-permute-start | bytes 786440 | tf_op jit(solution)/shard_map/ppermute | solution.py:18
  55.3 11.7 %collective-permute-start.6 = (s16[64,1664]{1,0:T(8,128)(2,1)S(1)}, s16[64,1664]{1,0:T(8,128)(2,1)S(1)}, u32[]{:S(2)}, u32[]{:S(2)}) collective-permute-start(s16[64,1664]{1,0:T(8,128)(2,1)S(1)} %get-tuple-element.25), channel_id=1, source_target_pairs={{0,32},{32,0},{64,96},{96,64},{128,160},{160,128},{192,224},{224,1... | collective-permute-start | bytes 638984 | tf_op jit(solution)/shard_map/ppermute | solution.py:18
  62.8 7.4 %collective-permute-start.2 = (f32[64,512]{1,0:T(8,128)S(1)}, f32[64,512]{1,0:T(8,128)S(1)}, u32[]{:S(2)}, u32[]{:S(2)}) collective-permute-start(f32[64,512]{1,0:T(8,128)S(1)} %slice.25), channel_id=1, source_target_pairs={{0,1},{1,0},{2,3},{3,2},{4,5},{5,4},{6,7},{7,6},{8,9},{9,8},{10,11... | collective-permute-start | bytes 393224 | tf_op jit(solution)/shard_map/ppermute | solution.py:18
  67.2 9.2 %collective-permute-start.7 = (s16[32,1664]{1,0:T(8,128)(2,1)S(1)}, s16[32,1664]{1,0:T(8,128)(2,1)S(1)}, u32[]{:S(2)}, u32[]{:S(2)}) collective-permute-start(s16[32,1664]{1,0:T(8,128)(2,1)S(1)} %get-tuple-element.27), channel_id=1, source_target_pairs={{0,64},{32,96},{64,0},{96,32},{128,192},{160,224},{192,128},{224,1... | collective-permute-start | bytes 319496 | tf_op jit(solution)/shard_map/ppermute | solution.py:18
  70.3 8.8 %collective-permute-start.3 = (f32[32,512]{1,0:T(8,128)S(1)}, f32[32,512]{1,0:T(8,128)S(1)}, u32[]{:S(2)}, u32[]{:S(2)}) collective-permute-start(f32[32,512]{1,0:T(8,128)S(1)} %slice.27), channel_id=1, source_target_pairs={{0,8},{4,12},{8,0},{12,4},{1,9},{5,13},{9,1},{13,5},{2,10},{6,14},... | collective-permute-start | bytes 196616 | tf_op jit(solution)/shard_map/ppermute | solution.py:18
  76.6 9.9 %collective-permute-start.8 = (s16[16,1664]{1,0:T(8,128)(2,1)S(1)}, s16[16,1664]{1,0:T(8,128)(2,1)S(1)}, u32[]{:S(2)}, u32[]{:S(2)}) collective-permute-start(s16[16,1664]{1,0:T(8,128)(2,1)S(1)} %get-tuple-element.29), channel_id=1, source_target_pairs={{0,128},{32,160},{64,192},{96,224},{128,0},{160,32},{192,64},{224,... | collective-permute-start | bytes 159752 | tf_op jit(solution)/shard_map/ppermute | solution.py:18
  79.1 12.5 %collective-permute-start.4 = (f32[16,512]{1,0:T(8,128)S(1)}, f32[16,512]{1,0:T(8,128)S(1)}, u32[]{:S(2)}, u32[]{:S(2)}) collective-permute-start(f32[16,512]{1,0:T(8,128)S(1)} %slice.29), channel_id=1, source_target_pairs={{0,2},{1,3},{2,0},{3,1},{4,6},{5,7},{6,4},{7,5},{8,10},{9,11},{10,... | collective-permute-start | bytes 98312 | tf_op jit(solution)/shard_map/ppermute | solution.py:18
  86.7 9.7 %collective-permute-start.9 = (s16[8,1664]{1,0:T(8,128)(2,1)S(1)}, s16[8,1664]{1,0:T(8,128)(2,1)S(1)}, u32[]{:S(2)}, u32[]{:S(2)}) collective-permute-start(s16[8,1664]{1,0:T(8,128)(2,1)S(1)} %get-tuple-element.31), channel_id=1, source_target_pairs={{0,256},{256,0},{1,257},{257,1},{2,258},{258,2},{3,259},{259,3},{4... | collective-permute-start | bytes 79880 | tf_op jit(solution)/shard_map/ppermute | solution.py:18

commit v5 on v4

--- a/solution.py
+++ b/solution.py
@@ -28,7 +28,7 @@
 
 def fused_kernel(
     trans_ref, ivar_ref, mask_ref, tangent_ref, coef_t_ref, full_ref, basis_ref,
-    own_ref, other_ref, kept_ref, given_ref,
+    own_ref, other_ref, coef_ref,
 ):
     step = pl.program_id(0)
     tiles = trans_ref.shape[1] // TILE
@@ -48,36 +48,22 @@
         parts.append((weights * moved[:, part]).astype(BF16))
     weighted = jnp.concatenate(parts, axis=1)
 
-    count = basis_ref.shape[0] // 16
-    core, z = lax.axis_index("c"), lax.axis_index("z")
+    half = own_ref.shape[0]
+    core = lax.axis_index("c")
     for out, which in ((own_ref, core), (other_ref, 1 - core)):
-        rows = [
-            block_of(coef_t_ref, which * 8 + (z ^ (a + 2 * b + 4 * c)), count)
-            for a in (0, 1)
-            for b in (0, 1)
-            for c in (0, 1)
-        ]
-        out[...] = jnp.dot(jnp.concatenate(rows, axis=0), weighted, preferred_element_type=F32)
-    x, y = lax.axis_index("x"), lax.axis_index("yl")
-    for out, a in ((kept_ref, 0), (given_ref, 1)):
-        rows = [
-            block_of(basis_ref, (x ^ (a + 2 * c)) * 4 + (y ^ (b + 2 * d)), count)
-            for b in (0, 1)
-            for c in (0, 1)
-            for d in (0, 1)
-        ]
-        term = lax.dot_general(
-            jnp.concatenate(rows, axis=0), weighted, (((1,), (1,)), ((), ())),
-            preferred_element_type=F32,
-        )
-
-        @pl.when(step == 0)
-        def _():
-            out[...] = term
-
-        @pl.when(step > 0)
-        def _():
-            out[...] += term
+        rows = block_of(coef_t_ref, which, half)
+        out[...] = jnp.dot(rows, weighted, preferred_element_type=F32)
+    term = lax.dot_general(
+        basis_ref[...], weighted, (((1,), (1,)), ((), ())), preferred_element_type=F32
+    )
+
+    @pl.when(step == 0)
+    def _():
+        coef_ref[...] = term
+
+    @pl.when(step > 0)
+    def _():
+        coef_ref[...] += term
 
 
 def encode(total, out_ref):
@@ -110,19 +96,32 @@
     )
 
 
-def halve_kernel(coded, by_y, mine_ref, came_ref, keep_ref, give_ref):
-    total = mine_ref[...] + (decode(came_ref) if coded else came_ref[...])
+def pack_kernel(*refs):
+    *terms, out_ref = refs
+    encode(sum(term[...] for term in terms), out_ref)
+
+
+def part_of(ref, i, count):
+    return ref.at[i * count : (i + 1) * count]
+
+
+def halve_kernel(in_ref, keep_ref, give_ref):
     n = keep_ref.shape[0]
-    keep, give = total[:n], total[n:]
-    if by_y:
-        first = lax.axis_index("yh") == 0
-        keep, give = jnp.where(first, keep, give), jnp.where(first, give, keep)
-    keep_ref[...] = keep
-    encode(give, give_ref)
+    total = sum(decode(part_of(in_ref, i, 2 * n)) for i in range(in_ref.shape[0] // (2 * n)))
+    first = lax.axis_index("yh") == 0
+    low, high = total[:n], total[n:]
+    keep_ref[...] = jnp.where(first, low, high)
+    encode(jnp.where(first, high, low), give_ref)
 
 
 def last_kernel(divisor, mine_ref, came_ref, out_ref):
     out_ref[...] = (mine_ref[...] + decode(came_ref)) * (1.0 / divisor)
+
+
+def coef_kernel(divisor, in_ref, out_ref):
+    n = out_ref.shape[0]
+    total = sum(decode(part_of(in_ref, i, n)) for i in range(in_ref.shape[0] // n))
+    out_ref[...] = total * (1.0 / divisor)
 
 
 def body(transmission, inverse_var, pixel_mask, coef, basis, coef_tangent, basis_tangent):
@@ -132,10 +131,11 @@
     exposures, pixels = rows * 32, cols * 16
 
     across = partner(basis_tangent, "yh", 1)
+    coef_t = coef.T.reshape(2, 8, 2, mine, rows).transpose(2, 1, 0, 3, 4).reshape(rank, rows)
     tangent = jnp.broadcast_to(coef_tangent.T[None], (16, ours, rows))
+    across, coef_t, tangent = lax.optimization_barrier((across, coef_t, tangent))
     tangent = lax.all_to_all(tangent, ("x", "yl"), 0, 0, tiled=True).reshape(rank, rows)
-    coef_t = coef.T.reshape(2, 8, 2, mine, rows).transpose(2, 1, 0, 3, 4).reshape(rank, rows)
-    across, tangent, coef_t = lax.optimization_barrier((across, tangent, coef_t))
+    across, tangent = lax.optimization_barrier((across, tangent))
 
     first = lax.axis_index("yh") == 0
     pair = jnp.stack(
@@ -147,47 +147,48 @@
     width = cols // 2
     whole = lambda *shape: pl.BlockSpec(shape, lambda i: (0,) * len(shape))
     tall = lambda n: pl.BlockSpec((n, width), lambda i: (0, i))
-    own, other, kept, given = pl.pallas_call(
+    own, other, coef_term = pl.pallas_call(
         fused_kernel,
         grid=(cols // width,),
         in_specs=[
             tall(rows), tall(rows), whole(cols // TILE, rows), whole(rank, rows),
             whole(rank, rows), tall(rank), tall(rank),
         ],
-        out_specs=[tall(half), tall(half), whole(half, rows), whole(half, rows)],
-        out_shape=[jax.ShapeDtypeStruct((half, cols), F32)] * 2
-        + [jax.ShapeDtypeStruct((half, rows), F32)] * 2,
+        out_specs=[tall(half), tall(half), whole(rank, rows)],
+        out_shape=[
+            jax.ShapeDtypeStruct((half, cols), F32),
+            jax.ShapeDtypeStruct((half, cols), F32),
+            jax.ShapeDtypeStruct((rank, rows), F32),
+        ],
         compiler_params=pltpu.CompilerParams(vmem_limit_bytes=32 << 20),
         cost_estimate=pl.CostEstimate(
             flops=8 * rows * cols * rank, bytes_accessed=6 * rows * cols, transcendentals=0
         ),
     )(*map(in_hbm, (transmission, inverse_var)), pixel_mask.T, tangent, coef_t, full, basis)
 
-    small = pltpu.CompilerParams(vmem_limit_bytes=8 << 20)
+    small = lambda kernel, *shapes: pl.pallas_call(
+        kernel,
+        out_shape=[jax.ShapeDtypeStruct(*shape) for shape in shapes],
+        compiler_params=pltpu.CompilerParams(vmem_limit_bytes=8 << 20),
+    )
+    exchange = lambda value, axis, n: lax.all_to_all(
+        value.reshape(n, -1, value.shape[1]), axis, 0, 0, tiled=True
+    ).reshape(value.shape)
+
     came = partner(other, "c", 1)
-    for coded, (axis, flip) in enumerate((("z", 1), ("z", 2), ("z", 4), ("yh", 1))):
-        n = own.shape[0] // 2
-        own, give = pl.pallas_call(
-            functools.partial(halve_kernel, coded > 0, axis == "yh"),
-            out_shape=[
-                jax.ShapeDtypeStruct((n, cols), F32),
-                jax.ShapeDtypeStruct((n, cols + TILE), I16),
-            ],
-            compiler_params=small,
-        )(own, came)
-        came = partner(give, axis, flip)
-    basis_grad = pl.pallas_call(
-        functools.partial(last_kernel, math.sqrt(exposures)),
-        out_shape=jax.ShapeDtypeStruct((mine, cols), F32),
-        compiler_params=small,
-    )(own, came)
-
-    for axis, flip in (("x", 1), ("yl", 1), ("x", 2), ("yl", 2)):
-        total = kept + partner(given, axis, flip)
-        n = total.shape[0] // 2
-        kept, given = total[:n], total[n:]
-    coef_grad = total.T / math.sqrt(pixels)
-    return (coef_grad, basis_grad)
+    [codes] = small(pack_kernel, ((rank, rows + TILE), I16))(coef_term)
+    codes = exchange(codes, ("x", "yl"), 16)
+    [coef_grad] = small(
+        functools.partial(coef_kernel, math.sqrt(pixels)), ((ours, rows), F32)
+    )(codes)
+
+    [codes] = small(pack_kernel, ((half, cols + TILE), I16))(own, came)
+    codes = exchange(codes, "z", 8)
+    keep, give = small(halve_kernel, ((mine, cols), F32), ((mine, cols + TILE), I16))(codes)
+    [basis_grad] = small(
+        functools.partial(last_kernel, math.sqrt(exposures)), ((mine, cols), F32)
+    )(keep, partner(give, "yh", 1))
+    return (coef_grad.T, basis_grad)
 
 
 def solution(mesh):

time: 97.7 us -> 101 us (1.034)
  waiting for transfers between devices: 21.9 us -> 30.6 us
  starting transfers between devices: 40.6 us -> 34.4 us
  Pallas kernels: 6.32 us -> 8.05 us
    all_to_all x0 -> x2, waiting for transfers between devices: none -> 20.5 us  [body(): lax.all_to_all(value.reshape(n, -1, value.shape[1]), axis, 0, 0, tiled=True)]
    ppermute x10 -> x3, waiting for transfers between devices: 21.9 us -> 3.11 us  [partner(): lax.ppermute(value, axis, [(i, i ^ flip) for i in range(lax.axis_size(axi...]
    ppermute x10 -> x3, starting transfers between devices: 31.3 us -> 14.8 us  [partner(): lax.ppermute(value, axis, [(i, i ^ flip) for i in range(lax.axis_size(axi...]
    all_to_all x0 -> x2, starting transfers between devices: none -> 10.2 us  [body(): lax.all_to_all(value.reshape(n, -1, value.shape[1]), axis, 0, 0, tiled=True)]
    all_to_all x1, waiting for transfers between devices: 0.01 us -> 6.94 us  [body(): lax.all_to_all(tangent, ('x', 'yl'), 0, 0, tiled=True).reshape(rank, rows)]
    pallas_call x5, Pallas kernels: 1.35 us -> 3.83 us  [the longest x1 1.07 us: body(): [codes] = small(pack_kernel, ((rank, rows + TILE), I16))(coef_term)]
  transfers between devices with their start and end apart: 11 -> 6, of which waited for: 6 -> 5; matrix products, arithmetic and copies ran while one was open for 2% -> 1% of each run, Pallas kernels for 1% -> 2%
where the time goes in v5:
time: 101 us; the launch traced here: 99.8 us
  starting transfers between devices  34.4 us (34%)
  waiting for transfers between devices  30.6 us (30%)
  blocking collectives  23.5 us (23%)
  Pallas kernels  8.05 us (8%)
  local copies, waits for them, and re-layouts  2.6 us (3%)
    all_to_all x1, blocking collectives, body(): lax.all_to_all(jnp.broadcast_to(pair, (8, 2 * mine, cols)), 'z', 0, 0, ti...  21.1 us
    all_to_all x2, waiting for transfers between devices, body(): lax.all_to_all(value.reshape(n, -1, value.shape[1]), axis, 0, 0, tiled=True)  20.5 us
    ppermute x3, starting transfers between devices, partner(): lax.ppermute(value, axis, [(i, i ^ flip) for i in range(lax.axis_size(axi...  14.8 us
    all_to_all x2, starting transfers between devices, body(): lax.all_to_all(value.reshape(n, -1, value.shape[1]), axis, 0, 0, tiled=True)  10.2 us
    all_to_all x1, starting transfers between devices, body(): lax.all_to_all(tangent, ('x', 'yl'), 0, 0, tiled=True).reshape(rank, rows)  9.38 us
    all_to_all x1, waiting for transfers between devices, body(): lax.all_to_all(tangent, ('x', 'yl'), 0, 0, tiled=True).reshape(rank, rows)  6.94 us
    pallas_call x1, Pallas kernels, body(): pl.pallas_call(fused_kernel, grid=(cols // width,), in_specs=[tall(rows),...  4.22 us
    ppermute x3, waiting for transfers between devices, partner(): lax.ppermute(value, axis, [(i, i ^ flip) for i in range(lax.axis_size(axi...  3.11 us
  transfers between devices with their start and end apart: 6, of which 5 were waited for; matrix products, arithmetic and copies ran while one was open for 1% of the time, Pallas kernels for 2%

profile of v5, /device:TPU:6, one launch (start us, length us, event | category | flops | bytes accessed | tf_op | source)
XLA Modules:
  0.0 99.8 jit_solution(369119049840055237)
XLA Ops:
  0.6 0.0 copy-start.2
  0.6 7.7 %collective-permute-start = (bf16[8,1536]{1,0:T(8,128)(2,1)}, bf16[8,1536]{1,0:T(8,128)(2,1)S(1)}, u32[]{:S(2)}, u32[]{:S(2)}) collective-permute-start(bf16[8,1536]{1,0:T(8,128)(2,1)} %param.13), channel_id=1, source_target_pairs={{0,256},{256,0},{1,257},{257,1},{2,258},{258,2},{3,259},{259,3},{4... | collective-permute-start | bytes 73736 | tf_op jit(solution)/shard_map/ppermute | solution.py:18
  8.4 1.1 %copy.10 = bf16[512,256]{0,1:T(8,128)(2,1)S(1)} copy(bf16[512,256]{1,0:T(8,128)(2,1)} %param.10) | data formatting | bytes 524288 | tf_op args[3]
  9.5 1.0 collective-permute-done
  10.5 1.4 %broadcast_in_dim.6 = bf16[16,16,512]{2,1,0:T(8,128)(2,1)} broadcast(bf16[16,512]{1,0:T(8,128)(2,1)} %bitcast.29), dimensions={1,2} | broadcast | bytes 278528 | tf_op jit(solution)/shard_map/broadcast_in_dim | solution.py:135
  11.9 9.4 %all-to-all-start = ((bf16[16,16,512]{2,1,0:T(8,128)(2,1)}), bf16[16,16,512]{2,1,0:T(8,128)(2,1)S(1)}, u32[]{:S(2)}, u32[]{:S(2)}) async-start(bf16[16,16,512]{2,1,0:T(8,128)(2,1)} %broadcast_in_dim.6), calls=%async_computation | async-start | bytes 524288 | tf_op jit(solution)/shard_map/all_to_all | solution.py:137
  21.3 6.9 %all-to-all-done = bf16[16,16,512]{2,1,0:T(8,128)(2,1)S(1)} async-done(((bf16[16,16,512]{2,1,0:T(8,128)(2,1)}), bf16[16,16,512]{2,1,0:T(8,128)(2,1)S(1)}, u32[]{:S(2)}, u32[]{:S(2)}) %all-to-all-start) | async-done | bytes 262176 | tf_op jit(solution)/shard_map/all_to_all | solution.py:137
  28.2 0.0 copy-done.2
  28.3 21.1 %all_to_all.20 = bf16[8,16,1536]{2,1,0:T(8,128)(2,1)S(1)} all-to-all(bf16[8,16,1536]{2,1,0:T(8,128)(2,1)S(1)} %broadcast_in_dim.15), channel_id=1, replica_groups=mesh['yh'=2,'z'=8,'c'=2,'x'=4,'yl'=4] {'z'}, dimensions={0} | all-to-all | bytes 786432 | tf_op jit(solution)/shard_map/all_to_all | solution.py:144
  49.4 2.4 %all_gather.3.full_ref = bf16[256,1536]{1,0:T(8,128)(2,1)S(1)} all-gather(bf16[128,1536]{1,0:T(8,128)(2,1)S(1)} %bitcast.26), channel_id=1, replica_groups=mesh['yh'=2,'z'=8,'c'=2,'x'=4,'yl'=4] {'c'}, dimensions={0}, use_global_device_ids=true | all-gather | bytes 1179648 | tf_op jit(solution)/shard_map/all_gather | solution.py:145
  51.8 4.2 %shard_map.86 = (f32[128,1536]{1,0:T(8,128)S(1)}, f32[128,1536]{1,0:T(8,128)S(1)}, f32[256,512]{1,0:T(8,128)S(1)}) custom-call(bf16[512,1536]{1,0:T(8,128)(2,1)} %trans_ref.1, bf16[512,1536]{1,0:T(8,128)(2,1)} %ivar_ref.1, s32[12,512]{1,0:T(8,128)S(1)} %bitcast.25, bf16[256,512]{1,0:T(8,128)(2,1)S(1)} %bitcast.24, bf16[256,512]{1,0:T(8,128)(2,1)S(1)} %bitcast.23, ...), custom_call_target="tpu_custom_call" | custom-call | flops 1610612736 | bytes 4718592 | tf_op jit(solution)/shard_map/pallas_call | solution.py:150
  56.0 2.0 %collective-permute-start.1 = (f32[128,1536]{1,0:T(8,128)S(1)}, f32[128,1536]{1,0:T(8,128)S(1)}, u32[]{:S(2)}, u32[]{:S(2)}) collective-permute-start(f32[128,1536]{1,0:T(8,128)S(1)} %get-tuple-element.19), channel_id=1, source_target_pairs={{0,16},{16,0},{1,17},{17,1},{2,18},{18,2},{3,19},{19,3},{4,20},{20... | collective-permute-start | bytes 2359304 | tf_op jit(solution)/shard_map/ppermute | solution.py:18
  58.1 2.1 %collective-permute-done.1.refs_1_ = f32[128,1536]{1,0:T(8,128)S(1)} collective-permute-done((f32[128,1536]{1,0:T(8,128)S(1)}, f32[128,1536]{1,0:T(8,128)S(1)}, u32[]{:S(2)}, u32[]{:S(2)}) %collective-permute-start.1) | collective-permute-done | bytes 786464 | tf_op jit(solution)/shard_map/ppermute | solution.py:18
  60.2 1.0 %shard_map.89 = s16[128,1664]{1,0:T(8,128)(2,1)} custom-call(f32[128,1536]{1,0:T(8,128)S(1)} %get-tuple-element.18.refs_0_, f32[128,1536]{1,0:T(8,128)S(1)} %collective-permute-done.1.refs_1_), custom_call_target="tpu_custom_call" | custom-call | tf_op jit(solution)/shard_map/pallas_call | solution.py:185
  61.2 3.5 %all-to-all-start.3 = ((s16[8,16,1664]{2,1,0:T(8,128)(2,1)}), s16[8,16,1664]{2,1,0:T(8,128)(2,1)S(1)}, u32[]{:S(2)}, u32[]{:S(2)}) async-start(s16[8,16,1664]{2,1,0:T(8,128)(2,1)} %bitcast.14), calls=%async_computation.3 | async-start | bytes 851968 | tf_op jit(solution)/shard_map/all_to_all | solution.py:174
  64.7 1.1 %shard_map.87 = s16[256,640]{1,0:T(8,128)(2,1)} custom-call(f32[256,512]{1,0:T(8,128)S(1)} %get-tuple-element.17.refs_0_), custom_call_target="tpu_custom_call" | custom-call | tf_op jit(solution)/shard_map/pallas_call | solution.py:179
  65.8 14.8 %all-to-all-done.3 = s16[8,16,1664]{2,1,0:T(8,128)(2,1)S(1)} async-done(((s16[8,16,1664]{2,1,0:T(8,128)(2,1)}), s16[8,16,1664]{2,1,0:T(8,128)(2,1)S(1)}, u32[]{:S(2)}, u32[]{:S(2)}) %all-to-all-start.3) | async-done | bytes 426016 | tf_op jit(solution)/shard_map/all_to_all | solution.py:174
  80.6 6.7 %all-to-all-start.2 = ((s16[16,16,640]{2,1,0:T(8,128)(2,1)}), s16[16,16,640]{2,1,0:T(8,128)(2,1)S(1)}, u32[]{:S(2)}, u32[]{:S(2)}) async-start(s16[16,16,640]{2,1,0:T(8,128)(2,1)} %bitcast.11), calls=%async_computation.2 | async-start | bytes 655360 | tf_op jit(solution)/shard_map/all_to_all | solution.py:174
  87.3 0.3 shard_map.90
  87.6 5.1 %collective-permute-start.2 = (s16[8,1664]{1,0:T(8,128)(2,1)S(1)}, s16[8,1664]{1,0:T(8,128)(2,1)S(1)}, u32[]{:S(2)}, u32[]{:S(2)}) collective-permute-start(s16[8,1664]{1,0:T(8,128)(2,1)S(1)} %get-tuple-element.21), channel_id=1, source_target_pairs={{0,256},{256,0},{1,257},{257,1},{2,258},{258,2},{3,259},{259,3},{4... | collective-permute-start | bytes 79880 | tf_op jit(solution)/shard_map/ppermute | solution.py:18
  92.7 5.7 %all-to-all-done.2 = s16[16,16,640]{2,1,0:T(8,128)(2,1)S(1)} async-done(((s16[16,16,640]{2,1,0:T(8,128)(2,1)}), s16[16,16,640]{2,1,0:T(8,128)(2,1)S(1)}, u32[]{:S(2)}, u32[]{:S(2)}) %all-to-all-start.2) | async-done | bytes 327712 | tf_op jit(solution)/shard_map/all_to_all | solution.py:174
  98.4 0.8 shard_map.88
  99.2 0.0 collective-permute-done.2.came_ref
  99.2 0.6 shard_map.91
  (8 shorter events, 0.1 us)
Async XLA Ops:
  0.6 27.6 %copy-start.2 = (bf16[8,1536]{1,0:T(8,128)(2,1)S(1)}, bf16[8,1536]{1,0:T(8,128)(2,1)}, u32[]{:S(2)}) copy-start(bf16[8,1536]{1,0:T(8,128)(2,1)} %param.13) | copy-start | bytes 73732
  0.6 9.8 %collective-permute-start = (bf16[8,1536]{1,0:T(8,128)(2,1)}, bf16[8,1536]{1,0:T(8,128)(2,1)S(1)}, u32[]{:S(2)}, u32[]{:S(2)}) collective-permute-start(bf16[8,1536]{1,0:T(8,128)(2,1)} %param.13), channel_id=1, source_target_pairs={{0,256},{256,0},{1,257},{257,1},{2,258},{258,2},{3,259},{259,3},{4... | collective-permute-start | bytes 73736 | tf_op jit(solution)/shard_map/ppermute | solution.py:18
  11.9 39.9 %copy-start = (bf16[256,1536]{1,0:T(8,128)(2,1)S(1)}, bf16[256,1536]{1,0:T(8,128)(2,1)}, u32[]{:S(2)}) copy-start(bf16[256,1536]{1,0:T(8,128)(2,1)} %basis_ref.1) | copy-start | bytes 2359300
  11.9 39.9 %copy-start.1 = (s32[512,12]{0,1:T(8,128)S(1)}, s32[512,12]{0,1:T(8,128)}, u32[]{:S(2)}) copy-start(s32[512,12]{0,1:T(8,128)} %param.9) | copy-start | bytes 73732
  11.9 16.3 %all-to-all-start = ((bf16[16,16,512]{2,1,0:T(8,128)(2,1)}), bf16[16,16,512]{2,1,0:T(8,128)(2,1)S(1)}, u32[]{:S(2)}, u32[]{:S(2)}) async-start(bf16[16,16,512]{2,1,0:T(8,128)(2,1)} %broadcast_in_dim.6), calls=%async_computation | async-start | bytes 524288 | tf_op jit(solution)/shard_map/all_to_all | solution.py:137
  56.0 4.2 %collective-permute-start.1 = (f32[128,1536]{1,0:T(8,128)S(1)}, f32[128,1536]{1,0:T(8,128)S(1)}, u32[]{:S(2)}, u32[]{:S(2)}) collective-permute-start(f32[128,1536]{1,0:T(8,128)S(1)} %get-tuple-element.19), channel_id=1, source_target_pairs={{0,16},{16,0},{1,17},{17,1},{2,18},{18,2},{3,19},{19,3},{4,20},{20... | collective-permute-start | bytes 2359304 | tf_op jit(solution)/shard_map/ppermute | solution.py:18
  61.2 19.4 %all-to-all-start.3 = ((s16[8,16,1664]{2,1,0:T(8,128)(2,1)}), s16[8,16,1664]{2,1,0:T(8,128)(2,1)S(1)}, u32[]{:S(2)}, u32[]{:S(2)}) async-start(s16[8,16,1664]{2,1,0:T(8,128)(2,1)} %bitcast.14), calls=%async_computation.3 | async-start | bytes 851968 | tf_op jit(solution)/shard_map/all_to_all | solution.py:174
  80.6 17.8 %all-to-all-start.2 = ((s16[16,16,640]{2,1,0:T(8,128)(2,1)}), s16[16,16,640]{2,1,0:T(8,128)(2,1)S(1)}, u32[]{:S(2)}, u32[]{:S(2)}) async-start(s16[16,16,640]{2,1,0:T(8,128)(2,1)} %bitcast.11), calls=%async_computation.2 | async-start | bytes 655360 | tf_op jit(solution)/shard_map/all_to_all | solution.py:174
  87.6 11.6 %collective-permute-start.2 = (s16[8,1664]{1,0:T(8,128)(2,1)S(1)}, s16[8,1664]{1,0:T(8,128)(2,1)S(1)}, u32[]{:S(2)}, u32[]{:S(2)}) collective-permute-start(s16[8,1664]{1,0:T(8,128)(2,1)S(1)} %get-tuple-element.21), channel_id=1, source_target_pairs={{0,256},{256,0},{1,257},{257,1},{2,258},{258,2},{3,259},{259,3},{4... | collective-permute-start | bytes 79880 | tf_op jit(solution)/shard_map/ppermute | solution.py:18

commit v6 on v5

--- a/solution.py
+++ b/solution.py
@@ -27,16 +27,28 @@
 
 
 def fused_kernel(
-    trans_ref, ivar_ref, mask_ref, tangent_ref, coef_t_ref, full_ref, basis_ref,
-    own_ref, other_ref, coef_ref,
+    trans_ref, ivar_ref, mask_ref, tangent_ref, coef_ref, full_ref, basis_ref,
+    own_ref, other_ref, term_ref, coef_p_ref, coef_t_ref,
 ):
     step = pl.program_id(0)
+
+    @pl.when(step == 0)
+    def _():
+        rank = coef_ref.shape[1]
+        take = lax.broadcasted_iota(I32, (rank, rank), 0)
+        place = lax.broadcasted_iota(I32, (rank, rank), 1)
+        low, mid, high = place & 7, place & 112, ((place >> 3) & 1) * 128 + ((place >> 7) & 1) * 8
+        chosen = (take == low + mid + high).astype(BF16)
+        coef = coef_ref[...]
+        coef_p_ref[...] = jnp.dot(coef, chosen, preferred_element_type=F32).astype(BF16)
+        coef_t_ref[...] = lax.dot_general(
+            chosen, coef, (((0,), (1,)), ((), ())), preferred_element_type=F32
+        ).astype(BF16)
+
     tiles = trans_ref.shape[1] // TILE
     moved = lax.dot_general(
         tangent_ref[...], basis_ref[...], (((0,), (0,)), ((), ())), preferred_element_type=F32
-    ) + lax.dot_general(
-        coef_t_ref[...], full_ref[...], (((0,), (0,)), ((), ())), preferred_element_type=F32
-    )
+    ) + jnp.dot(coef_p_ref[...], full_ref[...], preferred_element_type=F32)
     mask = mask_ref[...].astype(F32).T
     lanes = lax.broadcasted_iota(I32, mask.shape, 1)
     parts = []
@@ -59,11 +71,11 @@
 
     @pl.when(step == 0)
     def _():
-        coef_ref[...] = term
+        term_ref[...] = term
 
     @pl.when(step > 0)
     def _():
-        coef_ref[...] += term
+        term_ref[...] += term
 
 
 def encode(total, out_ref):
@@ -96,9 +108,28 @@
     )
 
 
-def pack_kernel(*refs):
-    *terms, out_ref = refs
-    encode(sum(term[...] for term in terms), out_ref)
+def spread_kernel(in_ref, out_ref):
+    for i in range(out_ref.shape[0]):
+        out_ref[i] = in_ref[...]
+
+
+def spread_pair_kernel(mine_ref, other_ref, out_ref):
+    mine, other = mine_ref[...].astype(F32), other_ref[...].astype(F32)
+    first = lax.axis_index("yh") == 0
+    pair = [jnp.where(first, mine, other), jnp.where(first, other, mine)]
+    pair = jnp.concatenate(pair, axis=0).astype(BF16)
+    for i in range(out_ref.shape[0]):
+        out_ref[i] = pair
+
+
+def pack_kernel(term_ref, out_ref):
+    encode(term_ref[...], out_ref)
+
+
+def add_kernel(own_ref, both_ref, out_ref):
+    n = own_ref.shape[0]
+    came = pl.ds(pl.multiple_of((1 - lax.axis_index("c")) * n, n), n)
+    encode(own_ref[...] + decode(both_ref.at[came]), out_ref)
 
 
 def part_of(ref, i, count):
@@ -130,29 +161,31 @@
     half, mine, ours = rank // 2, rank // 32, rank // 16
     exposures, pixels = rows * 32, cols * 16
 
+    small = lambda kernel, *shapes: pl.pallas_call(
+        kernel,
+        out_shape=[jax.ShapeDtypeStruct(*shape) for shape in shapes],
+        compiler_params=pltpu.CompilerParams(vmem_limit_bytes=8 << 20),
+    )
+    exchange = lambda value, axis: lax.all_to_all(value, axis, 0, 0, tiled=True)
+
     across = partner(basis_tangent, "yh", 1)
-    coef_t = coef.T.reshape(2, 8, 2, mine, rows).transpose(2, 1, 0, 3, 4).reshape(rank, rows)
-    tangent = jnp.broadcast_to(coef_tangent.T[None], (16, ours, rows))
-    across, coef_t, tangent = lax.optimization_barrier((across, coef_t, tangent))
-    tangent = lax.all_to_all(tangent, ("x", "yl"), 0, 0, tiled=True).reshape(rank, rows)
+    [tangent] = small(spread_kernel, ((16, ours, rows), BF16))(coef_tangent.T)
+    tangent = exchange(tangent, ("x", "yl")).reshape(rank, rows)
     across, tangent = lax.optimization_barrier((across, tangent))
 
-    first = lax.axis_index("yh") == 0
-    pair = jnp.stack(
-        [jnp.where(first, basis_tangent, across), jnp.where(first, across, basis_tangent)]
-    ).reshape(1, 2 * mine, cols)
-    arrived = lax.all_to_all(jnp.broadcast_to(pair, (8, 2 * mine, cols)), "z", 0, 0, tiled=True)
-    full = lax.all_gather(arrived.reshape(half, cols), "c", axis=0, tiled=True)
+    [pair] = small(spread_pair_kernel, ((8, 2 * mine, cols), BF16))(basis_tangent, across)
+    arrived = exchange(pair, "z").reshape(half, cols)
+    full = lax.all_gather(arrived, "c", axis=0, tiled=True)
 
     width = cols // 2
     whole = lambda *shape: pl.BlockSpec(shape, lambda i: (0,) * len(shape))
     tall = lambda n: pl.BlockSpec((n, width), lambda i: (0, i))
-    own, other, coef_term = pl.pallas_call(
+    own, other, term = pl.pallas_call(
         fused_kernel,
         grid=(cols // width,),
         in_specs=[
             tall(rows), tall(rows), whole(cols // TILE, rows), whole(rank, rows),
-            whole(rank, rows), tall(rank), tall(rank),
+            whole(rows, rank), tall(rank), tall(rank),
         ],
         out_specs=[tall(half), tall(half), whole(rank, rows)],
         out_shape=[
@@ -160,34 +193,28 @@
             jax.ShapeDtypeStruct((half, cols), F32),
             jax.ShapeDtypeStruct((rank, rows), F32),
         ],
+        scratch_shapes=[pltpu.VMEM((rows, rank), BF16), pltpu.VMEM((rank, rows), BF16)],
         compiler_params=pltpu.CompilerParams(vmem_limit_bytes=32 << 20),
         cost_estimate=pl.CostEstimate(
             flops=8 * rows * cols * rank, bytes_accessed=6 * rows * cols, transcendentals=0
         ),
-    )(*map(in_hbm, (transmission, inverse_var)), pixel_mask.T, tangent, coef_t, full, basis)
-
-    small = lambda kernel, *shapes: pl.pallas_call(
-        kernel,
-        out_shape=[jax.ShapeDtypeStruct(*shape) for shape in shapes],
-        compiler_params=pltpu.CompilerParams(vmem_limit_bytes=8 << 20),
-    )
-    exchange = lambda value, axis, n: lax.all_to_all(
-        value.reshape(n, -1, value.shape[1]), axis, 0, 0, tiled=True
-    ).reshape(value.shape)
-
-    came = partner(other, "c", 1)
-    [codes] = small(pack_kernel, ((rank, rows + TILE), I16))(coef_term)
-    codes = exchange(codes, ("x", "yl"), 16)
-    [coef_grad] = small(
-        functools.partial(coef_kernel, math.sqrt(pixels)), ((ours, rows), F32)
-    )(codes)
-
-    [codes] = small(pack_kernel, ((half, cols + TILE), I16))(own, came)
-    codes = exchange(codes, "z", 8)
+    )(*map(in_hbm, (transmission, inverse_var)), pixel_mask.T, tangent, coef, full, basis)
+
+    [codes] = small(pack_kernel, ((half, cols + TILE), I16))(other)
+    codes = lax.all_gather(codes, "c", axis=0, tiled=True)
+    [codes] = small(add_kernel, ((half, cols + TILE), I16))(own, codes)
+    [terms] = small(pack_kernel, ((rank, rows + TILE), I16))(term)
+    codes, terms = lax.optimization_barrier((codes, terms))
+    codes = exchange(codes.reshape(8, 2 * mine, cols + TILE), "z").reshape(half, cols + TILE)
+
     keep, give = small(halve_kernel, ((mine, cols), F32), ((mine, cols + TILE), I16))(codes)
     [basis_grad] = small(
         functools.partial(last_kernel, math.sqrt(exposures)), ((mine, cols), F32)
     )(keep, partner(give, "yh", 1))
+    terms = exchange(terms.reshape(16, ours, rows + TILE), ("x", "yl")).reshape(rank, rows + TILE)
+    [coef_grad] = small(
+        functools.partial(coef_kernel, math.sqrt(pixels)), ((ours, rows), F32)
+    )(terms)
     return (coef_grad.T, basis_grad)
 
 

time: 101 us -> 94.5 us (0.936)
  blocking collectives: 23.5 us -> 44.8 us
  waiting for transfers between devices: 30.6 us -> 12.1 us
  starting transfers between devices: 34.4 us -> 25.4 us
  local copies, waits for them, and re-layouts: 2.6 us -> 1.46 us
    all_to_all x3 -> x2, waiting for transfers between devices: 27.5 us -> 5.81 us  [body(): exchange = lambda value, axis: lax.all_to_all(value, axis, 0, 0, tiled=True)]
    all_to_all x1 -> x2, blocking collectives: 21.1 us -> 40.1 us  [body(): exchange = lambda value, axis: lax.all_to_all(value, axis, 0, 0, tiled=True)]
    ppermute x3 -> x2, starting transfers between devices: 14.8 us -> 8.59 us  [partner(): lax.ppermute(value, axis, [(i, i ^ flip) for i in range(lax.axis_size(axi...]
    ppermute x3 -> x2, waiting for transfers between devices: 3.11 us -> 6.33 us  [partner(): lax.ppermute(value, axis, [(i, i ^ flip) for i in range(lax.axis_size(axi...]
    all_to_all x3 -> x2, starting transfers between devices: 19.6 us -> 16.9 us  [body(): exchange = lambda value, axis: lax.all_to_all(value, axis, 0, 0, tiled=True)]
    all_gather x1 -> x2, blocking collectives: 2.36 us -> 4.77 us  [the longest x1 2.42 us: body(): codes = lax.all_gather(codes, 'c', axis=0, tiled=True)]
    broadcast_in_dim x2 -> x0, local copies, waits for them, and re-layouts: 1.47 us -> none  [the longest x1 1.45 us: body(): tangent = jnp.broadcast_to(coef_tangent.T[None], (16, ours, rows))]
    pallas_call x2 -> x5, Pallas kernels: 2.11 us -> 2.45 us  [the longest x1 1.07 us: body(): [terms] = small(pack_kernel, ((rank, rows + TILE), I16))(term)]
  transfers between devices with their start and end apart: 6 -> 4, of which waited for: 5 -> 2; matrix products, arithmetic and copies ran while one was open for 1% -> 0% of each run, Pallas kernels for 2% -> 1%
where the time goes in v6:
time: 94.5 us; the launch traced here: 93.2 us
  blocking collectives  44.8 us (47%)
  starting transfers between devices  25.4 us (27%)
  waiting for transfers between devices  12.1 us (13%)
  Pallas kernels  8.67 us (9%)
  local copies, waits for them, and re-layouts  1.46 us (2%)
    all_to_all x2, blocking collectives, body(): exchange = lambda value, axis: lax.all_to_all(value, axis, 0, 0, tiled=True)  40.1 us
    all_to_all x2, starting transfers between devices, body(): exchange = lambda value, axis: lax.all_to_all(value, axis, 0, 0, tiled=True)  16.9 us
    ppermute x2, starting transfers between devices, partner(): lax.ppermute(value, axis, [(i, i ^ flip) for i in range(lax.axis_size(axi...  8.59 us
    ppermute x2, waiting for transfers between devices, partner(): lax.ppermute(value, axis, [(i, i ^ flip) for i in range(lax.axis_size(axi...  6.33 us
    all_to_all x2, waiting for transfers between devices, body(): exchange = lambda value, axis: lax.all_to_all(value, axis, 0, 0, tiled=True)  5.81 us
    pallas_call x1, Pallas kernels, body(): pl.pallas_call(fused_kernel, grid=(cols // width,), in_specs=[tall(rows),...  4.5 us
    all_gather x1, blocking collectives, body(): codes = lax.all_gather(codes, 'c', axis=0, tiled=True)  2.42 us
    all_gather x1, blocking collectives, body(): full = lax.all_gather(arrived, 'c', axis=0, tiled=True)  2.36 us
  transfers between devices with their start and end apart: 4, of which 2 were waited for; matrix products, arithmetic and copies ran while one was open for 0% of the time, Pallas kernels for 1%

profile of v6, /device:TPU:6, one launch (start us, length us, event | category | flops | bytes accessed | tf_op | source)
XLA Modules:
  0.0 93.2 jit_solution(5905100414543488244)
XLA Ops:
  0.6 0.0 copy-start.1
  0.6 0.7 copy-done.1
  1.4 0.7 shard_map.86
  2.1 9.2 %all-to-all-start = ((bf16[16,16,512]{2,1,0:T(8,128)(2,1)}), bf16[16,16,512]{2,1,0:T(8,128)(2,1)S(1)}, u32[]{:S(2)}, u32[]{:S(2)}) async-start(bf16[16,16,512]{2,1,0:T(8,128)(2,1)} %shard_map.86), calls=%async_computation | async-start | bytes 524288 | tf_op jit(solution)/shard_map/all_to_all | solution.py:169
  11.3 3.6 %collective-permute-start = (bf16[8,1536]{1,0:T(8,128)(2,1)}, bf16[8,1536]{1,0:T(8,128)(2,1)S(1)}, u32[]{:S(2)}, u32[]{:S(2)}) collective-permute-start(bf16[8,1536]{1,0:T(8,128)(2,1)} %mine_ref.1), channel_id=1, source_target_pairs={{0,256},{256,0},{1,257},{257,1},{2,258},{258,2},{3,259},{259,3},{4... | collective-permute-start | bytes 73736 | tf_op jit(solution)/shard_map/ppermute | solution.py:18
  14.9 6.3 %collective-permute-done.other_ref = bf16[8,1536]{1,0:T(8,128)(2,1)S(1)} collective-permute-done((bf16[8,1536]{1,0:T(8,128)(2,1)}, bf16[8,1536]{1,0:T(8,128)(2,1)S(1)}, u32[]{:S(2)}, u32[]{:S(2)}) %collective-permute-start) | collective-permute-done | bytes 24608 | tf_op jit(solution)/shard_map/ppermute | solution.py:18
  21.3 0.0 all-to-all-done
  21.3 0.7 copy-done
  22.1 21.7 %all_to_all.20 = bf16[8,16,1536]{2,1,0:T(8,128)(2,1)S(1)} all-to-all(bf16[8,16,1536]{2,1,0:T(8,128)(2,1)S(1)} %shard_map.87), channel_id=1, replica_groups=mesh['yh'=2,'z'=8,'c'=2,'x'=4,'yl'=4] {'z'}, dimensions={0} | all-to-all | bytes 786432 | tf_op jit(solution)/shard_map/all_to_all | solution.py:169
  43.8 2.4 %all_gather.6.full_ref = bf16[256,1536]{1,0:T(8,128)(2,1)S(1)} all-gather(bf16[128,1536]{1,0:T(8,128)(2,1)S(1)} %bitcast.15), channel_id=1, replica_groups=mesh['yh'=2,'z'=8,'c'=2,'x'=4,'yl'=4] {'c'}, dimensions={0}, use_global_device_ids=true | all-gather | bytes 1179648 | tf_op jit(solution)/shard_map/all_gather | solution.py:178
  46.1 0.0 copy-done.4
  46.1 4.5 %shard_map.88 = (f32[128,1536]{1,0:T(8,128)S(1)}, f32[128,1536]{1,0:T(8,128)S(1)}, f32[256,512]{1,0:T(8,128)S(1)}) custom-call(bf16[512,1536]{1,0:T(8,128)(2,1)} %trans_ref.1, bf16[512,1536]{1,0:T(8,128)(2,1)} %ivar_ref.1, s32[12,512]{1,0:T(8,128)S(1)} %bitcast.14, bf16[256,512]{1,0:T(8,128)(2,1)S(1)} %bitcast.12, bf16[512,256]{1,0:T(8,128)(2,1)S(1)} %copy-done.3, ...), custom_call_target="tpu_custom_call" | custom-call | flops 1610612736 | bytes 4718592 | tf_op jit(solution)/shard_map/pallas_call | solution.py:183
  50.6 1.1 %shard_map.91 = s16[256,640]{1,0:T(8,128)(2,1)} custom-call(f32[256,512]{1,0:T(8,128)S(1)} %get-tuple-element.15.term_ref), custom_call_target="tpu_custom_call" | custom-call | tf_op jit(solution)/shard_map/pallas_call | solution.py:206
  51.7 0.3 shard_map.89
  52.0 2.4 %all_gather.7.both_ref = s16[256,1664]{1,0:T(8,128)(2,1)S(1)} all-gather(s16[128,1664]{1,0:T(8,128)(2,1)S(1)} %shard_map.89), channel_id=1, replica_groups=mesh['yh'=2,'z'=8,'c'=2,'x'=4,'yl'=4] {'c'}, dimensions={0}, use_global_device_ids=true | all-gather | bytes 1277952 | tf_op jit(solution)/shard_map/all_gather | solution.py:204
  54.4 0.4 shard_map.90
  54.7 18.4 %all_to_all.21 = s16[8,16,1664]{2,1,0:T(8,128)(2,1)S(1)} all-to-all(s16[8,16,1664]{2,1,0:T(8,128)(2,1)S(1)} %bitcast.10), channel_id=1, replica_groups=mesh['yh'=2,'z'=8,'c'=2,'x'=4,'yl'=4] {'z'}, dimensions={0} | all-to-all | bytes 851968 | tf_op jit(solution)/shard_map/all_to_all | solution.py:169
  73.1 7.6 %all-to-all-start.2 = ((s16[16,16,640]{2,1,0:T(8,128)(2,1)}), s16[16,16,640]{2,1,0:T(8,128)(2,1)S(1)}, u32[]{:S(2)}, u32[]{:S(2)}) async-start(s16[16,16,640]{2,1,0:T(8,128)(2,1)} %bitcast.4), calls=%async_computation.2 | async-start | bytes 655360 | tf_op jit(solution)/shard_map/all_to_all | solution.py:169
  80.7 0.3 shard_map.93
  81.0 5.0 %collective-permute-start.1 = (s16[8,1664]{1,0:T(8,128)(2,1)S(1)}, s16[8,1664]{1,0:T(8,128)(2,1)S(1)}, u32[]{:S(2)}, u32[]{:S(2)}) collective-permute-start(s16[8,1664]{1,0:T(8,128)(2,1)S(1)} %get-tuple-element.19), channel_id=1, source_target_pairs={{0,256},{256,0},{1,257},{257,1},{2,258},{258,2},{3,259},{259,3},{4... | collective-permute-start | bytes 79880 | tf_op jit(solution)/shard_map/ppermute | solution.py:18
  86.0 5.8 %all-to-all-done.2 = s16[16,16,640]{2,1,0:T(8,128)(2,1)S(1)} async-done(((s16[16,16,640]{2,1,0:T(8,128)(2,1)}), s16[16,16,640]{2,1,0:T(8,128)(2,1)S(1)}, u32[]{:S(2)}, u32[]{:S(2)}) %all-to-all-start.2) | async-done | bytes 327712 | tf_op jit(solution)/shard_map/all_to_all | solution.py:169
  91.8 0.8 shard_map.92
  92.6 0.0 collective-permute-done.1.came_ref
  92.6 0.6 shard_map.94
  (7 shorter events, 0.0 us)
Async XLA Ops:
  0.6 0.7 copy-start.1
  1.3 44.8 %copy-start.2 = (bf16[256,1536]{1,0:T(8,128)(2,1)S(1)}, bf16[256,1536]{1,0:T(8,128)(2,1)}, u32[]{:S(2)}) copy-start(bf16[256,1536]{1,0:T(8,128)(2,1)} %basis_ref.1) | copy-start | bytes 2359300
  2.1 19.2 %all-to-all-start = ((bf16[16,16,512]{2,1,0:T(8,128)(2,1)}), bf16[16,16,512]{2,1,0:T(8,128)(2,1)S(1)}, u32[]{:S(2)}, u32[]{:S(2)}) async-start(bf16[16,16,512]{2,1,0:T(8,128)(2,1)} %shard_map.86), calls=%async_computation | async-start | bytes 524288 | tf_op jit(solution)/shard_map/all_to_all | solution.py:169
  11.3 10.0 %collective-permute-start = (bf16[8,1536]{1,0:T(8,128)(2,1)}, bf16[8,1536]{1,0:T(8,128)(2,1)S(1)}, u32[]{:S(2)}, u32[]{:S(2)}) collective-permute-start(bf16[8,1536]{1,0:T(8,128)(2,1)} %mine_ref.1), channel_id=1, source_target_pairs={{0,256},{256,0},{1,257},{257,1},{2,258},{258,2},{3,259},{259,3},{4... | collective-permute-start | bytes 73736 | tf_op jit(solution)/shard_map/ppermute | solution.py:18
  21.3 0.7 copy-start
  22.0 24.1 %copy-start.3 = (bf16[512,256]{1,0:T(8,128)(2,1)S(1)}, bf16[512,256]{1,0:T(8,128)(2,1)}, u32[]{:S(2)}) copy-start(bf16[512,256]{1,0:T(8,128)(2,1)} %coef_ref.1) | copy-start | bytes 786436
  22.0 24.1 %copy-start.4 = (s32[512,12]{0,1:T(8,128)S(1)}, s32[512,12]{0,1:T(8,128)}, u32[]{:S(2)}) copy-start(s32[512,12]{0,1:T(8,128)} %param.9) | copy-start | bytes 73732
  73.1 18.7 %all-to-all-start.2 = ((s16[16,16,640]{2,1,0:T(8,128)(2,1)}), s16[16,16,640]{2,1,0:T(8,128)(2,1)S(1)}, u32[]{:S(2)}, u32[]{:S(2)}) async-start(s16[16,16,640]{2,1,0:T(8,128)(2,1)} %bitcast.4), calls=%async_computation.2 | async-start | bytes 655360 | tf_op jit(solution)/shard_map/all_to_all | solution.py:169
  81.0 11.6 %collective-permute-start.1 = (s16[8,1664]{1,0:T(8,128)(2,1)S(1)}, s16[8,1664]{1,0:T(8,128)(2,1)S(1)}, u32[]{:S(2)}, u32[]{:S(2)}) collective-permute-start(s16[8,1664]{1,0:T(8,128)(2,1)S(1)} %get-tuple-element.19), channel_id=1, source_target_pairs={{0,256},{256,0},{1,257},{257,1},{2,258},{258,2},{3,259},{259,3},{4... | collective-permute-start | bytes 79880 | tf_op jit(solution)/shard_map/ppermute | solution.py:18

commit v7 on v6

--- a/solution.py
+++ b/solution.py
@@ -28,7 +28,7 @@
 
 def fused_kernel(
     trans_ref, ivar_ref, mask_ref, tangent_ref, coef_ref, full_ref, basis_ref,
-    own_ref, other_ref, term_ref, coef_p_ref, coef_t_ref,
+    own_ref, other_codes_ref, term_codes_ref, coef_p_ref, coef_t_ref, other_ref, term_ref,
 ):
     step = pl.program_id(0)
 
@@ -60,11 +60,18 @@
         parts.append((weights * moved[:, part]).astype(BF16))
     weighted = jnp.concatenate(parts, axis=1)
 
-    half = own_ref.shape[0]
+    half, width = own_ref.shape
     core = lax.axis_index("c")
-    for out, which in ((own_ref, core), (other_ref, 1 - core)):
-        rows = block_of(coef_t_ref, which, half)
-        out[...] = jnp.dot(rows, weighted, preferred_element_type=F32)
+    own_ref[...] = jnp.dot(
+        block_of(coef_t_ref, core, half), weighted, preferred_element_type=F32
+    )
+    other = jnp.dot(block_of(coef_t_ref, 1 - core, half), weighted, preferred_element_type=F32)
+    for i in range(other_ref.shape[1] // width):
+
+        @pl.when(step == i)
+        def _():
+            other_ref[:, i * width : (i + 1) * width] = other
+
     term = lax.dot_general(
         basis_ref[...], weighted, (((1,), (1,)), ((), ())), preferred_element_type=F32
     )
@@ -76,6 +83,11 @@
     @pl.when(step > 0)
     def _():
         term_ref[...] += term
+
+    @pl.when(step == pl.num_programs(0) - 1)
+    def _():
+        encode(other_ref[...], other_codes_ref)
+        encode(term_ref[...], term_codes_ref)
 
 
 def encode(total, out_ref):
@@ -122,10 +134,6 @@
         out_ref[i] = pair
 
 
-def pack_kernel(term_ref, out_ref):
-    encode(term_ref[...], out_ref)
-
-
 def add_kernel(own_ref, both_ref, out_ref):
     n = own_ref.shape[0]
     came = pl.ds(pl.multiple_of((1 - lax.axis_index("c")) * n, n), n)
@@ -169,49 +177,55 @@
     exchange = lambda value, axis: lax.all_to_all(value, axis, 0, 0, tiled=True)
 
     across = partner(basis_tangent, "yh", 1)
-    [tangent] = small(spread_kernel, ((16, ours, rows), BF16))(coef_tangent.T)
+    [pair] = small(spread_pair_kernel, ((8, 2 * mine, cols), BF16))(in_hbm(basis_tangent), across)
+    [tangent] = small(spread_kernel, ((16, ours, rows), BF16))(in_hbm(coef_tangent.T))
+    pair, tangent = lax.optimization_barrier((pair, tangent))
+    arrived = exchange(pair, "z").reshape(half, cols)
+
+    arrived, tangent = lax.optimization_barrier((arrived, tangent))
     tangent = exchange(tangent, ("x", "yl")).reshape(rank, rows)
-    across, tangent = lax.optimization_barrier((across, tangent))
-
-    [pair] = small(spread_pair_kernel, ((8, 2 * mine, cols), BF16))(basis_tangent, across)
-    arrived = exchange(pair, "z").reshape(half, cols)
     full = lax.all_gather(arrived, "c", axis=0, tiled=True)
 
     width = cols // 2
     whole = lambda *shape: pl.BlockSpec(shape, lambda i: (0,) * len(shape))
     tall = lambda n: pl.BlockSpec((n, width), lambda i: (0, i))
-    own, other, term = pl.pallas_call(
+    own, codes, terms = pl.pallas_call(
         fused_kernel,
         grid=(cols // width,),
         in_specs=[
             tall(rows), tall(rows), whole(cols // TILE, rows), whole(rank, rows),
             whole(rows, rank), tall(rank), tall(rank),
         ],
-        out_specs=[tall(half), tall(half), whole(rank, rows)],
+        out_specs=[tall(half), whole(half, cols + TILE), whole(rank, rows + TILE)],
         out_shape=[
             jax.ShapeDtypeStruct((half, cols), F32),
-            jax.ShapeDtypeStruct((half, cols), F32),
-            jax.ShapeDtypeStruct((rank, rows), F32),
-        ],
-        scratch_shapes=[pltpu.VMEM((rows, rank), BF16), pltpu.VMEM((rank, rows), BF16)],
+            jax.ShapeDtypeStruct((half, cols + TILE), I16),
+            jax.ShapeDtypeStruct((rank, rows + TILE), I16),
+        ],
+        scratch_shapes=[
+            pltpu.VMEM((rows, rank), BF16), pltpu.VMEM((rank, rows), BF16),
+            pltpu.VMEM((half, cols), F32), pltpu.VMEM((rank, rows), F32),
+        ],
         compiler_params=pltpu.CompilerParams(vmem_limit_bytes=32 << 20),
         cost_estimate=pl.CostEstimate(
             flops=8 * rows * cols * rank, bytes_accessed=6 * rows * cols, transcendentals=0
         ),
-    )(*map(in_hbm, (transmission, inverse_var)), pixel_mask.T, tangent, coef, full, basis)
-
-    [codes] = small(pack_kernel, ((half, cols + TILE), I16))(other)
+    )(
+        in_hbm(transmission), in_hbm(inverse_var), in_hbm(pixel_mask.T), tangent,
+        in_hbm(coef), full, in_hbm(basis),
+    )
+
+    terms = exchange(terms.reshape(16, ours, rows + TILE), ("x", "yl")).reshape(rank, rows + TILE)
     codes = lax.all_gather(codes, "c", axis=0, tiled=True)
     [codes] = small(add_kernel, ((half, cols + TILE), I16))(own, codes)
-    [terms] = small(pack_kernel, ((rank, rows + TILE), I16))(term)
     codes, terms = lax.optimization_barrier((codes, terms))
+
     codes = exchange(codes.reshape(8, 2 * mine, cols + TILE), "z").reshape(half, cols + TILE)
-
+    codes, terms = lax.optimization_barrier((codes, terms))
     keep, give = small(halve_kernel, ((mine, cols), F32), ((mine, cols + TILE), I16))(codes)
     [basis_grad] = small(
         functools.partial(last_kernel, math.sqrt(exposures)), ((mine, cols), F32)
     )(keep, partner(give, "yh", 1))
-    terms = exchange(terms.reshape(16, ours, rows + TILE), ("x", "yl")).reshape(rank, rows + TILE)
     [coef_grad] = small(
         functools.partial(coef_kernel, math.sqrt(pixels)), ((ours, rows), F32)
     )(terms)

time: 94.5 us -> 98.3 us (1.040)
  Pallas kernels: 8.67 us -> 10.5 us
  blocking collectives: 44.8 us -> 46.6 us
  waiting for transfers between devices: 12.1 us -> 13.9 us
  local copies, waits for them, and re-layouts: 1.46 us -> 0 us
    ppermute x2, starting transfers between devices: 8.59 us -> 12.8 us  [partner(): lax.ppermute(value, axis, [(i, i ^ flip) for i in range(lax.axis_size(axi...]
    all_to_all x2, waiting for transfers between devices: 5.81 us -> 9.53 us  [body(): exchange = lambda value, axis: lax.all_to_all(value, axis, 0, 0, tiled=True)]
    all_to_all x2, starting transfers between devices: 16.9 us -> 13.3 us  [body(): exchange = lambda value, axis: lax.all_to_all(value, axis, 0, 0, tiled=True)]
    ppermute x2, waiting for transfers between devices: 6.33 us -> 4.39 us  [partner(): lax.ppermute(value, axis, [(i, i ^ flip) for i in range(lax.axis_size(axi...]
    all_to_all x2, blocking collectives: 40.1 us -> 41.8 us  [body(): exchange = lambda value, axis: lax.all_to_all(value, axis, 0, 0, tiled=True)]
    pallas_call x1, Pallas kernels: 4.5 us -> 6.2 us  [body(): pl.pallas_call(fused_kernel, grid=(cols // width,), in_specs=[tall(rows),...]
    unnamed x10 -> x0, local copies, waits for them, and re-layouts: 1.46 us -> none
    pallas_call x3 -> x1, Pallas kernels: 2.05 us -> 1.44 us  [body(): small(spread_kernel, ((16, ours, rows), BF16))(in_hbm(coef_tangent.T))]
  transfers between devices with their start and end apart: 4 -> 4, of which waited for: 2 -> 4; matrix products, arithmetic and copies ran while one was open for 0% -> 0% of each run, Pallas kernels for 1% -> 3%
where the time goes in v7:
time: 98.3 us; the launch traced here: 97.8 us
  blocking collectives  46.6 us (47%)
  starting transfers between devices  26.1 us (27%)
  waiting for transfers between devices  13.9 us (14%)
  Pallas kernels  10.5 us (11%)
    all_to_all x2, blocking collectives, body(): exchange = lambda value, axis: lax.all_to_all(value, axis, 0, 0, tiled=True)  41.8 us
    all_to_all x2, starting transfers between devices, body(): exchange = lambda value, axis: lax.all_to_all(value, axis, 0, 0, tiled=True)  13.3 us
    ppermute x2, starting transfers between devices, partner(): lax.ppermute(value, axis, [(i, i ^ flip) for i in range(lax.axis_size(axi...  12.8 us
    all_to_all x2, waiting for transfers between devices, body(): exchange = lambda value, axis: lax.all_to_all(value, axis, 0, 0, tiled=True)  9.53 us
    pallas_call x1, Pallas kernels, body(): pl.pallas_call(fused_kernel, grid=(cols // width,), in_specs=[tall(rows),...  6.2 us
    ppermute x2, waiting for transfers between devices, partner(): lax.ppermute(value, axis, [(i, i ^ flip) for i in range(lax.axis_size(axi...  4.39 us
    all_gather x1, blocking collectives, body(): codes = lax.all_gather(codes, 'c', axis=0, tiled=True)  2.4 us
    all_gather x1, blocking collectives, body(): full = lax.all_gather(arrived, 'c', axis=0, tiled=True)  2.36 us
  transfers between devices with their start and end apart: 4, of which 4 were waited for; matrix products, arithmetic and copies ran while one was open for 0% of the time, Pallas kernels for 3%

profile of v7, /device:TPU:6, one launch (start us, length us, event | category | flops | bytes accessed | tf_op | source)
XLA Modules:
  0.0 97.8 jit_solution(40414082325562957)
XLA Ops:
  0.6 7.7 %collective-permute-start = (bf16[8,1536]{1,0:T(8,128)(2,1)}, bf16[8,1536]{1,0:T(8,128)(2,1)S(1)}, u32[]{:S(2)}, u32[]{:S(2)}) collective-permute-start(bf16[8,1536]{1,0:T(8,128)(2,1)} %mine_ref.1), channel_id=1, source_target_pairs={{0,256},{256,0},{1,257},{257,1},{2,258},{258,2},{3,259},{259,3},{4... | collective-permute-start | bytes 73736 | tf_op jit(solution)/shard_map/ppermute | solution.py:18
  8.4 1.4 %shard_map.87 = bf16[16,16,512]{2,1,0:T(8,128)(2,1)} custom-call(bf16[16,512]{1,0:T(8,128)(2,1)} %bitcast.15), custom_call_target="tpu_custom_call" | custom-call | tf_op jit(solution)/shard_map/pallas_call | solution.py:181
  9.8 0.7 collective-permute-done.other_ref
  10.5 0.8 shard_map.86
  11.2 23.9 %all_to_all.20 = bf16[8,16,1536]{2,1,0:T(8,128)(2,1)S(1)} all-to-all(bf16[8,16,1536]{2,1,0:T(8,128)(2,1)S(1)} %shard_map.86), channel_id=1, replica_groups=mesh['yh'=2,'z'=8,'c'=2,'x'=4,'yl'=4] {'z'}, dimensions={0} | all-to-all | bytes 786432 | tf_op jit(solution)/shard_map/all_to_all | solution.py:177
  35.1 7.6 %all-to-all-start.1 = ((bf16[16,16,512]{2,1,0:T(8,128)(2,1)}), bf16[16,16,512]{2,1,0:T(8,128)(2,1)S(1)}, u32[]{:S(2)}, u32[]{:S(2)}) async-start(bf16[16,16,512]{2,1,0:T(8,128)(2,1)} %shard_map.87), calls=%async_computation.1 | async-start | bytes 524288 | tf_op jit(solution)/shard_map/all_to_all | solution.py:177
  42.7 2.4 %all_gather.6.full_ref = bf16[256,1536]{1,0:T(8,128)(2,1)S(1)} all-gather(bf16[128,1536]{1,0:T(8,128)(2,1)S(1)} %bitcast.13), channel_id=1, replica_groups=mesh['yh'=2,'z'=8,'c'=2,'x'=4,'yl'=4] {'c'}, dimensions={0}, use_global_device_ids=true | all-gather | bytes 1179648 | tf_op jit(solution)/shard_map/all_gather | solution.py:187
  45.1 4.6 %all-to-all-done.1 = bf16[16,16,512]{2,1,0:T(8,128)(2,1)S(1)} async-done(((bf16[16,16,512]{2,1,0:T(8,128)(2,1)}), bf16[16,16,512]{2,1,0:T(8,128)(2,1)S(1)}, u32[]{:S(2)}, u32[]{:S(2)}) %all-to-all-start.1) | async-done | bytes 262176 | tf_op jit(solution)/shard_map/all_to_all | solution.py:177
  49.7 6.2 %shard_map.88 = (f32[128,1536]{1,0:T(8,128)S(1)}, s16[128,1664]{1,0:T(8,128)(2,1)S(1)}, s16[256,640]{1,0:T(8,128)(2,1)}) custom-call(bf16[512,1536]{1,0:T(8,128)(2,1)} %trans_ref.1, bf16[512,1536]{1,0:T(8,128)(2,1)} %ivar_ref.1, s32[12,512]{1,0:T(8,128)} %bitcast.16, bf16[256,512]{1,0:T(8,128)(2,1)S(1)} %bitcast.12, bf16[512,256]{1,0:T(8,128)(2,1)} %coef_ref.1, ...), custom_call_target="tpu_custom_call" | custom-call | flops 1610612736 | bytes 4718592 | tf_op jit(solution)/shard_map/pallas_call | solution.py:192
  55.9 5.7 %all-to-all-start.2 = ((s16[16,16,640]{2,1,0:T(8,128)(2,1)}), s16[16,16,640]{2,1,0:T(8,128)(2,1)S(1)}, u32[]{:S(2)}, u32[]{:S(2)}) async-start(s16[16,16,640]{2,1,0:T(8,128)(2,1)} %bitcast.4), calls=%async_computation.2 | async-start | bytes 655360 | tf_op jit(solution)/shard_map/all_to_all | solution.py:177
  61.6 2.4 %all_gather.7.both_ref = s16[256,1664]{1,0:T(8,128)(2,1)S(1)} all-gather(s16[128,1664]{1,0:T(8,128)(2,1)S(1)} %get-tuple-element.20), channel_id=1, replica_groups=mesh['yh'=2,'z'=8,'c'=2,'x'=4,'yl'=4] {'c'}, dimensions={0}, use_global_device_ids=true | all-gather | bytes 1277952 | tf_op jit(solution)/shard_map/all_gather | solution.py:219
  64.0 0.4 shard_map.89
  64.3 4.9 %all-to-all-done.2 = s16[16,16,640]{2,1,0:T(8,128)(2,1)S(1)} async-done(((s16[16,16,640]{2,1,0:T(8,128)(2,1)}), s16[16,16,640]{2,1,0:T(8,128)(2,1)S(1)}, u32[]{:S(2)}, u32[]{:S(2)}) %all-to-all-start.2) | async-done | bytes 327712 | tf_op jit(solution)/shard_map/all_to_all | solution.py:177
  69.2 18.0 %all_to_all.21 = s16[8,16,1664]{2,1,0:T(8,128)(2,1)S(1)} all-to-all(s16[8,16,1664]{2,1,0:T(8,128)(2,1)S(1)} %bitcast.9), channel_id=1, replica_groups=mesh['yh'=2,'z'=8,'c'=2,'x'=4,'yl'=4] {'z'}, dimensions={0} | all-to-all | bytes 851968 | tf_op jit(solution)/shard_map/all_to_all | solution.py:177
  87.2 0.3 shard_map.91
  87.5 5.1 %collective-permute-start.1 = (s16[8,1664]{1,0:T(8,128)(2,1)S(1)}, s16[8,1664]{1,0:T(8,128)(2,1)S(1)}, u32[]{:S(2)}, u32[]{:S(2)}) collective-permute-start(s16[8,1664]{1,0:T(8,128)(2,1)S(1)} %get-tuple-element.27), channel_id=1, source_target_pairs={{0,256},{256,0},{1,257},{257,1},{2,258},{258,2},{3,259},{259,3},{4... | collective-permute-start | bytes 79880 | tf_op jit(solution)/shard_map/ppermute | solution.py:18
  92.6 0.8 shard_map.90
  93.4 3.7 %collective-permute-done.1.came_ref = s16[8,1664]{1,0:T(8,128)(2,1)S(1)} collective-permute-done((s16[8,1664]{1,0:T(8,128)(2,1)S(1)}, s16[8,1664]{1,0:T(8,128)(2,1)S(1)}, u32[]{:S(2)}, u32[]{:S(2)}) %collective-permute-start.1) | collective-permute-done | bytes 26656 | tf_op jit(solution)/shard_map/ppermute | solution.py:18
  97.1 0.6 shard_map.92
Async XLA Ops:
  0.6 9.8 %collective-permute-start = (bf16[8,1536]{1,0:T(8,128)(2,1)}, bf16[8,1536]{1,0:T(8,128)(2,1)S(1)}, u32[]{:S(2)}, u32[]{:S(2)}) collective-permute-start(bf16[8,1536]{1,0:T(8,128)(2,1)} %mine_ref.1), channel_id=1, source_target_pairs={{0,256},{256,0},{1,257},{257,1},{2,258},{258,2},{3,259},{259,3},{4... | collective-permute-start | bytes 73736 | tf_op jit(solution)/shard_map/ppermute | solution.py:18
  35.1 14.6 %all-to-all-start.1 = ((bf16[16,16,512]{2,1,0:T(8,128)(2,1)}), bf16[16,16,512]{2,1,0:T(8,128)(2,1)S(1)}, u32[]{:S(2)}, u32[]{:S(2)}) async-start(bf16[16,16,512]{2,1,0:T(8,128)(2,1)} %shard_map.87), calls=%async_computation.1 | async-start | bytes 524288 | tf_op jit(solution)/shard_map/all_to_all | solution.py:177
  55.9 13.3 %all-to-all-start.2 = ((s16[16,16,640]{2,1,0:T(8,128)(2,1)}), s16[16,16,640]{2,1,0:T(8,128)(2,1)S(1)}, u32[]{:S(2)}, u32[]{:S(2)}) async-start(s16[16,16,640]{2,1,0:T(8,128)(2,1)} %bitcast.4), calls=%async_computation.2 | async-start | bytes 655360 | tf_op jit(solution)/shard_map/all_to_all | solution.py:177
  87.5 9.7 %collective-permute-start.1 = (s16[8,1664]{1,0:T(8,128)(2,1)S(1)}, s16[8,1664]{1,0:T(8,128)(2,1)S(1)}, u32[]{:S(2)}, u32[]{:S(2)}) collective-permute-start(s16[8,1664]{1,0:T(8,128)(2,1)S(1)} %get-tuple-element.27), channel_id=1, source_target_pairs={{0,256},{256,0},{1,257},{257,1},{2,258},{258,2},{3,259},{259,3},{4... | collective-permute-start | bytes 79880 | tf_op jit(solution)/shard_map/ppermute | solution.py:18

commit v8 on v6

--- a/solution.py
+++ b/solution.py
@@ -11,6 +11,7 @@
 
 TILE = 128
 BF16, F32, I16, I32 = jnp.bfloat16, jnp.float32, jnp.int16, jnp.int32
+HALVINGS = (("yl", 1), ("x", 1), ("yl", 2), ("x", 2))
 BASE, RUNG_BITS, LARGEST = 14, (64, 32, 16, 8, 4, 2, 1), 32767.0
 
 
@@ -28,7 +29,7 @@
 
 def fused_kernel(
     trans_ref, ivar_ref, mask_ref, tangent_ref, coef_ref, full_ref, basis_ref,
-    own_ref, other_ref, term_ref, coef_p_ref, coef_t_ref,
+    own_ref, other_ref, kept_ref, given_ref, coef_p_ref, coef_t_ref,
 ):
     step = pl.program_id(0)
 
@@ -46,8 +47,20 @@
         ).astype(BF16)
 
     tiles = trans_ref.shape[1] // TILE
+    x, y = lax.axis_index("x"), lax.axis_index("yl")
+    count = basis_ref.shape[0] // 16
+    basis = jnp.concatenate(
+        [
+            block_of(basis_ref, (x ^ (b + 2 * d)) * 4 + (y ^ (a + 2 * c)), count)
+            for a in (0, 1)
+            for b in (0, 1)
+            for c in (0, 1)
+            for d in (0, 1)
+        ],
+        axis=0,
+    )
     moved = lax.dot_general(
-        tangent_ref[...], basis_ref[...], (((0,), (0,)), ((), ())), preferred_element_type=F32
+        tangent_ref[...], basis, (((0,), (0,)), ((), ())), preferred_element_type=F32
     ) + jnp.dot(coef_p_ref[...], full_ref[...], preferred_element_type=F32)
     mask = mask_ref[...].astype(F32).T
     lanes = lax.broadcasted_iota(I32, mask.shape, 1)
@@ -66,16 +79,19 @@
         rows = block_of(coef_t_ref, which, half)
         out[...] = jnp.dot(rows, weighted, preferred_element_type=F32)
     term = lax.dot_general(
-        basis_ref[...], weighted, (((1,), (1,)), ((), ())), preferred_element_type=F32
-    )
+        basis, weighted, (((1,), (1,)), ((), ())), preferred_element_type=F32
+    )
+    n = kept_ref.shape[0]
 
     @pl.when(step == 0)
     def _():
-        term_ref[...] = term
+        kept_ref[...] = term[:n]
+        given_ref[...] = term[n:]
 
     @pl.when(step > 0)
     def _():
-        term_ref[...] += term
+        kept_ref[...] += term[:n]
+        given_ref[...] += term[n:]
 
 
 def encode(total, out_ref):
@@ -108,9 +124,10 @@
     )
 
 
-def spread_kernel(in_ref, out_ref):
-    for i in range(out_ref.shape[0]):
-        out_ref[i] = in_ref[...]
+def join_kernel(mine_ref, came_ref, out_ref):
+    n = mine_ref.shape[0]
+    out_ref[:n] = mine_ref[...]
+    out_ref[n:] = came_ref[...]
 
 
 def spread_pair_kernel(mine_ref, other_ref, out_ref):
@@ -149,12 +166,6 @@
     out_ref[...] = (mine_ref[...] + decode(came_ref)) * (1.0 / divisor)
 
 
-def coef_kernel(divisor, in_ref, out_ref):
-    n = out_ref.shape[0]
-    total = sum(decode(part_of(in_ref, i, n)) for i in range(in_ref.shape[0] // n))
-    out_ref[...] = total * (1.0 / divisor)
-
-
 def body(transmission, inverse_var, pixel_mask, coef, basis, coef_tangent, basis_tangent):
     rows, cols = transmission.shape
     rank = basis.shape[0]
@@ -168,30 +179,38 @@
     )
     exchange = lambda value, axis: lax.all_to_all(value, axis, 0, 0, tiled=True)
 
+    def joined(tangent, stage):
+        came = partner(tangent, *stage)
+        [tangent] = small(join_kernel, ((2 * tangent.shape[0], rows), BF16))(tangent, came)
+        return tangent
+
     across = partner(basis_tangent, "yh", 1)
-    [tangent] = small(spread_kernel, ((16, ours, rows), BF16))(coef_tangent.T)
-    tangent = exchange(tangent, ("x", "yl")).reshape(rank, rows)
-    across, tangent = lax.optimization_barrier((across, tangent))
-
-    [pair] = small(spread_pair_kernel, ((8, 2 * mine, cols), BF16))(basis_tangent, across)
+    *doublings, first = HALVINGS
+    tangent = joined(coef_tangent.T, first)
+    [pair] = small(spread_pair_kernel, ((8, 2 * mine, cols), BF16))(in_hbm(basis_tangent), across)
+    pair, tangent = lax.optimization_barrier((pair, tangent))
+
     arrived = exchange(pair, "z").reshape(half, cols)
     full = lax.all_gather(arrived, "c", axis=0, tiled=True)
+    for stage in reversed(doublings):
+        tangent = joined(tangent, stage)
 
     width = cols // 2
     whole = lambda *shape: pl.BlockSpec(shape, lambda i: (0,) * len(shape))
     tall = lambda n: pl.BlockSpec((n, width), lambda i: (0, i))
-    own, other, term = pl.pallas_call(
+    own, other, kept, given = pl.pallas_call(
         fused_kernel,
         grid=(cols // width,),
         in_specs=[
             tall(rows), tall(rows), whole(cols // TILE, rows), whole(rank, rows),
             whole(rows, rank), tall(rank), tall(rank),
         ],
-        out_specs=[tall(half), tall(half), whole(rank, rows)],
+        out_specs=[tall(half), tall(half), whole(half, rows), whole(half, rows)],
         out_shape=[
             jax.ShapeDtypeStruct((half, cols), F32),
             jax.ShapeDtypeStruct((half, cols), F32),
-            jax.ShapeDtypeStruct((rank, rows), F32),
+            jax.ShapeDtypeStruct((half, rows), F32),
+            jax.ShapeDtypeStruct((half, rows), F32),
         ],
         scratch_shapes=[pltpu.VMEM((rows, rank), BF16), pltpu.VMEM((rank, rows), BF16)],
         compiler_params=pltpu.CompilerParams(vmem_limit_bytes=32 << 20),
@@ -203,18 +222,19 @@
     [codes] = small(pack_kernel, ((half, cols + TILE), I16))(other)
     codes = lax.all_gather(codes, "c", axis=0, tiled=True)
     [codes] = small(add_kernel, ((half, cols + TILE), I16))(own, codes)
-    [terms] = small(pack_kernel, ((rank, rows + TILE), I16))(term)
-    codes, terms = lax.optimization_barrier((codes, terms))
     codes = exchange(codes.reshape(8, 2 * mine, cols + TILE), "z").reshape(half, cols + TILE)
-
     keep, give = small(halve_kernel, ((mine, cols), F32), ((mine, cols + TILE), I16))(codes)
+
+    for axis, flip in HALVINGS:
+        if (axis, flip) == HALVINGS[-1]:
+            given, give = lax.optimization_barrier((given, give))
+        total = kept + partner(given, axis, flip)
+        n = total.shape[0] // 2
+        kept, given = total[:n], total[n:]
+    coef_grad = total * (1.0 / math.sqrt(pixels))
     [basis_grad] = small(
         functools.partial(last_kernel, math.sqrt(exposures)), ((mine, cols), F32)
     )(keep, partner(give, "yh", 1))
-    terms = exchange(terms.reshape(16, ours, rows + TILE), ("x", "yl")).reshape(rank, rows + TILE)
-    [coef_grad] = small(
-        functools.partial(coef_kernel, math.sqrt(pixels)), ((ours, rows), F32)
-    )(terms)
     return (coef_grad.T, basis_grad)
 
 

time: 94.5 us -> 101 us (1.069)
  the two profiles are of different devices: /device:TPU:6 before, /device:TPU:8 now
where the time goes in v8:
time: 101 us
  starting transfers between devices  55 us (54%)
  waiting for transfers between devices  30.3 us (30%)
  Pallas kernels  8.45 us (8%)
  blocking collectives  4.78 us (5%)
    ppermute x10, starting transfers between devices, partner(): lax.ppermute(value, axis, [(i, i ^ flip) for i in range(lax.axis_size(axi...  37.5 us
    ppermute x10, waiting for transfers between devices, partner(): lax.ppermute(value, axis, [(i, i ^ flip) for i in range(lax.axis_size(axi...  28.9 us
    all_to_all x2, starting transfers between devices, body(): exchange = lambda value, axis: lax.all_to_all(value, axis, 0, 0, tiled=True)  17.5 us
    pallas_call x1, Pallas kernels, body(): pl.pallas_call(fused_kernel, grid=(cols // width,), in_specs=[tall(rows),...  4.53 us
    all_gather x1, blocking collectives, body(): codes = lax.all_gather(codes, 'c', axis=0, tiled=True)  2.42 us
    all_gather x1, blocking collectives, body(): full = lax.all_gather(arrived, 'c', axis=0, tiled=True)  2.37 us
  transfers between devices with their start and end apart: 12, of which 8 were waited for; matrix products, arithmetic and copies ran while one was open for 0% of the time, Pallas kernels for 2%

profile of v8, /device:TPU:8, one launch (start us, length us, event | category | flops | bytes accessed | tf_op | source)
XLA Modules:
  0.0 100.8 jit_solution(12941301403023578658)
XLA Ops:
  0.6 6.8 %collective-permute-start = (bf16[8,1536]{1,0:T(8,128)(2,1)}, bf16[8,1536]{1,0:T(8,128)(2,1)S(1)}, u32[]{:S(2)}, u32[]{:S(2)}) collective-permute-start(bf16[8,1536]{1,0:T(8,128)(2,1)} %mine_ref.1), channel_id=1, source_target_pairs={{0,256},{256,0},{1,257},{257,1},{2,258},{258,2},{3,259},{259,3},{4... | collective-permute-start | bytes 73736 | tf_op jit(solution)/shard_map/ppermute | solution.py:19
  7.5 4.9 %collective-permute-start.1 = (bf16[16,512]{1,0:T(8,128)(2,1)}, bf16[16,512]{1,0:T(8,128)(2,1)S(1)}, u32[]{:S(2)}, u32[]{:S(2)}) collective-permute-start(bf16[16,512]{1,0:T(8,128)(2,1)} %bitcast.8), channel_id=1, source_target_pairs={{0,8},{4,12},{8,0},{12,4},{1,9},{5,13},{9,1},{13,5},{2,10},{6,14},... | collective-permute-start | bytes 49160 | tf_op jit(solution)/shard_map/ppermute | solution.py:19
  12.4 2.4 %collective-permute-done.1.came_ref = bf16[16,512]{1,0:T(8,128)(2,1)S(1)} collective-permute-done((bf16[16,512]{1,0:T(8,128)(2,1)}, bf16[16,512]{1,0:T(8,128)(2,1)S(1)}, u32[]{:S(2)}, u32[]{:S(2)}) %collective-permute-start.1) | collective-permute-done | bytes 16416 | tf_op jit(solution)/shard_map/ppermute | solution.py:19
  15.6 1.6 %shard_map.86 = bf16[8,16,1536]{2,1,0:T(8,128)(2,1)} custom-call(bf16[8,1536]{1,0:T(8,128)(2,1)} %mine_ref.1, bf16[8,1536]{1,0:T(8,128)(2,1)S(1)} %collective-permute-done.other_ref), custom_call_target="tpu_custom_call" | custom-call | tf_op jit(solution)/shard_map/pallas_call | solution.py:190
  17.2 10.3 %all-to-all-start = ((bf16[8,16,1536]{2,1,0:T(8,128)(2,1)}), bf16[8,16,1536]{2,1,0:T(8,128)(2,1)S(1)}, u32[]{:S(2)}, u32[]{:S(2)}) async-start(bf16[8,16,1536]{2,1,0:T(8,128)(2,1)} %shard_map.86), calls=%async_computation | async-start | bytes 786432 | tf_op jit(solution)/shard_map/all_to_all | solution.py:180
  27.5 2.7 %collective-permute-start.2 = (bf16[32,512]{1,0:T(8,128)(2,1)S(1)}, bf16[32,512]{1,0:T(8,128)(2,1)S(1)}, u32[]{:S(2)}, u32[]{:S(2)}) collective-permute-start(bf16[32,512]{1,0:T(8,128)(2,1)S(1)} %shard_map.87.mine_ref), channel_id=1, source_target_pairs={{0,2},{1,3},{2,0},{3,1},{4,6},{5,7},{6,4},{7,5},{8,10},{9,11},{10,... | collective-permute-start | bytes 98312 | tf_op jit(solution)/shard_map/ppermute | solution.py:19
  30.2 4.1 %collective-permute-done.2.came_ref = bf16[32,512]{1,0:T(8,128)(2,1)S(1)} collective-permute-done((bf16[32,512]{1,0:T(8,128)(2,1)S(1)}, bf16[32,512]{1,0:T(8,128)(2,1)S(1)}, u32[]{:S(2)}, u32[]{:S(2)}) %collective-permute-start.2) | collective-permute-done | bytes 32800 | tf_op jit(solution)/shard_map/ppermute | solution.py:19
  34.3 3.4 %collective-permute-start.3 = (bf16[64,512]{1,0:T(8,128)(2,1)S(1)}, bf16[64,512]{1,0:T(8,128)(2,1)S(1)}, u32[]{:S(2)}, u32[]{:S(2)}) collective-permute-start(bf16[64,512]{1,0:T(8,128)(2,1)S(1)} %shard_map.88.mine_ref), channel_id=1, source_target_pairs={{0,4},{4,0},{8,12},{12,8},{1,5},{5,1},{9,13},{13,9},{2,6},{6,2},{1... | collective-permute-start | bytes 196616 | tf_op jit(solution)/shard_map/ppermute | solution.py:19
  37.7 2.8 %collective-permute-done.3.came_ref = bf16[64,512]{1,0:T(8,128)(2,1)S(1)} collective-permute-done((bf16[64,512]{1,0:T(8,128)(2,1)S(1)}, bf16[64,512]{1,0:T(8,128)(2,1)S(1)}, u32[]{:S(2)}, u32[]{:S(2)}) %collective-permute-start.3) | collective-permute-done | bytes 65568 | tf_op jit(solution)/shard_map/ppermute | solution.py:19
  40.4 3.5 %collective-permute-start.4 = (bf16[128,512]{1,0:T(8,128)(2,1)S(1)}, bf16[128,512]{1,0:T(8,128)(2,1)S(1)}, u32[]{:S(2)}, u32[]{:S(2)}) collective-permute-start(bf16[128,512]{1,0:T(8,128)(2,1)S(1)} %shard_map.89.mine_ref), channel_id=1, source_target_pairs={{0,1},{1,0},{2,3},{3,2},{4,5},{5,4},{6,7},{7,6},{8,9},{9,8},{10,11... | collective-permute-start | bytes 393224 | tf_op jit(solution)/shard_map/ppermute | solution.py:19
  44.0 3.3 %collective-permute-done.4.came_ref = bf16[128,512]{1,0:T(8,128)(2,1)S(1)} collective-permute-done((bf16[128,512]{1,0:T(8,128)(2,1)S(1)}, bf16[128,512]{1,0:T(8,128)(2,1)S(1)}, u32[]{:S(2)}, u32[]{:S(2)}) %collective-permute-start.4) | collective-permute-done | bytes 131104 | tf_op jit(solution)/shard_map/ppermute | solution.py:19
  47.3 2.4 %all_gather.6.full_ref = bf16[256,1536]{1,0:T(8,128)(2,1)S(1)} all-gather(bf16[128,1536]{1,0:T(8,128)(2,1)S(1)} %bitcast.11), channel_id=1, replica_groups=mesh['yh'=2,'z'=8,'c'=2,'x'=4,'yl'=4] {'c'}, dimensions={0}, use_global_device_ids=true | all-gather | bytes 1179648 | tf_op jit(solution)/shard_map/all_gather | solution.py:194
  49.7 4.5 %shard_map.91 = (f32[128,1536]{1,0:T(8,128)S(1)}, f32[128,1536]{1,0:T(8,128)S(1)}, f32[128,512]{1,0:T(8,128)S(1)}, f32[128,512]{1,0:T(8,128)S(1)}) custom-call(bf16[512,1536]{1,0:T(8,128)(2,1)} %trans_ref.1, bf16[512,1536]{1,0:T(8,128)(2,1)} %ivar_ref.1, s32[12,512]{1,0:T(8,128)S(1)} %bitcast.10, bf16[256,512]{1,0:T(8,128)(2,1)S(1)} %shard_map.90.tangent_ref, ...), custom_call_target="tpu_custom_call" | custom-call | flops 1610612736 | bytes 4718592 | tf_op jit(solution)/shard_map/pallas_call | solution.py:201
  54.3 3.5 %collective-permute-start.5 = (f32[128,512]{1,0:T(8,128)S(1)}, f32[128,512]{1,0:T(8,128)S(1)}, u32[]{:S(2)}, u32[]{:S(2)}) collective-permute-start(f32[128,512]{1,0:T(8,128)S(1)} %get-tuple-element.15), channel_id=1, source_target_pairs={{0,1},{1,0},{2,3},{3,2},{4,5},{5,4},{6,7},{7,6},{8,9},{9,8},{10,11... | collective-permute-start | bytes 786440 | tf_op jit(solution)/shard_map/ppermute | solution.py:19
  58.1 2.4 %all_gather.7.both_ref = s16[256,1664]{1,0:T(8,128)(2,1)S(1)} all-gather(s16[128,1664]{1,0:T(8,128)(2,1)S(1)} %shard_map.92), channel_id=1, replica_groups=mesh['yh'=2,'z'=8,'c'=2,'x'=4,'yl'=4] {'c'}, dimensions={0}, use_global_device_ids=true | all-gather | bytes 1277952 | tf_op jit(solution)/shard_map/all_gather | solution.py:223
  61.6 7.2 %all-to-all-start.1 = ((s16[8,16,1664]{2,1,0:T(8,128)(2,1)}), s16[8,16,1664]{2,1,0:T(8,128)(2,1)S(1)}, u32[]{:S(2)}, u32[]{:S(2)}) async-start(s16[8,16,1664]{2,1,0:T(8,128)(2,1)} %bitcast.3), calls=%async_computation.1 | async-start | bytes 851968 | tf_op jit(solution)/shard_map/all_to_all | solution.py:180
  68.9 3.4 %collective-permute-start.6 = (f32[64,512]{1,0:T(8,128)S(1)}, f32[64,512]{1,0:T(8,128)S(1)}, u32[]{:S(2)}, u32[]{:S(2)}) collective-permute-start(f32[64,512]{1,0:T(8,128)S(1)} %slice.25), channel_id=1, source_target_pairs={{0,4},{4,0},{8,12},{12,8},{1,5},{5,1},{9,13},{13,9},{2,6},{6,2},{1... | collective-permute-start | bytes 393224 | tf_op jit(solution)/shard_map/ppermute | solution.py:19
  72.3 3.7 %collective-permute-done.6 = f32[64,512]{1,0:T(8,128)S(1)} collective-permute-done((f32[64,512]{1,0:T(8,128)S(1)}, f32[64,512]{1,0:T(8,128)S(1)}, u32[]{:S(2)}, u32[]{:S(2)}) %collective-permute-start.6) | collective-permute-done | bytes 131104 | tf_op jit(solution)/shard_map/ppermute | solution.py:19
  76.0 2.4 %collective-permute-start.7 = (f32[32,512]{1,0:T(8,128)S(1)}, f32[32,512]{1,0:T(8,128)S(1)}, u32[]{:S(2)}, u32[]{:S(2)}) collective-permute-start(f32[32,512]{1,0:T(8,128)S(1)} %slice.27), channel_id=1, source_target_pairs={{0,2},{1,3},{2,0},{3,1},{4,6},{5,7},{6,4},{7,5},{8,10},{9,11},{10,... | collective-permute-start | bytes 196616 | tf_op jit(solution)/shard_map/ppermute | solution.py:19
  78.4 4.7 %collective-permute-done.7 = f32[32,512]{1,0:T(8,128)S(1)} collective-permute-done((f32[32,512]{1,0:T(8,128)S(1)}, f32[32,512]{1,0:T(8,128)S(1)}, u32[]{:S(2)}, u32[]{:S(2)}) %collective-permute-start.7) | collective-permute-done | bytes 65568 | tf_op jit(solution)/shard_map/ppermute | solution.py:19
  83.1 1.3 %all-to-all-done.1 = s16[8,16,1664]{2,1,0:T(8,128)(2,1)S(1)} async-done(((s16[8,16,1664]{2,1,0:T(8,128)(2,1)}), s16[8,16,1664]{2,1,0:T(8,128)(2,1)S(1)}, u32[]{:S(2)}, u32[]{:S(2)}) %all-to-all-start.1) | async-done | bytes 426016 | tf_op jit(solution)/shard_map/all_to_all | solution.py:180
  84.7 4.9 %collective-permute-start.8 = (f32[16,512]{1,0:T(8,128)S(1)}, f32[16,512]{1,0:T(8,128)S(1)}, u32[]{:S(2)}, u32[]{:S(2)}) collective-permute-start(f32[16,512]{1,0:T(8,128)S(1)} %slice.29), channel_id=1, source_target_pairs={{0,8},{4,12},{8,0},{12,4},{1,9},{5,13},{9,1},{13,5},{2,10},{6,14},... | collective-permute-start | bytes 98312 | tf_op jit(solution)/shard_map/ppermute | solution.py:19
  89.7 1.9 %collective-permute-start.9 = (s16[8,1664]{1,0:T(8,128)(2,1)S(1)}, s16[8,1664]{1,0:T(8,128)(2,1)S(1)}, u32[]{:S(2)}, u32[]{:S(2)}) collective-permute-start(s16[8,1664]{1,0:T(8,128)(2,1)S(1)} %get-tuple-element.21), channel_id=1, source_target_pairs={{0,256},{256,0},{1,257},{257,1},{2,258},{258,2},{3,259},{259,3},{4... | collective-permute-start | bytes 79880 | tf_op jit(solution)/shard_map/ppermute | solution.py:19
  91.6 7.9 %collective-permute-done.9.came_ref = s16[8,1664]{1,0:T(8,128)(2,1)S(1)} collective-permute-done((s16[8,1664]{1,0:T(8,128)(2,1)S(1)}, s16[8,1664]{1,0:T(8,128)(2,1)S(1)}, u32[]{:S(2)}, u32[]{:S(2)}) %collective-permute-start.9) | collective-permute-done | bytes 26656 | tf_op jit(solution)/shard_map/ppermute | solution.py:19
  (27 shorter events, 3.8 us)
Async XLA Ops:
  0.6 14.9 %collective-permute-start = (bf16[8,1536]{1,0:T(8,128)(2,1)}, bf16[8,1536]{1,0:T(8,128)(2,1)S(1)}, u32[]{:S(2)}, u32[]{:S(2)}) collective-permute-start(bf16[8,1536]{1,0:T(8,128)(2,1)} %mine_ref.1), channel_id=1, source_target_pairs={{0,256},{256,0},{1,257},{257,1},{2,258},{258,2},{3,259},{259,3},{4... | collective-permute-start | bytes 73736 | tf_op jit(solution)/shard_map/ppermute | solution.py:19
  7.5 7.3 %collective-permute-start.1 = (bf16[16,512]{1,0:T(8,128)(2,1)}, bf16[16,512]{1,0:T(8,128)(2,1)S(1)}, u32[]{:S(2)}, u32[]{:S(2)}) collective-permute-start(bf16[16,512]{1,0:T(8,128)(2,1)} %bitcast.8), channel_id=1, source_target_pairs={{0,8},{4,12},{8,0},{12,4},{1,9},{5,13},{9,1},{13,5},{2,10},{6,14},... | collective-permute-start | bytes 49160 | tf_op jit(solution)/shard_map/ppermute | solution.py:19
  14.8 0.7 copy-start
  15.5 34.2 %copy-start.1 = (bf16[256,1536]{1,0:T(8,128)(2,1)S(1)}, bf16[256,1536]{1,0:T(8,128)(2,1)}, u32[]{:S(2)}) copy-start(bf16[256,1536]{1,0:T(8,128)(2,1)} %basis_ref.1) | copy-start | bytes 2359300
  15.5 34.2 %copy-start.2 = (bf16[512,256]{1,0:T(8,128)(2,1)S(1)}, bf16[512,256]{1,0:T(8,128)(2,1)}, u32[]{:S(2)}) copy-start(bf16[512,256]{1,0:T(8,128)(2,1)} %coef_ref.1) | copy-start | bytes 786436
  15.5 34.2 %copy-start.3 = (s32[512,12]{0,1:T(8,128)S(1)}, s32[512,12]{0,1:T(8,128)}, u32[]{:S(2)}) copy-start(s32[512,12]{0,1:T(8,128)} %param.9) | copy-start | bytes 73732
  17.2 30.2 %all-to-all-start = ((bf16[8,16,1536]{2,1,0:T(8,128)(2,1)}), bf16[8,16,1536]{2,1,0:T(8,128)(2,1)S(1)}, u32[]{:S(2)}, u32[]{:S(2)}) async-start(bf16[8,16,1536]{2,1,0:T(8,128)(2,1)} %shard_map.86), calls=%async_computation | async-start | bytes 786432 | tf_op jit(solution)/shard_map/all_to_all | solution.py:180
  27.5 6.8 %collective-permute-start.2 = (bf16[32,512]{1,0:T(8,128)(2,1)S(1)}, bf16[32,512]{1,0:T(8,128)(2,1)S(1)}, u32[]{:S(2)}, u32[]{:S(2)}) collective-permute-start(bf16[32,512]{1,0:T(8,128)(2,1)S(1)} %shard_map.87.mine_ref), channel_id=1, source_target_pairs={{0,2},{1,3},{2,0},{3,1},{4,6},{5,7},{6,4},{7,5},{8,10},{9,11},{10,... | collective-permute-start | bytes 98312 | tf_op jit(solution)/shard_map/ppermute | solution.py:19
  34.3 6.1 %collective-permute-start.3 = (bf16[64,512]{1,0:T(8,128)(2,1)S(1)}, bf16[64,512]{1,0:T(8,128)(2,1)S(1)}, u32[]{:S(2)}, u32[]{:S(2)}) collective-permute-start(bf16[64,512]{1,0:T(8,128)(2,1)S(1)} %shard_map.88.mine_ref), channel_id=1, source_target_pairs={{0,4},{4,0},{8,12},{12,8},{1,5},{5,1},{9,13},{13,9},{2,6},{6,2},{1... | collective-permute-start | bytes 196616 | tf_op jit(solution)/shard_map/ppermute | solution.py:19
  40.4 6.9 %collective-permute-start.4 = (bf16[128,512]{1,0:T(8,128)(2,1)S(1)}, bf16[128,512]{1,0:T(8,128)(2,1)S(1)}, u32[]{:S(2)}, u32[]{:S(2)}) collective-permute-start(bf16[128,512]{1,0:T(8,128)(2,1)S(1)} %shard_map.89.mine_ref), channel_id=1, source_target_pairs={{0,1},{1,0},{2,3},{3,2},{4,5},{5,4},{6,7},{7,6},{8,9},{9,8},{10,11... | collective-permute-start | bytes 393224 | tf_op jit(solution)/shard_map/ppermute | solution.py:19
  54.3 14.5 %collective-permute-start.5 = (f32[128,512]{1,0:T(8,128)S(1)}, f32[128,512]{1,0:T(8,128)S(1)}, u32[]{:S(2)}, u32[]{:S(2)}) collective-permute-start(f32[128,512]{1,0:T(8,128)S(1)} %get-tuple-element.15), channel_id=1, source_target_pairs={{0,1},{1,0},{2,3},{3,2},{4,5},{5,4},{6,7},{7,6},{8,9},{9,8},{10,11... | collective-permute-start | bytes 786440 | tf_op jit(solution)/shard_map/ppermute | solution.py:19
  61.6 22.9 %all-to-all-start.1 = ((s16[8,16,1664]{2,1,0:T(8,128)(2,1)}), s16[8,16,1664]{2,1,0:T(8,128)(2,1)S(1)}, u32[]{:S(2)}, u32[]{:S(2)}) async-start(s16[8,16,1664]{2,1,0:T(8,128)(2,1)} %bitcast.3), calls=%async_computation.1 | async-start | bytes 851968 | tf_op jit(solution)/shard_map/all_to_all | solution.py:180
  68.9 7.2 %collective-permute-start.6 = (f32[64,512]{1,0:T(8,128)S(1)}, f32[64,512]{1,0:T(8,128)S(1)}, u32[]{:S(2)}, u32[]{:S(2)}) collective-permute-start(f32[64,512]{1,0:T(8,128)S(1)} %slice.25), channel_id=1, source_target_pairs={{0,4},{4,0},{8,12},{12,8},{1,5},{5,1},{9,13},{13,9},{2,6},{6,2},{1... | collective-permute-start | bytes 393224 | tf_op jit(solution)/shard_map/ppermute | solution.py:19
  76.0 7.1 %collective-permute-start.7 = (f32[32,512]{1,0:T(8,128)S(1)}, f32[32,512]{1,0:T(8,128)S(1)}, u32[]{:S(2)}, u32[]{:S(2)}) collective-permute-start(f32[32,512]{1,0:T(8,128)S(1)} %slice.27), channel_id=1, source_target_pairs={{0,2},{1,3},{2,0},{3,1},{4,6},{5,7},{6,4},{7,5},{8,10},{9,11},{10,... | collective-permute-start | bytes 196616 | tf_op jit(solution)/shard_map/ppermute | solution.py:19
  84.7 15.4 %collective-permute-start.8 = (f32[16,512]{1,0:T(8,128)S(1)}, f32[16,512]{1,0:T(8,128)S(1)}, u32[]{:S(2)}, u32[]{:S(2)}) collective-permute-start(f32[16,512]{1,0:T(8,128)S(1)} %slice.29), channel_id=1, source_target_pairs={{0,8},{4,12},{8,0},{12,4},{1,9},{5,13},{9,1},{13,5},{2,10},{6,14},... | collective-permute-start | bytes 98312 | tf_op jit(solution)/shard_map/ppermute | solution.py:19
  89.7 9.8 %collective-permute-start.9 = (s16[8,1664]{1,0:T(8,128)(2,1)S(1)}, s16[8,1664]{1,0:T(8,128)(2,1)S(1)}, u32[]{:S(2)}, u32[]{:S(2)}) collective-permute-start(s16[8,1664]{1,0:T(8,128)(2,1)S(1)} %get-tuple-element.21), channel_id=1, source_target_pairs={{0,256},{256,0},{1,257},{257,1},{2,258},{258,2},{3,259},{259,3},{4... | collective-permute-start | bytes 79880 | tf_op jit(solution)/shard_map/ppermute | solution.py:19

commit v9 on v6

--- a/solution.py
+++ b/solution.py
@@ -28,12 +28,22 @@
 
 def fused_kernel(
     trans_ref, ivar_ref, mask_ref, tangent_ref, coef_ref, full_ref, basis_ref,
-    own_ref, other_ref, term_ref, coef_p_ref, coef_t_ref,
+    own_ref, other_ref, term_ref, coef_p_ref, coef_t_ref, trans_here, ivar_here, arrivals,
 ):
     step = pl.program_id(0)
+    steps, _, width = trans_here.shape
+
+    def arrival(k, i):
+        source, here = ((trans_ref, trans_here), (ivar_ref, ivar_here))[k]
+        return pltpu.make_async_copy(
+            source.at[:, i * width : (i + 1) * width], here.at[i], arrivals.at[k, i]
+        )
 
     @pl.when(step == 0)
     def _():
+        for i in range(steps):
+            arrival(0, i).start()
+            arrival(1, i).start()
         rank = coef_ref.shape[1]
         take = lax.broadcasted_iota(I32, (rank, rank), 0)
         place = lax.broadcasted_iota(I32, (rank, rank), 1)
@@ -45,18 +55,25 @@
             chosen, coef, (((0,), (1,)), ((), ())), preferred_element_type=F32
         ).astype(BF16)
 
-    tiles = trans_ref.shape[1] // TILE
+    tiles = width // TILE
     moved = lax.dot_general(
         tangent_ref[...], basis_ref[...], (((0,), (0,)), ((), ())), preferred_element_type=F32
     ) + jnp.dot(coef_p_ref[...], full_ref[...], preferred_element_type=F32)
     mask = mask_ref[...].astype(F32).T
     lanes = lax.broadcasted_iota(I32, mask.shape, 1)
+    for i in range(steps):
+
+        @pl.when(step == i)
+        def _():
+            arrival(0, i).wait()
+            arrival(1, i).wait()
+
     parts = []
     for t in range(tiles):
         part = slice(t * TILE, (t + 1) * TILE)
         column = jnp.sum(jnp.where(lanes == step * tiles + t, mask, 0.0), axis=1, keepdims=True)
-        trans = trans_ref[:, part].astype(F32)
-        weights = trans * trans * ivar_ref[:, part].astype(F32) * column
+        trans = trans_here[step, :, part].astype(F32)
+        weights = trans * trans * ivar_here[step, :, part].astype(F32) * column
         parts.append((weights * moved[:, part]).astype(BF16))
     weighted = jnp.concatenate(parts, axis=1)
 
@@ -108,9 +125,14 @@
     )
 
 
-def spread_kernel(in_ref, out_ref):
-    for i in range(out_ref.shape[0]):
-        out_ref[i] = in_ref[...]
+def spread_kernel(in_ref, out_ref, sent):
+    copies = [
+        pltpu.make_async_copy(in_ref, out_ref.at[i], sent.at[i]) for i in range(out_ref.shape[0])
+    ]
+    for copy in copies:
+        copy.start()
+    for copy in copies:
+        copy.wait()
 
 
 def spread_pair_kernel(mine_ref, other_ref, out_ref):
@@ -169,22 +191,29 @@
     exchange = lambda value, axis: lax.all_to_all(value, axis, 0, 0, tiled=True)
 
     across = partner(basis_tangent, "yh", 1)
-    [tangent] = small(spread_kernel, ((16, ours, rows), BF16))(coef_tangent.T)
+    tangent = pl.pallas_call(
+        spread_kernel,
+        out_shape=jax.ShapeDtypeStruct((16, ours, rows), BF16),
+        out_specs=pl.BlockSpec(memory_space=pl.ANY),
+        scratch_shapes=[pltpu.SemaphoreType.DMA((16,))],
+        compiler_params=pltpu.CompilerParams(vmem_limit_bytes=8 << 20),
+    )(in_hbm(coef_tangent.T))
     tangent = exchange(tangent, ("x", "yl")).reshape(rank, rows)
     across, tangent = lax.optimization_barrier((across, tangent))
 
-    [pair] = small(spread_pair_kernel, ((8, 2 * mine, cols), BF16))(basis_tangent, across)
+    [pair] = small(spread_pair_kernel, ((8, 2 * mine, cols), BF16))(in_hbm(basis_tangent), across)
     arrived = exchange(pair, "z").reshape(half, cols)
     full = lax.all_gather(arrived, "c", axis=0, tiled=True)
 
     width = cols // 2
+    anywhere = pl.BlockSpec(memory_space=pl.ANY)
     whole = lambda *shape: pl.BlockSpec(shape, lambda i: (0,) * len(shape))
     tall = lambda n: pl.BlockSpec((n, width), lambda i: (0, i))
     own, other, term = pl.pallas_call(
         fused_kernel,
         grid=(cols // width,),
         in_specs=[
-            tall(rows), tall(rows), whole(cols // TILE, rows), whole(rank, rows),
+            anywhere, anywhere, whole(cols // TILE, rows), whole(rank, rows),
             whole(rows, rank), tall(rank), tall(rank),
         ],
         out_specs=[tall(half), tall(half), whole(rank, rows)],
@@ -193,7 +222,13 @@
             jax.ShapeDtypeStruct((half, cols), F32),
             jax.ShapeDtypeStruct((rank, rows), F32),
         ],
-        scratch_shapes=[pltpu.VMEM((rows, rank), BF16), pltpu.VMEM((rank, rows), BF16)],
+        scratch_shapes=[
+            pltpu.VMEM((rows, rank), BF16),
+            pltpu.VMEM((rank, rows), BF16),
+            pltpu.VMEM((cols // width, rows, width), BF16),
+            pltpu.VMEM((cols // width, rows, width), BF16),
+            pltpu.SemaphoreType.DMA((2, cols // width)),
+        ],
         compiler_params=pltpu.CompilerParams(vmem_limit_bytes=32 << 20),
         cost_estimate=pl.CostEstimate(
             flops=8 * rows * cols * rank, bytes_accessed=6 * rows * cols, transcendentals=0
@@ -203,7 +238,14 @@
     [codes] = small(pack_kernel, ((half, cols + TILE), I16))(other)
     codes = lax.all_gather(codes, "c", axis=0, tiled=True)
     [codes] = small(add_kernel, ((half, cols + TILE), I16))(own, codes)
-    [terms] = small(pack_kernel, ((rank, rows + TILE), I16))(term)
+    terms = pl.pallas_call(
+        pack_kernel,
+        grid=(4,),
+        in_specs=[pl.BlockSpec((rank // 4, rows), lambda i: (i, 0))],
+        out_specs=pl.BlockSpec((rank // 4, rows + TILE), lambda i: (i, 0)),
+        out_shape=jax.ShapeDtypeStruct((rank, rows + TILE), I16),
+        compiler_params=pltpu.CompilerParams(vmem_limit_bytes=8 << 20),
+    )(term)
     codes, terms = lax.optimization_barrier((codes, terms))
     codes = exchange(codes.reshape(8, 2 * mine, cols + TILE), "z").reshape(half, cols + TILE)
 

time: 94.5 us -> 95.3 us (level)
  Pallas kernels: 8.67 us -> 11.1 us
  local copies, waits for them, and re-layouts: 1.46 us -> 0.01 us
    pallas_call x3, Pallas kernels: 6.29 us -> 8.03 us  [the longest x1 4.61 us: body(): pl.pallas_call(fused_kernel, grid=(cols // width,), in_specs=[anywhere, a...]
    unnamed x10 -> x6, local copies, waits for them, and re-layouts: 1.46 us -> 0.01 us
where the time goes in v9:
time: 95.3 us; the launch traced here: 94.1 us
  blocking collectives  44.7 us (47%)
  starting transfers between devices  25.5 us (27%)
  waiting for transfers between devices  12.1 us (13%)
  Pallas kernels  11.1 us (12%)
    all_to_all x2, blocking collectives, body(): exchange = lambda value, axis: lax.all_to_all(value, axis, 0, 0, tiled=True)  39.9 us
    all_to_all x2, starting transfers between devices, body(): exchange = lambda value, axis: lax.all_to_all(value, axis, 0, 0, tiled=True)  16.9 us
    ppermute x2, starting transfers between devices, partner(): lax.ppermute(value, axis, [(i, i ^ flip) for i in range(lax.axis_size(axi...  8.58 us
    ppermute x2, waiting for transfers between devices, partner(): lax.ppermute(value, axis, [(i, i ^ flip) for i in range(lax.axis_size(axi...  6.33 us
    all_to_all x2, waiting for transfers between devices, body(): exchange = lambda value, axis: lax.all_to_all(value, axis, 0, 0, tiled=True)  5.82 us
    pallas_call x1, Pallas kernels, body(): pl.pallas_call(fused_kernel, grid=(cols // width,), in_specs=[anywhere, a...  4.61 us
    all_gather x1, blocking collectives, body(): codes = lax.all_gather(codes, 'c', axis=0, tiled=True)  2.42 us
    all_gather x1, blocking collectives, body(): full = lax.all_gather(arrived, 'c', axis=0, tiled=True)  2.36 us
  transfers between devices with their start and end apart: 4, of which 2 were waited for; matrix products, arithmetic and copies ran while one was open for 0% of the time, Pallas kernels for 1%

profile of v9, /device:TPU:6, one launch (start us, length us, event | category | flops | bytes accessed | tf_op | source)
XLA Modules:
  0.0 94.1 jit_solution(8253704113769527445)
XLA Ops:
  0.6 0.0 copy-start
  0.6 0.0 copy-start.1
  0.7 0.0 copy-start.2
  0.7 1.7 %shard_map.86 = bf16[16,16,512]{2,1,0:T(8,128)(2,1)} custom-call(bf16[16,512]{1,0:T(8,128)(2,1)} %bitcast.16), custom_call_target="tpu_custom_call" | custom-call | tf_op jit(solution)/shard_map/pallas_call | solution.py:194
  2.3 9.3 %all-to-all-start = ((bf16[16,16,512]{2,1,0:T(8,128)(2,1)}), bf16[16,16,512]{2,1,0:T(8,128)(2,1)S(1)}, u32[]{:S(2)}, u32[]{:S(2)}) async-start(bf16[16,16,512]{2,1,0:T(8,128)(2,1)} %shard_map.86), calls=%async_computation | async-start | bytes 524288 | tf_op jit(solution)/shard_map/all_to_all | solution.py:191
  11.6 3.6 %collective-permute-start = (bf16[8,1536]{1,0:T(8,128)(2,1)}, bf16[8,1536]{1,0:T(8,128)(2,1)S(1)}, u32[]{:S(2)}, u32[]{:S(2)}) collective-permute-start(bf16[8,1536]{1,0:T(8,128)(2,1)} %mine_ref.1), channel_id=1, source_target_pairs={{0,256},{256,0},{1,257},{257,1},{2,258},{258,2},{3,259},{259,3},{4... | collective-permute-start | bytes 73736 | tf_op jit(solution)/shard_map/ppermute | solution.py:18
  15.2 6.3 %collective-permute-done.other_ref = bf16[8,1536]{1,0:T(8,128)(2,1)S(1)} collective-permute-done((bf16[8,1536]{1,0:T(8,128)(2,1)}, bf16[8,1536]{1,0:T(8,128)(2,1)S(1)}, u32[]{:S(2)}, u32[]{:S(2)}) %collective-permute-start) | collective-permute-done | bytes 24608 | tf_op jit(solution)/shard_map/ppermute | solution.py:18
  21.5 0.0 all-to-all-done
  21.5 0.8 shard_map.87
  22.3 21.6 %all_to_all.20 = bf16[8,16,1536]{2,1,0:T(8,128)(2,1)S(1)} all-to-all(bf16[8,16,1536]{2,1,0:T(8,128)(2,1)S(1)} %shard_map.87), channel_id=1, replica_groups=mesh['yh'=2,'z'=8,'c'=2,'x'=4,'yl'=4] {'z'}, dimensions={0} | all-to-all | bytes 786432 | tf_op jit(solution)/shard_map/all_to_all | solution.py:191
  43.9 2.4 %all_gather.6.full_ref = bf16[256,1536]{1,0:T(8,128)(2,1)S(1)} all-gather(bf16[128,1536]{1,0:T(8,128)(2,1)S(1)} %bitcast.14), channel_id=1, replica_groups=mesh['yh'=2,'z'=8,'c'=2,'x'=4,'yl'=4] {'c'}, dimensions={0}, use_global_device_ids=true | all-gather | bytes 1179648 | tf_op jit(solution)/shard_map/all_gather | solution.py:206
  46.2 4.6 %shard_map.88 = (f32[128,1536]{1,0:T(8,128)S(1)}, f32[128,1536]{1,0:T(8,128)S(1)}, f32[256,512]{1,0:T(8,128)S(1)}) custom-call(bf16[512,1536]{1,0:T(8,128)(2,1)} %trans_ref.1, bf16[512,1536]{1,0:T(8,128)(2,1)} %ivar_ref.1, s32[12,512]{1,0:T(8,128)S(1)} %bitcast.13, bf16[256,512]{1,0:T(8,128)(2,1)S(1)} %bitcast.12, bf16[512,256]{1,0:T(8,128)(2,1)S(1)} %copy-done.1, ...), custom_call_target="tpu_custom_call" | custom-call | flops 1610612736 | bytes 4718592 | tf_op jit(solution)/shard_map/pallas_call | solution.py:212
  50.9 1.8 %shard_map.91 = s16[256,640]{1,0:T(8,128)(2,1)} custom-call(f32[256,512]{1,0:T(8,128)S(1)} %get-tuple-element.15.term_ref), custom_call_target="tpu_custom_call" | custom-call | tf_op jit(solution)/shard_map/pallas_call | solution.py:241
  52.6 0.3 shard_map.89
  52.9 2.4 %all_gather.7.both_ref = s16[256,1664]{1,0:T(8,128)(2,1)S(1)} all-gather(s16[128,1664]{1,0:T(8,128)(2,1)S(1)} %shard_map.89), channel_id=1, replica_groups=mesh['yh'=2,'z'=8,'c'=2,'x'=4,'yl'=4] {'c'}, dimensions={0}, use_global_device_ids=true | all-gather | bytes 1277952 | tf_op jit(solution)/shard_map/all_gather | solution.py:239
  55.3 0.4 shard_map.90
  55.7 18.4 %all_to_all.21 = s16[8,16,1664]{2,1,0:T(8,128)(2,1)S(1)} all-to-all(s16[8,16,1664]{2,1,0:T(8,128)(2,1)S(1)} %bitcast.10), channel_id=1, replica_groups=mesh['yh'=2,'z'=8,'c'=2,'x'=4,'yl'=4] {'z'}, dimensions={0} | all-to-all | bytes 851968 | tf_op jit(solution)/shard_map/all_to_all | solution.py:191
  74.0 7.6 %all-to-all-start.2 = ((s16[16,16,640]{2,1,0:T(8,128)(2,1)}), s16[16,16,640]{2,1,0:T(8,128)(2,1)S(1)}, u32[]{:S(2)}, u32[]{:S(2)}) async-start(s16[16,16,640]{2,1,0:T(8,128)(2,1)} %bitcast.4), calls=%async_computation.2 | async-start | bytes 655360 | tf_op jit(solution)/shard_map/all_to_all | solution.py:191
  81.6 0.3 shard_map.93
  81.9 5.0 %collective-permute-start.1 = (s16[8,1664]{1,0:T(8,128)(2,1)S(1)}, s16[8,1664]{1,0:T(8,128)(2,1)S(1)}, u32[]{:S(2)}, u32[]{:S(2)}) collective-permute-start(s16[8,1664]{1,0:T(8,128)(2,1)S(1)} %get-tuple-element.19), channel_id=1, source_target_pairs={{0,256},{256,0},{1,257},{257,1},{2,258},{258,2},{3,259},{259,3},{4... | collective-permute-start | bytes 79880 | tf_op jit(solution)/shard_map/ppermute | solution.py:18
  86.9 5.8 %all-to-all-done.2 = s16[16,16,640]{2,1,0:T(8,128)(2,1)S(1)} async-done(((s16[16,16,640]{2,1,0:T(8,128)(2,1)}), s16[16,16,640]{2,1,0:T(8,128)(2,1)S(1)}, u32[]{:S(2)}, u32[]{:S(2)}) %all-to-all-start.2) | async-done | bytes 327712 | tf_op jit(solution)/shard_map/all_to_all | solution.py:191
  92.7 0.8 shard_map.92
  93.5 0.0 collective-permute-done.1.came_ref
  93.5 0.6 shard_map.94
  (3 shorter events, 0.0 us)
Async XLA Ops:
  0.6 45.6 %copy-start = (bf16[256,1536]{1,0:T(8,128)(2,1)S(1)}, bf16[256,1536]{1,0:T(8,128)(2,1)}, u32[]{:S(2)}) copy-start(bf16[256,1536]{1,0:T(8,128)(2,1)} %basis_ref.1) | copy-start | bytes 2359300
  0.6 45.6 %copy-start.1 = (bf16[512,256]{1,0:T(8,128)(2,1)S(1)}, bf16[512,256]{1,0:T(8,128)(2,1)}, u32[]{:S(2)}) copy-start(bf16[512,256]{1,0:T(8,128)(2,1)} %coef_ref.1) | copy-start | bytes 786436
  0.7 45.6 %copy-start.2 = (s32[512,12]{0,1:T(8,128)S(1)}, s32[512,12]{0,1:T(8,128)}, u32[]{:S(2)}) copy-start(s32[512,12]{0,1:T(8,128)} %param.9) | copy-start | bytes 73732
  2.3 19.2 %all-to-all-start = ((bf16[16,16,512]{2,1,0:T(8,128)(2,1)}), bf16[16,16,512]{2,1,0:T(8,128)(2,1)S(1)}, u32[]{:S(2)}, u32[]{:S(2)}) async-start(bf16[16,16,512]{2,1,0:T(8,128)(2,1)} %shard_map.86), calls=%async_computation | async-start | bytes 524288 | tf_op jit(solution)/shard_map/all_to_all | solution.py:191
  11.6 10.0 %collective-permute-start = (bf16[8,1536]{1,0:T(8,128)(2,1)}, bf16[8,1536]{1,0:T(8,128)(2,1)S(1)}, u32[]{:S(2)}, u32[]{:S(2)}) collective-permute-start(bf16[8,1536]{1,0:T(8,128)(2,1)} %mine_ref.1), channel_id=1, source_target_pairs={{0,256},{256,0},{1,257},{257,1},{2,258},{258,2},{3,259},{259,3},{4... | collective-permute-start | bytes 73736 | tf_op jit(solution)/shard_map/ppermute | solution.py:18
  74.0 18.7 %all-to-all-start.2 = ((s16[16,16,640]{2,1,0:T(8,128)(2,1)}), s16[16,16,640]{2,1,0:T(8,128)(2,1)S(1)}, u32[]{:S(2)}, u32[]{:S(2)}) async-start(s16[16,16,640]{2,1,0:T(8,128)(2,1)} %bitcast.4), calls=%async_computation.2 | async-start | bytes 655360 | tf_op jit(solution)/shard_map/all_to_all | solution.py:191
  81.9 11.6 %collective-permute-start.1 = (s16[8,1664]{1,0:T(8,128)(2,1)S(1)}, s16[8,1664]{1,0:T(8,128)(2,1)S(1)}, u32[]{:S(2)}, u32[]{:S(2)}) collective-permute-start(s16[8,1664]{1,0:T(8,128)(2,1)S(1)} %get-tuple-element.19), channel_id=1, source_target_pairs={{0,256},{256,0},{1,257},{257,1},{2,258},{258,2},{3,259},{259,3},{4... | collective-permute-start | bytes 79880 | tf_op jit(solution)/shard_map/ppermute | solution.py:18

commit v10 on v6

--- a/solution.py
+++ b/solution.py
@@ -37,12 +37,13 @@
         rank = coef_ref.shape[1]
         take = lax.broadcasted_iota(I32, (rank, rank), 0)
         place = lax.broadcasted_iota(I32, (rank, rank), 1)
-        low, mid, high = place & 7, place & 112, ((place >> 3) & 1) * 128 + ((place >> 7) & 1) * 8
-        chosen = (take == low + mid + high).astype(BF16)
+        core, row = (place >> 7) * 8, place & 7
+        by_column = (take == ((place >> 3) & 15) * 16 + core + row).astype(BF16)
+        by_row = (take == ((place >> 3) & 1) * 128 + (place & 112) + core + row).astype(BF16)
         coef = coef_ref[...]
-        coef_p_ref[...] = jnp.dot(coef, chosen, preferred_element_type=F32).astype(BF16)
+        coef_p_ref[...] = jnp.dot(coef, by_column, preferred_element_type=F32).astype(BF16)
         coef_t_ref[...] = lax.dot_general(
-            chosen, coef, (((0,), (1,)), ((), ())), preferred_element_type=F32
+            by_row, coef, (((0,), (1,)), ((), ())), preferred_element_type=F32
         ).astype(BF16)
 
     tiles = trans_ref.shape[1] // TILE
@@ -113,15 +114,6 @@
         out_ref[i] = in_ref[...]
 
 
-def spread_pair_kernel(mine_ref, other_ref, out_ref):
-    mine, other = mine_ref[...].astype(F32), other_ref[...].astype(F32)
-    first = lax.axis_index("yh") == 0
-    pair = [jnp.where(first, mine, other), jnp.where(first, other, mine)]
-    pair = jnp.concatenate(pair, axis=0).astype(BF16)
-    for i in range(out_ref.shape[0]):
-        out_ref[i] = pair
-
-
 def pack_kernel(term_ref, out_ref):
     encode(term_ref[...], out_ref)
 
@@ -168,13 +160,12 @@
     )
     exchange = lambda value, axis: lax.all_to_all(value, axis, 0, 0, tiled=True)
 
-    across = partner(basis_tangent, "yh", 1)
     [tangent] = small(spread_kernel, ((16, ours, rows), BF16))(coef_tangent.T)
+    [spread] = small(spread_kernel, ((16, mine, cols), BF16))(in_hbm(basis_tangent))
+    tangent, spread = lax.optimization_barrier((tangent, spread))
     tangent = exchange(tangent, ("x", "yl")).reshape(rank, rows)
-    across, tangent = lax.optimization_barrier((across, tangent))
-
-    [pair] = small(spread_pair_kernel, ((8, 2 * mine, cols), BF16))(basis_tangent, across)
-    arrived = exchange(pair, "z").reshape(half, cols)
+    spread, tangent = lax.optimization_barrier((spread, tangent))
+    arrived = exchange(spread, ("yh", "z")).reshape(half, cols)
     full = lax.all_gather(arrived, "c", axis=0, tiled=True)
 
     width = cols // 2
@@ -198,7 +189,7 @@
         cost_estimate=pl.CostEstimate(
             flops=8 * rows * cols * rank, bytes_accessed=6 * rows * cols, transcendentals=0
         ),
-    )(*map(in_hbm, (transmission, inverse_var)), pixel_mask.T, tangent, coef, full, basis)
+    )(transmission, in_hbm(inverse_var), pixel_mask.T, tangent, coef, full, basis)
 
     [codes] = small(pack_kernel, ((half, cols + TILE), I16))(other)
     codes = lax.all_gather(codes, "c", axis=0, tiled=True)

time: 94.5 us -> 96.1 us (1.017)
  blocking collectives: 44.8 us -> 67.3 us
  starting transfers between devices: 25.4 us -> 10.8 us
  waiting for transfers between devices: 12.1 us -> 6.94 us
    all_to_all x2 -> x3, blocking collectives: 40.1 us -> 62.5 us  [body(): exchange = lambda value, axis: lax.all_to_all(value, axis, 0, 0, tiled=True)]
    all_to_all x2 -> x1, starting transfers between devices: 16.9 us -> 8.2 us  [body(): exchange = lambda value, axis: lax.all_to_all(value, axis, 0, 0, tiled=True)]
    ppermute x2 -> x1, waiting for transfers between devices: 6.33 us -> 0.01 us  [partner(): lax.ppermute(value, axis, [(i, i ^ flip) for i in range(lax.axis_size(axi...]
    ppermute x2 -> x1, starting transfers between devices: 8.59 us -> 2.57 us  [partner(): lax.ppermute(value, axis, [(i, i ^ flip) for i in range(lax.axis_size(axi...]
    all_to_all x2 -> x1, waiting for transfers between devices: 5.81 us -> 6.94 us  [body(): exchange = lambda value, axis: lax.all_to_all(value, axis, 0, 0, tiled=True)]
  transfers between devices with their start and end apart: 4 -> 2, of which waited for: 2 -> 1; matrix products, arithmetic and copies ran while one was open for 0% -> 0% of each run, Pallas kernels for 1% -> 1%
where the time goes in v10:
time: 96.1 us; the launch traced here: 95.1 us
  blocking collectives  67.3 us (70%)
  starting transfers between devices  10.8 us (11%)
  Pallas kernels  8.64 us (9%)
  waiting for transfers between devices  6.94 us (7%)
    all_to_all x3, blocking collectives, body(): exchange = lambda value, axis: lax.all_to_all(value, axis, 0, 0, tiled=True)  62.5 us
    all_to_all x1, starting transfers between devices, body(): exchange = lambda value, axis: lax.all_to_all(value, axis, 0, 0, tiled=True)  8.2 us
    all_to_all x1, waiting for transfers between devices, body(): exchange = lambda value, axis: lax.all_to_all(value, axis, 0, 0, tiled=True)  6.94 us
    pallas_call x1, Pallas kernels, body(): pl.pallas_call(fused_kernel, grid=(cols // width,), in_specs=[tall(rows),...  4.3 us
    ppermute x1, starting transfers between devices, partner(): lax.ppermute(value, axis, [(i, i ^ flip) for i in range(lax.axis_size(axi...  2.57 us
    all_gather x1, blocking collectives, body(): codes = lax.all_gather(codes, 'c', axis=0, tiled=True)  2.42 us
    all_gather x1, blocking collectives, body(): full = lax.all_gather(arrived, 'c', axis=0, tiled=True)  2.36 us
  transfers between devices with their start and end apart: 2, of which 1 were waited for; matrix products, arithmetic and copies ran while one was open for 0% of the time, Pallas kernels for 1%

profile of v10, /device:TPU:6, one launch (start us, length us, event | category | flops | bytes accessed | tf_op | source)
XLA Modules:
  0.0 95.1 jit_solution(4006956084969207900)
XLA Ops:
  0.6 0.0 copy-start
  0.6 0.7 copy-done
  1.3 0.0 copy-start.1
  1.4 0.9 shard_map.87
  2.3 16.2 %all_to_all.20 = bf16[16,16,512]{2,1,0:T(8,128)(2,1)S(1)} all-to-all(bf16[16,16,512]{2,1,0:T(8,128)(2,1)S(1)} %shard_map.86), channel_id=1, replica_groups=mesh['yh'=2,'z'=8,'c'=2,'x'=4,'yl'=4] {'x','yl'}, dimensions={0} | all-to-all | bytes 524288 | tf_op jit(solution)/shard_map/all_to_all | solution.py:161
  18.5 26.7 %all_to_all.21 = bf16[16,8,1536]{2,1,0:T(8,128)(2,1)S(1)} all-to-all(bf16[16,8,1536]{2,1,0:T(8,128)(2,1)S(1)} %shard_map.87), channel_id=1, replica_groups=mesh['yh'=2,'z'=8,'c'=2,'x'=4,'yl'=4] {'yh','z'}, dimensions={0} | all-to-all | bytes 786432 | tf_op jit(solution)/shard_map/all_to_all | solution.py:161
  45.3 2.4 %all_gather.6.full_ref = bf16[256,1536]{1,0:T(8,128)(2,1)S(1)} all-gather(bf16[128,1536]{1,0:T(8,128)(2,1)S(1)} %bitcast.15), channel_id=1, replica_groups=mesh['yh'=2,'z'=8,'c'=2,'x'=4,'yl'=4] {'c'}, dimensions={0}, use_global_device_ids=true | all-gather | bytes 1179648 | tf_op jit(solution)/shard_map/all_gather | solution.py:169
  47.6 0.0 copy-done.1
  47.6 0.0 copy-done.2
  47.6 0.0 copy-done.3
  47.6 0.0 copy-done.4
  47.7 4.3 %shard_map.88 = (f32[128,1536]{1,0:T(8,128)S(1)}, f32[128,1536]{1,0:T(8,128)S(1)}, f32[256,512]{1,0:T(8,128)S(1)}) custom-call(bf16[512,1536]{1,0:T(8,128)(2,1)S(1)} %copy-done.1, bf16[512,1536]{1,0:T(8,128)(2,1)} %ivar_ref.1, s32[12,512]{1,0:T(8,128)S(1)} %bitcast.14, bf16[256,512]{1,0:T(8,128)(2,1)S(1)} %bitcast.12, bf16[512,256]{1,0:T(8,128)(2,1)S(1)} %copy-done.3, ...), custom_call_target="tpu_custom_call" | custom-call | flops 1610612736 | bytes 4718592 | tf_op jit(solution)/shard_map/pallas_call | solution.py:174
  52.0 1.1 %shard_map.91 = s16[256,640]{1,0:T(8,128)(2,1)} custom-call(f32[256,512]{1,0:T(8,128)S(1)} %get-tuple-element.19.term_ref), custom_call_target="tpu_custom_call" | custom-call | tf_op jit(solution)/shard_map/pallas_call | solution.py:197
  53.0 0.3 shard_map.89
  53.3 2.4 %all_gather.7.both_ref = s16[256,1664]{1,0:T(8,128)(2,1)S(1)} all-gather(s16[128,1664]{1,0:T(8,128)(2,1)S(1)} %shard_map.89), channel_id=1, replica_groups=mesh['yh'=2,'z'=8,'c'=2,'x'=4,'yl'=4] {'c'}, dimensions={0}, use_global_device_ids=true | all-gather | bytes 1277952 | tf_op jit(solution)/shard_map/all_gather | solution.py:195
  55.7 0.4 shard_map.90
  56.1 19.6 %all_to_all.22 = s16[8,16,1664]{2,1,0:T(8,128)(2,1)S(1)} all-to-all(s16[8,16,1664]{2,1,0:T(8,128)(2,1)S(1)} %bitcast.10), channel_id=1, replica_groups=mesh['yh'=2,'z'=8,'c'=2,'x'=4,'yl'=4] {'z'}, dimensions={0} | all-to-all | bytes 851968 | tf_op jit(solution)/shard_map/all_to_all | solution.py:161
  75.6 8.2 %all-to-all-start.2 = ((s16[16,16,640]{2,1,0:T(8,128)(2,1)}), s16[16,16,640]{2,1,0:T(8,128)(2,1)S(1)}, u32[]{:S(2)}, u32[]{:S(2)}) async-start(s16[16,16,640]{2,1,0:T(8,128)(2,1)} %bitcast.4), calls=%async_computation.2 | async-start | bytes 655360 | tf_op jit(solution)/shard_map/all_to_all | solution.py:161
  83.8 0.3 shard_map.93
  84.1 2.6 %collective-permute-start = (s16[8,1664]{1,0:T(8,128)(2,1)S(1)}, s16[8,1664]{1,0:T(8,128)(2,1)S(1)}, u32[]{:S(2)}, u32[]{:S(2)}) collective-permute-start(s16[8,1664]{1,0:T(8,128)(2,1)S(1)} %get-tuple-element.23), channel_id=1, source_target_pairs={{0,256},{256,0},{1,257},{257,1},{2,258},{258,2},{3,259},{259,3},{4... | collective-permute-start | bytes 79880 | tf_op jit(solution)/shard_map/ppermute | solution.py:18
  86.7 6.9 %all-to-all-done.2 = s16[16,16,640]{2,1,0:T(8,128)(2,1)S(1)} async-done(((s16[16,16,640]{2,1,0:T(8,128)(2,1)}), s16[16,16,640]{2,1,0:T(8,128)(2,1)S(1)}, u32[]{:S(2)}, u32[]{:S(2)}) %all-to-all-start.2) | async-done | bytes 327712 | tf_op jit(solution)/shard_map/all_to_all | solution.py:161
  93.6 0.8 shard_map.92
  94.4 0.0 collective-permute-done.came_ref
  94.5 0.6 shard_map.94
  (4 shorter events, 0.0 us)
Async XLA Ops:
  0.6 0.7 copy-start
  1.3 46.3 %copy-start.1 = (bf16[512,1536]{1,0:T(8,128)(2,1)S(1)}, bf16[512,1536]{1,0:T(8,128)(2,1)}, u32[]{:S(2)}) copy-start(bf16[512,1536]{1,0:T(8,128)(2,1)} %trans_ref.1) | copy-start | bytes 4718596
  1.4 46.3 %copy-start.2 = (bf16[256,1536]{1,0:T(8,128)(2,1)S(1)}, bf16[256,1536]{1,0:T(8,128)(2,1)}, u32[]{:S(2)}) copy-start(bf16[256,1536]{1,0:T(8,128)(2,1)} %basis_ref.1) | copy-start | bytes 2359300
  1.4 46.3 %copy-start.3 = (bf16[512,256]{1,0:T(8,128)(2,1)S(1)}, bf16[512,256]{1,0:T(8,128)(2,1)}, u32[]{:S(2)}) copy-start(bf16[512,256]{1,0:T(8,128)(2,1)} %coef_ref.1) | copy-start | bytes 786436
  1.4 46.3 %copy-start.4 = (s32[512,12]{0,1:T(8,128)S(1)}, s32[512,12]{0,1:T(8,128)}, u32[]{:S(2)}) copy-start(s32[512,12]{0,1:T(8,128)} %param.9) | copy-start | bytes 73732
  75.6 18.0 %all-to-all-start.2 = ((s16[16,16,640]{2,1,0:T(8,128)(2,1)}), s16[16,16,640]{2,1,0:T(8,128)(2,1)S(1)}, u32[]{:S(2)}, u32[]{:S(2)}) async-start(s16[16,16,640]{2,1,0:T(8,128)(2,1)} %bitcast.4), calls=%async_computation.2 | async-start | bytes 655360 | tf_op jit(solution)/shard_map/all_to_all | solution.py:161
  84.1 10.3 %collective-permute-start = (s16[8,1664]{1,0:T(8,128)(2,1)S(1)}, s16[8,1664]{1,0:T(8,128)(2,1)S(1)}, u32[]{:S(2)}, u32[]{:S(2)}) collective-permute-start(s16[8,1664]{1,0:T(8,128)(2,1)S(1)} %get-tuple-element.23), channel_id=1, source_target_pairs={{0,256},{256,0},{1,257},{257,1},{2,258},{258,2},{3,259},{259,3},{4... | collective-permute-start | bytes 79880 | tf_op jit(solution)/shard_map/ppermute | solution.py:18

commit v11 on v6

--- a/solution.py
+++ b/solution.py
@@ -122,8 +122,9 @@
         out_ref[i] = pair
 
 
-def pack_kernel(term_ref, out_ref):
-    encode(term_ref[...], out_ref)
+def pack_kernel(term_ref, other_ref, term_codes_ref, other_codes_ref):
+    encode(term_ref[...], term_codes_ref)
+    encode(other_ref[...], other_codes_ref)
 
 
 def add_kernel(own_ref, both_ref, out_ref):
@@ -145,14 +146,11 @@
     encode(jnp.where(first, high, low), give_ref)
 
 
-def last_kernel(divisor, mine_ref, came_ref, out_ref):
-    out_ref[...] = (mine_ref[...] + decode(came_ref)) * (1.0 / divisor)
-
-
-def coef_kernel(divisor, in_ref, out_ref):
-    n = out_ref.shape[0]
-    total = sum(decode(part_of(in_ref, i, n)) for i in range(in_ref.shape[0] // n))
-    out_ref[...] = total * (1.0 / divisor)
+def last_kernel(divisors, terms_ref, mine_ref, came_ref, coef_ref, basis_ref):
+    n = coef_ref.shape[0]
+    total = sum(decode(part_of(terms_ref, i, n)) for i in range(terms_ref.shape[0] // n))
+    coef_ref[...] = total * (1.0 / divisors[0])
+    basis_ref[...] = (mine_ref[...] + decode(came_ref)) * (1.0 / divisors[1])
 
 
 def body(transmission, inverse_var, pixel_mask, coef, basis, coef_tangent, basis_tangent):
@@ -173,7 +171,7 @@
     tangent = exchange(tangent, ("x", "yl")).reshape(rank, rows)
     across, tangent = lax.optimization_barrier((across, tangent))
 
-    [pair] = small(spread_pair_kernel, ((8, 2 * mine, cols), BF16))(basis_tangent, across)
+    [pair] = small(spread_pair_kernel, ((8, 2 * mine, cols), BF16))(in_hbm(basis_tangent), across)
     arrived = exchange(pair, "z").reshape(half, cols)
     full = lax.all_gather(arrived, "c", axis=0, tiled=True)
 
@@ -194,27 +192,28 @@
             jax.ShapeDtypeStruct((rank, rows), F32),
         ],
         scratch_shapes=[pltpu.VMEM((rows, rank), BF16), pltpu.VMEM((rank, rows), BF16)],
-        compiler_params=pltpu.CompilerParams(vmem_limit_bytes=32 << 20),
+        compiler_params=pltpu.CompilerParams(vmem_limit_bytes=16 << 20),
         cost_estimate=pl.CostEstimate(
             flops=8 * rows * cols * rank, bytes_accessed=6 * rows * cols, transcendentals=0
         ),
-    )(*map(in_hbm, (transmission, inverse_var)), pixel_mask.T, tangent, coef, full, basis)
-
-    [codes] = small(pack_kernel, ((half, cols + TILE), I16))(other)
+    )(transmission, inverse_var, pixel_mask.T, tangent, in_hbm(coef), full, in_hbm(basis))
+
+    terms, codes = small(
+        pack_kernel, ((rank, rows + TILE), I16), ((half, cols + TILE), I16)
+    )(term, other)
     codes = lax.all_gather(codes, "c", axis=0, tiled=True)
     [codes] = small(add_kernel, ((half, cols + TILE), I16))(own, codes)
-    [terms] = small(pack_kernel, ((rank, rows + TILE), I16))(term)
+    codes = exchange(codes.reshape(8, 2 * mine, cols + TILE), "z").reshape(half, cols + TILE)
     codes, terms = lax.optimization_barrier((codes, terms))
-    codes = exchange(codes.reshape(8, 2 * mine, cols + TILE), "z").reshape(half, cols + TILE)
 
     keep, give = small(halve_kernel, ((mine, cols), F32), ((mine, cols + TILE), I16))(codes)
-    [basis_grad] = small(
-        functools.partial(last_kernel, math.sqrt(exposures)), ((mine, cols), F32)
-    )(keep, partner(give, "yh", 1))
+    came = partner(give, "yh", 1)
     terms = exchange(terms.reshape(16, ours, rows + TILE), ("x", "yl")).reshape(rank, rows + TILE)
-    [coef_grad] = small(
-        functools.partial(coef_kernel, math.sqrt(pixels)), ((ours, rows), F32)
-    )(terms)
+    coef_grad, basis_grad = small(
+        functools.partial(last_kernel, (math.sqrt(pixels), math.sqrt(exposures))),
+        ((ours, rows), F32),
+        ((mine, cols), F32),
+    )(terms, keep, came)
     return (coef_grad.T, basis_grad)
 
 

time: 94.5 us -> 93.4 us (0.988)
    all_to_all x2, waiting for transfers between devices: 5.81 us -> 1.04 us  [body(): exchange = lambda value, axis: lax.all_to_all(value, axis, 0, 0, tiled=True)]
    ppermute x2, waiting for transfers between devices: 6.33 us -> 11.1 us  [partner(): lax.ppermute(value, axis, [(i, i ^ flip) for i in range(lax.axis_size(axi...]
    pallas_call x4 -> x2, Pallas kernels: 2.78 us -> 1.89 us  [the longest x1 1.06 us: body(): small(pack_kernel, ((rank, rows + TILE), I16), ((half, cols + TILE), I16))]
  transfers between devices with their start and end apart: 4 -> 4, of which waited for: 2 -> 3; matrix products, arithmetic and copies ran while one was open for 0% -> 0% of each run, Pallas kernels for 1% -> 0%
where the time goes in v11:
time: 93.4 us; the launch traced here: 92.1 us
  blocking collectives  44.7 us (48%)
  starting transfers between devices  25.6 us (27%)
  waiting for transfers between devices  12.1 us (13%)
  Pallas kernels  8.33 us (9%)
    all_to_all x2, blocking collectives, body(): exchange = lambda value, axis: lax.all_to_all(value, axis, 0, 0, tiled=True)  39.9 us
    all_to_all x2, starting transfers between devices, body(): exchange = lambda value, axis: lax.all_to_all(value, axis, 0, 0, tiled=True)  17 us
    ppermute x2, waiting for transfers between devices, partner(): lax.ppermute(value, axis, [(i, i ^ flip) for i in range(lax.axis_size(axi...  11.1 us
    ppermute x2, starting transfers between devices, partner(): lax.ppermute(value, axis, [(i, i ^ flip) for i in range(lax.axis_size(axi...  8.59 us
    pallas_call x1, Pallas kernels, body(): pl.pallas_call(fused_kernel, grid=(cols // width,), in_specs=[tall(rows),...  4.32 us
    all_gather x1, blocking collectives, body(): codes = lax.all_gather(codes, 'c', axis=0, tiled=True)  2.4 us
    all_gather x1, blocking collectives, body(): full = lax.all_gather(arrived, 'c', axis=0, tiled=True)  2.36 us
  transfers between devices with their start and end apart: 4, of which 3 were waited for; matrix products, arithmetic and copies ran while one was open for 0% of the time, Pallas kernels for 0%

profile of v11, /device:TPU:6, one launch (start us, length us, event | category | flops | bytes accessed | tf_op | source)
XLA Modules:
  0.0 92.1 jit_solution(8802251530736388336)
XLA Ops:
  0.6 0.0 copy-start
  0.6 0.7 copy-done
  1.4 0.7 shard_map.86
  2.1 9.4 %all-to-all-start = ((bf16[16,16,512]{2,1,0:T(8,128)(2,1)}), bf16[16,16,512]{2,1,0:T(8,128)(2,1)S(1)}, u32[]{:S(2)}, u32[]{:S(2)}) async-start(bf16[16,16,512]{2,1,0:T(8,128)(2,1)} %shard_map.86), calls=%async_computation | async-start | bytes 524288 | tf_op jit(solution)/shard_map/all_to_all | solution.py:167
  11.4 3.6 %collective-permute-start = (bf16[8,1536]{1,0:T(8,128)(2,1)}, bf16[8,1536]{1,0:T(8,128)(2,1)S(1)}, u32[]{:S(2)}, u32[]{:S(2)}) collective-permute-start(bf16[8,1536]{1,0:T(8,128)(2,1)} %mine_ref.1), channel_id=1, source_target_pairs={{0,256},{256,0},{1,257},{257,1},{2,258},{258,2},{3,259},{259,3},{4... | collective-permute-start | bytes 73736 | tf_op jit(solution)/shard_map/ppermute | solution.py:18
  15.1 6.3 %collective-permute-done.other_ref = bf16[8,1536]{1,0:T(8,128)(2,1)S(1)} collective-permute-done((bf16[8,1536]{1,0:T(8,128)(2,1)}, bf16[8,1536]{1,0:T(8,128)(2,1)S(1)}, u32[]{:S(2)}, u32[]{:S(2)}) %collective-permute-start) | collective-permute-done | bytes 24608 | tf_op jit(solution)/shard_map/ppermute | solution.py:18
  21.4 0.0 all-to-all-done
  21.4 0.8 shard_map.87
  22.2 21.6 %all_to_all.20 = bf16[8,16,1536]{2,1,0:T(8,128)(2,1)S(1)} all-to-all(bf16[8,16,1536]{2,1,0:T(8,128)(2,1)S(1)} %shard_map.87), channel_id=1, replica_groups=mesh['yh'=2,'z'=8,'c'=2,'x'=4,'yl'=4] {'z'}, dimensions={0} | all-to-all | bytes 786432 | tf_op jit(solution)/shard_map/all_to_all | solution.py:167
  43.7 2.4 %all_gather.6.full_ref = bf16[256,1536]{1,0:T(8,128)(2,1)S(1)} all-gather(bf16[128,1536]{1,0:T(8,128)(2,1)S(1)} %bitcast.15), channel_id=1, replica_groups=mesh['yh'=2,'z'=8,'c'=2,'x'=4,'yl'=4] {'c'}, dimensions={0}, use_global_device_ids=true | all-gather | bytes 1179648 | tf_op jit(solution)/shard_map/all_gather | solution.py:176
  46.1 0.0 copy-done.1
  46.1 0.0 copy-done.2
  46.1 0.0 copy-done.3
  46.1 4.3 %shard_map.88 = (f32[128,1536]{1,0:T(8,128)S(1)}, f32[128,1536]{1,0:T(8,128)S(1)}, f32[256,512]{1,0:T(8,128)S(1)}) custom-call(bf16[512,1536]{1,0:T(8,128)(2,1)S(1)} %copy-done.1, bf16[512,1536]{1,0:T(8,128)(2,1)S(1)} %copy-done.2, s32[12,512]{1,0:T(8,128)S(1)} %bitcast.14, bf16[256,512]{1,0:T(8,128)(2,1)S(1)} %bitcast.12, bf16[512,256]{1,0:T(8,128)(2,1)} %coef_ref.1, ...), custom_call_target="tpu_custom_call" | custom-call | flops 1610612736 | bytes 4718592 | tf_op jit(solution)/shard_map/pallas_call | solution.py:181
  50.4 1.1 %shard_map.89 = (s16[256,640]{1,0:T(8,128)(2,1)}, s16[128,1664]{1,0:T(8,128)(2,1)S(1)}) custom-call(f32[256,512]{1,0:T(8,128)S(1)} %get-tuple-element.18.term_ref, f32[128,1536]{1,0:T(8,128)S(1)} %get-tuple-element.19.other_ref), custom_call_target="tpu_custom_call" | custom-call | tf_op jit(solution)/shard_map/pallas_call | solution.py:201
  51.5 2.4 %all_gather.7.both_ref = s16[256,1664]{1,0:T(8,128)(2,1)S(1)} all-gather(s16[128,1664]{1,0:T(8,128)(2,1)S(1)} %get-tuple-element.20), channel_id=1, replica_groups=mesh['yh'=2,'z'=8,'c'=2,'x'=4,'yl'=4] {'c'}, dimensions={0}, use_global_device_ids=true | all-gather | bytes 1277952 | tf_op jit(solution)/shard_map/all_gather | solution.py:204
  53.9 0.4 shard_map.90
  54.3 18.4 %all_to_all.21 = s16[8,16,1664]{2,1,0:T(8,128)(2,1)S(1)} all-to-all(s16[8,16,1664]{2,1,0:T(8,128)(2,1)S(1)} %bitcast.10), channel_id=1, replica_groups=mesh['yh'=2,'z'=8,'c'=2,'x'=4,'yl'=4] {'z'}, dimensions={0} | all-to-all | bytes 851968 | tf_op jit(solution)/shard_map/all_to_all | solution.py:167
  72.6 7.6 %all-to-all-start.3 = ((s16[16,16,640]{2,1,0:T(8,128)(2,1)}), s16[16,16,640]{2,1,0:T(8,128)(2,1)S(1)}, u32[]{:S(2)}, u32[]{:S(2)}) async-start(s16[16,16,640]{2,1,0:T(8,128)(2,1)} %bitcast.6), calls=%async_computation.3 | async-start | bytes 655360 | tf_op jit(solution)/shard_map/all_to_all | solution.py:167
  80.2 0.3 shard_map.91
  80.5 5.0 %collective-permute-start.1 = (s16[8,1664]{1,0:T(8,128)(2,1)S(1)}, s16[8,1664]{1,0:T(8,128)(2,1)S(1)}, u32[]{:S(2)}, u32[]{:S(2)}) collective-permute-start(s16[8,1664]{1,0:T(8,128)(2,1)S(1)} %get-tuple-element.25), channel_id=1, source_target_pairs={{0,256},{256,0},{1,257},{257,1},{2,258},{258,2},{3,259},{259,3},{4... | collective-permute-start | bytes 79880 | tf_op jit(solution)/shard_map/ppermute | solution.py:18
  85.5 4.8 %collective-permute-done.1.came_ref = s16[8,1664]{1,0:T(8,128)(2,1)S(1)} collective-permute-done((s16[8,1664]{1,0:T(8,128)(2,1)S(1)}, s16[8,1664]{1,0:T(8,128)(2,1)S(1)}, u32[]{:S(2)}, u32[]{:S(2)}) %collective-permute-start.1) | collective-permute-done | bytes 26656 | tf_op jit(solution)/shard_map/ppermute | solution.py:18
  90.3 1.0 %all-to-all-done.3 = s16[16,16,640]{2,1,0:T(8,128)(2,1)S(1)} async-done(((s16[16,16,640]{2,1,0:T(8,128)(2,1)}), s16[16,16,640]{2,1,0:T(8,128)(2,1)S(1)}, u32[]{:S(2)}, u32[]{:S(2)}) %all-to-all-start.3) | async-done | bytes 327712 | tf_op jit(solution)/shard_map/all_to_all | solution.py:167
  91.3 0.8 shard_map.92
  (3 shorter events, 0.0 us)
Async XLA Ops:
  0.6 0.7 copy-start
  1.3 44.7 %copy-start.1 = (bf16[512,1536]{1,0:T(8,128)(2,1)S(1)}, bf16[512,1536]{1,0:T(8,128)(2,1)}, u32[]{:S(2)}) copy-start(bf16[512,1536]{1,0:T(8,128)(2,1)} %trans_ref.1) | copy-start | bytes 4718596
  1.4 44.7 %copy-start.2 = (bf16[512,1536]{1,0:T(8,128)(2,1)S(1)}, bf16[512,1536]{1,0:T(8,128)(2,1)}, u32[]{:S(2)}) copy-start(bf16[512,1536]{1,0:T(8,128)(2,1)} %ivar_ref.1) | copy-start | bytes 4718596
  1.4 44.7 %copy-start.3 = (s32[512,12]{0,1:T(8,128)S(1)}, s32[512,12]{0,1:T(8,128)}, u32[]{:S(2)}) copy-start(s32[512,12]{0,1:T(8,128)} %param.9) | copy-start | bytes 73732
  2.1 19.3 %all-to-all-start = ((bf16[16,16,512]{2,1,0:T(8,128)(2,1)}), bf16[16,16,512]{2,1,0:T(8,128)(2,1)S(1)}, u32[]{:S(2)}, u32[]{:S(2)}) async-start(bf16[16,16,512]{2,1,0:T(8,128)(2,1)} %shard_map.86), calls=%async_computation | async-start | bytes 524288 | tf_op jit(solution)/shard_map/all_to_all | solution.py:167
  11.4 10.0 %collective-permute-start = (bf16[8,1536]{1,0:T(8,128)(2,1)}, bf16[8,1536]{1,0:T(8,128)(2,1)S(1)}, u32[]{:S(2)}, u32[]{:S(2)}) collective-permute-start(bf16[8,1536]{1,0:T(8,128)(2,1)} %mine_ref.1), channel_id=1, source_target_pairs={{0,256},{256,0},{1,257},{257,1},{2,258},{258,2},{3,259},{259,3},{4... | collective-permute-start | bytes 73736 | tf_op jit(solution)/shard_map/ppermute | solution.py:18
  72.6 18.7 %all-to-all-start.3 = ((s16[16,16,640]{2,1,0:T(8,128)(2,1)}), s16[16,16,640]{2,1,0:T(8,128)(2,1)S(1)}, u32[]{:S(2)}, u32[]{:S(2)}) async-start(s16[16,16,640]{2,1,0:T(8,128)(2,1)} %bitcast.6), calls=%async_computation.3 | async-start | bytes 655360 | tf_op jit(solution)/shard_map/all_to_all | solution.py:167
  80.5 9.8 %collective-permute-start.1 = (s16[8,1664]{1,0:T(8,128)(2,1)S(1)}, s16[8,1664]{1,0:T(8,128)(2,1)S(1)}, u32[]{:S(2)}, u32[]{:S(2)}) collective-permute-start(s16[8,1664]{1,0:T(8,128)(2,1)S(1)} %get-tuple-element.25), channel_id=1, source_target_pairs={{0,256},{256,0},{1,257},{257,1},{2,258},{258,2},{3,259},{259,3},{4... | collective-permute-start | bytes 79880 | tf_op jit(solution)/shard_map/ppermute | solution.py:18

commit v12 on v11

--- a/solution.py
+++ b/solution.py
@@ -28,7 +28,7 @@
 
 def fused_kernel(
     trans_ref, ivar_ref, mask_ref, tangent_ref, coef_ref, full_ref, basis_ref,
-    own_ref, other_ref, term_ref, coef_p_ref, coef_t_ref,
+    own_ref, other_ref, weighted_ref, coef_p_ref, coef_t_ref,
 ):
     step = pl.program_id(0)
 
@@ -59,23 +59,13 @@
         weights = trans * trans * ivar_ref[:, part].astype(F32) * column
         parts.append((weights * moved[:, part]).astype(BF16))
     weighted = jnp.concatenate(parts, axis=1)
+    weighted_ref[...] = weighted
 
     half = own_ref.shape[0]
     core = lax.axis_index("c")
     for out, which in ((own_ref, core), (other_ref, 1 - core)):
         rows = block_of(coef_t_ref, which, half)
         out[...] = jnp.dot(rows, weighted, preferred_element_type=F32)
-    term = lax.dot_general(
-        basis_ref[...], weighted, (((1,), (1,)), ((), ())), preferred_element_type=F32
-    )
-
-    @pl.when(step == 0)
-    def _():
-        term_ref[...] = term
-
-    @pl.when(step > 0)
-    def _():
-        term_ref[...] += term
 
 
 def encode(total, out_ref):
@@ -122,9 +112,15 @@
         out_ref[i] = pair
 
 
-def pack_kernel(term_ref, other_ref, term_codes_ref, other_codes_ref):
-    encode(term_ref[...], term_codes_ref)
-    encode(other_ref[...], other_codes_ref)
+def pack_kernel(other_ref, out_ref):
+    encode(other_ref[...], out_ref)
+
+
+def term_kernel(basis_ref, weighted_ref, out_ref):
+    term = lax.dot_general(
+        basis_ref[...], weighted_ref[...], (((1,), (1,)), ((), ())), preferred_element_type=F32
+    )
+    encode(term, out_ref)
 
 
 def add_kernel(own_ref, both_ref, out_ref):
@@ -167,7 +163,11 @@
     exchange = lambda value, axis: lax.all_to_all(value, axis, 0, 0, tiled=True)
 
     across = partner(basis_tangent, "yh", 1)
-    [tangent] = small(spread_kernel, ((16, ours, rows), BF16))(coef_tangent.T)
+    tangent = pl.pallas_call(
+        spread_kernel,
+        out_shape=pltpu.HBM((16, ours, rows), BF16),
+        compiler_params=pltpu.CompilerParams(vmem_limit_bytes=8 << 20),
+    )(coef_tangent.T)
     tangent = exchange(tangent, ("x", "yl")).reshape(rank, rows)
     across, tangent = lax.optimization_barrier((across, tangent))
 
@@ -178,32 +178,38 @@
     width = cols // 2
     whole = lambda *shape: pl.BlockSpec(shape, lambda i: (0,) * len(shape))
     tall = lambda n: pl.BlockSpec((n, width), lambda i: (0, i))
-    own, other, term = pl.pallas_call(
+    own, other, weighted = pl.pallas_call(
         fused_kernel,
         grid=(cols // width,),
         in_specs=[
             tall(rows), tall(rows), whole(cols // TILE, rows), whole(rank, rows),
             whole(rows, rank), tall(rank), tall(rank),
         ],
-        out_specs=[tall(half), tall(half), whole(rank, rows)],
+        out_specs=[tall(half), tall(half), tall(rows)],
         out_shape=[
             jax.ShapeDtypeStruct((half, cols), F32),
             jax.ShapeDtypeStruct((half, cols), F32),
-            jax.ShapeDtypeStruct((rank, rows), F32),
+            pltpu.HBM((rows, cols), BF16),
         ],
         scratch_shapes=[pltpu.VMEM((rows, rank), BF16), pltpu.VMEM((rank, rows), BF16)],
         compiler_params=pltpu.CompilerParams(vmem_limit_bytes=16 << 20),
         cost_estimate=pl.CostEstimate(
-            flops=8 * rows * cols * rank, bytes_accessed=6 * rows * cols, transcendentals=0
+            flops=6 * rows * cols * rank, bytes_accessed=6 * rows * cols, transcendentals=0
         ),
     )(transmission, inverse_var, pixel_mask.T, tangent, in_hbm(coef), full, in_hbm(basis))
 
-    terms, codes = small(
-        pack_kernel, ((rank, rows + TILE), I16), ((half, cols + TILE), I16)
-    )(term, other)
+    [codes] = small(pack_kernel, ((half, cols + TILE), I16))(other)
     codes = lax.all_gather(codes, "c", axis=0, tiled=True)
     [codes] = small(add_kernel, ((half, cols + TILE), I16))(own, codes)
     codes = exchange(codes.reshape(8, 2 * mine, cols + TILE), "z").reshape(half, cols + TILE)
+    terms = pl.pallas_call(
+        term_kernel,
+        out_shape=jax.ShapeDtypeStruct((rank, rows + TILE), I16),
+        compiler_params=pltpu.CompilerParams(vmem_limit_bytes=16 << 20),
+        cost_estimate=pl.CostEstimate(
+            flops=2 * rows * cols * rank, bytes_accessed=4 * rows * cols, transcendentals=0
+        ),
+    )(in_hbm(basis), in_hbm(weighted))
     codes, terms = lax.optimization_barrier((codes, terms))
 
     keep, give = small(halve_kernel, ((mine, cols), F32), ((mine, cols + TILE), I16))(codes)

time: 93.4 us -> 94.7 us (1.014)
  blocking collectives: 44.7 us -> 26.3 us
  waiting for transfers between devices: 12.1 us -> 24.8 us
  Pallas kernels: 8.33 us -> 11.9 us
  starting transfers between devices: 25.6 us -> 29 us
    all_to_all x2 -> x1, blocking collectives: 39.9 us -> 21.6 us  [body(): exchange = lambda value, axis: lax.all_to_all(value, axis, 0, 0, tiled=True)]
    all_to_all x2 -> x3, waiting for transfers between devices: 1.04 us -> 13.7 us  [body(): exchange = lambda value, axis: lax.all_to_all(value, axis, 0, 0, tiled=True)]
    all_to_all x2 -> x3, starting transfers between devices: 17 us -> 20.4 us  [body(): exchange = lambda value, axis: lax.all_to_all(value, axis, 0, 0, tiled=True)]
    pallas_call x2 -> x3, Pallas kernels: 1.78 us -> 4.24 us  [the longest x1 3.25 us: body(): pl.pallas_call(term_kernel, out_shape=jax.ShapeDtypeStruct((rank, rows +...]
  transfers between devices with their start and end apart: 4 -> 5, of which waited for: 3 -> 4; matrix products, arithmetic and copies ran while one was open for 0% -> 0% of each run, Pallas kernels for 0% -> 4%
where the time goes in v12:
time: 94.7 us; the launch traced here: 93.4 us
  starting transfers between devices  29 us (31%)
  blocking collectives  26.3 us (28%)
  waiting for transfers between devices  24.8 us (26%)
  Pallas kernels  11.9 us (13%)
    all_to_all x1, blocking collectives, body(): exchange = lambda value, axis: lax.all_to_all(value, axis, 0, 0, tiled=True)  21.6 us
    all_to_all x3, starting transfers between devices, body(): exchange = lambda value, axis: lax.all_to_all(value, axis, 0, 0, tiled=True)  20.4 us
    all_to_all x3, waiting for transfers between devices, body(): exchange = lambda value, axis: lax.all_to_all(value, axis, 0, 0, tiled=True)  13.7 us
    ppermute x2, waiting for transfers between devices, partner(): lax.ppermute(value, axis, [(i, i ^ flip) for i in range(lax.axis_size(axi...  11.1 us
    ppermute x2, starting transfers between devices, partner(): lax.ppermute(value, axis, [(i, i ^ flip) for i in range(lax.axis_size(axi...  8.59 us
    pallas_call x1, Pallas kernels, body(): pl.pallas_call(fused_kernel, grid=(cols // width,), in_specs=[tall(rows),...  4.64 us
    pallas_call x1, Pallas kernels, body(): pl.pallas_call(term_kernel, out_shape=jax.ShapeDtypeStruct((rank, rows +...  3.25 us
    all_gather x1, blocking collectives, body(): codes = lax.all_gather(codes, 'c', axis=0, tiled=True)  2.42 us
  transfers between devices with their start and end apart: 5, of which 4 were waited for; matrix products, arithmetic and copies ran while one was open for 0% of the time, Pallas kernels for 4%

profile of v12, /device:TPU:6, one launch (start us, length us, event | category | flops | bytes accessed | tf_op | source)
XLA Modules:
  0.0 93.4 jit_solution(14561884331784417361)
XLA Ops:
  0.6 0.0 copy-start.3
  0.6 0.7 copy-done.3
  1.4 0.7 shard_map.86
  2.1 9.4 %all-to-all-start = ((bf16[16,16,512]{2,1,0:T(8,128)(2,1)}), bf16[16,16,512]{2,1,0:T(8,128)(2,1)S(1)}, u32[]{:S(2)}, u32[]{:S(2)}) async-start(bf16[16,16,512]{2,1,0:T(8,128)(2,1)} %shard_map.86), calls=%async_computation | async-start | bytes 524288 | tf_op jit(solution)/shard_map/all_to_all | solution.py:163
  11.5 3.6 %collective-permute-start = (bf16[8,1536]{1,0:T(8,128)(2,1)}, bf16[8,1536]{1,0:T(8,128)(2,1)S(1)}, u32[]{:S(2)}, u32[]{:S(2)}) collective-permute-start(bf16[8,1536]{1,0:T(8,128)(2,1)} %mine_ref.1), channel_id=1, source_target_pairs={{0,256},{256,0},{1,257},{257,1},{2,258},{258,2},{3,259},{259,3},{4... | collective-permute-start | bytes 73736 | tf_op jit(solution)/shard_map/ppermute | solution.py:18
  15.1 6.3 %collective-permute-done.other_ref = bf16[8,1536]{1,0:T(8,128)(2,1)S(1)} collective-permute-done((bf16[8,1536]{1,0:T(8,128)(2,1)}, bf16[8,1536]{1,0:T(8,128)(2,1)S(1)}, u32[]{:S(2)}, u32[]{:S(2)}) %collective-permute-start) | collective-permute-done | bytes 24608 | tf_op jit(solution)/shard_map/ppermute | solution.py:18
  21.4 0.0 all-to-all-done
  21.4 0.8 shard_map.87
  22.2 21.6 %all_to_all.20 = bf16[8,16,1536]{2,1,0:T(8,128)(2,1)S(1)} all-to-all(bf16[8,16,1536]{2,1,0:T(8,128)(2,1)S(1)} %shard_map.87), channel_id=1, replica_groups=mesh['yh'=2,'z'=8,'c'=2,'x'=4,'yl'=4] {'z'}, dimensions={0} | all-to-all | bytes 786432 | tf_op jit(solution)/shard_map/all_to_all | solution.py:163
  43.7 2.4 %all_gather.6.full_ref = bf16[256,1536]{1,0:T(8,128)(2,1)S(1)} all-gather(bf16[128,1536]{1,0:T(8,128)(2,1)S(1)} %bitcast.14), channel_id=1, replica_groups=mesh['yh'=2,'z'=8,'c'=2,'x'=4,'yl'=4] {'c'}, dimensions={0}, use_global_device_ids=true | all-gather | bytes 1179648 | tf_op jit(solution)/shard_map/all_gather | solution.py:176
  46.1 0.0 copy-done
  46.1 4.6 %shard_map.88 = (f32[128,1536]{1,0:T(8,128)S(1)}, f32[128,1536]{1,0:T(8,128)S(1)}, bf16[512,1536]{1,0:T(8,128)(2,1)}) custom-call(bf16[512,1536]{1,0:T(8,128)(2,1)S(1)} %copy-done, bf16[512,1536]{1,0:T(8,128)(2,1)S(1)} %copy-done.1, s32[12,512]{1,0:T(8,128)S(1)} %bitcast.12, bf16[256,512]{1,0:T(8,128)(2,1)S(1)} %bitcast.11, bf16[512,256]{1,0:T(8,128)(2,1)} %coef_ref.1, ...), custom_call_target="tpu_custom_call" | custom-call | flops 1207959552 | bytes 4718592 | tf_op jit(solution)/shard_map/pallas_call | solution.py:181
  50.8 0.3 shard_map.89
  51.0 2.4 %all_gather.7.both_ref = s16[256,1664]{1,0:T(8,128)(2,1)S(1)} all-gather(s16[128,1664]{1,0:T(8,128)(2,1)S(1)} %shard_map.89), channel_id=1, replica_groups=mesh['yh'=2,'z'=8,'c'=2,'x'=4,'yl'=4] {'c'}, dimensions={0}, use_global_device_ids=true | all-gather | bytes 1277952 | tf_op jit(solution)/shard_map/all_gather | solution.py:202
  53.4 1.1 %shard_map.90 = s16[128,1664]{1,0:T(8,128)(2,1)} custom-call(f32[128,1536]{1,0:T(8,128)S(1)} %get-tuple-element.15.own_ref, s16[256,1664]{1,0:T(8,128)(2,1)S(1)} %all_gather.7.both_ref), custom_call_target="tpu_custom_call" | custom-call | tf_op jit(solution)/shard_map/pallas_call | solution.py:203
  54.6 3.5 %all-to-all-start.2 = ((s16[8,16,1664]{2,1,0:T(8,128)(2,1)}), s16[8,16,1664]{2,1,0:T(8,128)(2,1)S(1)}, u32[]{:S(2)}, u32[]{:S(2)}) async-start(s16[8,16,1664]{2,1,0:T(8,128)(2,1)} %bitcast.4), calls=%async_computation.2 | async-start | bytes 851968 | tf_op jit(solution)/shard_map/all_to_all | solution.py:163
  58.0 3.3 %shard_map.91 = s16[256,640]{1,0:T(8,128)(2,1)} custom-call(bf16[256,1536]{1,0:T(8,128)(2,1)} %basis_ref.3, bf16[512,1536]{1,0:T(8,128)(2,1)} %get-tuple-element.17.weighted_ref), custom_call_target="tpu_custom_call" | custom-call | flops 402653184 | bytes 3145728 | tf_op jit(solution)/shard_map/pallas_call | solution.py:205
  61.3 12.6 %all-to-all-done.2 = s16[8,16,1664]{2,1,0:T(8,128)(2,1)S(1)} async-done(((s16[8,16,1664]{2,1,0:T(8,128)(2,1)}), s16[8,16,1664]{2,1,0:T(8,128)(2,1)S(1)}, u32[]{:S(2)}, u32[]{:S(2)}) %all-to-all-start.2) | async-done | bytes 426016 | tf_op jit(solution)/shard_map/all_to_all | solution.py:163
  73.9 7.6 %all-to-all-start.3 = ((s16[16,16,640]{2,1,0:T(8,128)(2,1)}), s16[16,16,640]{2,1,0:T(8,128)(2,1)S(1)}, u32[]{:S(2)}, u32[]{:S(2)}) async-start(s16[16,16,640]{2,1,0:T(8,128)(2,1)} %bitcast.6), calls=%async_computation.3 | async-start | bytes 655360 | tf_op jit(solution)/shard_map/all_to_all | solution.py:163
  81.5 0.3 shard_map.92
  81.8 5.0 %collective-permute-start.1 = (s16[8,1664]{1,0:T(8,128)(2,1)S(1)}, s16[8,1664]{1,0:T(8,128)(2,1)S(1)}, u32[]{:S(2)}, u32[]{:S(2)}) collective-permute-start(s16[8,1664]{1,0:T(8,128)(2,1)S(1)} %get-tuple-element.21), channel_id=1, source_target_pairs={{0,256},{256,0},{1,257},{257,1},{2,258},{258,2},{3,259},{259,3},{4... | collective-permute-start | bytes 79880 | tf_op jit(solution)/shard_map/ppermute | solution.py:18
  86.8 4.8 %collective-permute-done.1.came_ref = s16[8,1664]{1,0:T(8,128)(2,1)S(1)} collective-permute-done((s16[8,1664]{1,0:T(8,128)(2,1)S(1)}, s16[8,1664]{1,0:T(8,128)(2,1)S(1)}, u32[]{:S(2)}, u32[]{:S(2)}) %collective-permute-start.1) | collective-permute-done | bytes 26656 | tf_op jit(solution)/shard_map/ppermute | solution.py:18
  91.5 1.0 %all-to-all-done.3 = s16[16,16,640]{2,1,0:T(8,128)(2,1)S(1)} async-done(((s16[16,16,640]{2,1,0:T(8,128)(2,1)}), s16[16,16,640]{2,1,0:T(8,128)(2,1)S(1)}, u32[]{:S(2)}, u32[]{:S(2)}) %all-to-all-start.3) | async-done | bytes 327712 | tf_op jit(solution)/shard_map/all_to_all | solution.py:163
  92.6 0.8 shard_map.93
  (5 shorter events, 0.0 us)
Async XLA Ops:
  0.6 0.7 copy-start.3
  1.3 44.8 %copy-start = (bf16[512,1536]{1,0:T(8,128)(2,1)S(1)}, bf16[512,1536]{1,0:T(8,128)(2,1)}, u32[]{:S(2)}) copy-start(bf16[512,1536]{1,0:T(8,128)(2,1)} %trans_ref.1) | copy-start | bytes 4718596
  1.4 44.8 %copy-start.1 = (bf16[512,1536]{1,0:T(8,128)(2,1)S(1)}, bf16[512,1536]{1,0:T(8,128)(2,1)}, u32[]{:S(2)}) copy-start(bf16[512,1536]{1,0:T(8,128)(2,1)} %ivar_ref.1) | copy-start | bytes 4718596
  1.4 44.8 %copy-start.2 = (s32[512,12]{0,1:T(8,128)S(1)}, s32[512,12]{0,1:T(8,128)}, u32[]{:S(2)}) copy-start(s32[512,12]{0,1:T(8,128)} %param.9) | copy-start | bytes 73732
  2.1 19.3 %all-to-all-start = ((bf16[16,16,512]{2,1,0:T(8,128)(2,1)}), bf16[16,16,512]{2,1,0:T(8,128)(2,1)S(1)}, u32[]{:S(2)}, u32[]{:S(2)}) async-start(bf16[16,16,512]{2,1,0:T(8,128)(2,1)} %shard_map.86), calls=%async_computation | async-start | bytes 524288 | tf_op jit(solution)/shard_map/all_to_all | solution.py:163
  11.5 10.0 %collective-permute-start = (bf16[8,1536]{1,0:T(8,128)(2,1)}, bf16[8,1536]{1,0:T(8,128)(2,1)S(1)}, u32[]{:S(2)}, u32[]{:S(2)}) collective-permute-start(bf16[8,1536]{1,0:T(8,128)(2,1)} %mine_ref.1), channel_id=1, source_target_pairs={{0,256},{256,0},{1,257},{257,1},{2,258},{258,2},{3,259},{259,3},{4... | collective-permute-start | bytes 73736 | tf_op jit(solution)/shard_map/ppermute | solution.py:18
  54.6 19.4 %all-to-all-start.2 = ((s16[8,16,1664]{2,1,0:T(8,128)(2,1)}), s16[8,16,1664]{2,1,0:T(8,128)(2,1)S(1)}, u32[]{:S(2)}, u32[]{:S(2)}) async-start(s16[8,16,1664]{2,1,0:T(8,128)(2,1)} %bitcast.4), calls=%async_computation.2 | async-start | bytes 851968 | tf_op jit(solution)/shard_map/all_to_all | solution.py:163
  73.9 18.7 %all-to-all-start.3 = ((s16[16,16,640]{2,1,0:T(8,128)(2,1)}), s16[16,16,640]{2,1,0:T(8,128)(2,1)S(1)}, u32[]{:S(2)}, u32[]{:S(2)}) async-start(s16[16,16,640]{2,1,0:T(8,128)(2,1)} %bitcast.6), calls=%async_computation.3 | async-start | bytes 655360 | tf_op jit(solution)/shard_map/all_to_all | solution.py:163
  81.8 9.8 %collective-permute-start.1 = (s16[8,1664]{1,0:T(8,128)(2,1)S(1)}, s16[8,1664]{1,0:T(8,128)(2,1)S(1)}, u32[]{:S(2)}, u32[]{:S(2)}) collective-permute-start(s16[8,1664]{1,0:T(8,128)(2,1)S(1)} %get-tuple-element.21), channel_id=1, source_target_pairs={{0,256},{256,0},{1,257},{257,1},{2,258},{258,2},{3,259},{259,3},{4... | collective-permute-start | bytes 79880 | tf_op jit(solution)/shard_map/ppermute | solution.py:18

commit v13 on v11

--- a/solution.py
+++ b/solution.py
@@ -175,7 +175,7 @@
     arrived = exchange(pair, "z").reshape(half, cols)
     full = lax.all_gather(arrived, "c", axis=0, tiled=True)
 
-    width = cols // 2
+    width = cols
     whole = lambda *shape: pl.BlockSpec(shape, lambda i: (0,) * len(shape))
     tall = lambda n: pl.BlockSpec((n, width), lambda i: (0, i))
     own, other, term = pl.pallas_call(
@@ -192,7 +192,7 @@
             jax.ShapeDtypeStruct((rank, rows), F32),
         ],
         scratch_shapes=[pltpu.VMEM((rows, rank), BF16), pltpu.VMEM((rank, rows), BF16)],
-        compiler_params=pltpu.CompilerParams(vmem_limit_bytes=16 << 20),
+        compiler_params=pltpu.CompilerParams(vmem_limit_bytes=24 << 20),
         cost_estimate=pl.CostEstimate(
             flops=8 * rows * cols * rank, bytes_accessed=6 * rows * cols, transcendentals=0
         ),

time: 93.4 us -> 92.7 us (level)
  no operation moved by 1% of the time
where the time goes in v13:
time: 92.7 us; the launch traced here: 91.4 us
  blocking collectives  44.7 us (48%)
  starting transfers between devices  25.6 us (28%)
  waiting for transfers between devices  12.1 us (13%)
  Pallas kernels  7.62 us (8%)
    all_to_all x2, blocking collectives, body(): exchange = lambda value, axis: lax.all_to_all(value, axis, 0, 0, tiled=True)  39.9 us
    all_to_all x2, starting transfers between devices, body(): exchange = lambda value, axis: lax.all_to_all(value, axis, 0, 0, tiled=True)  17 us
    ppermute x2, waiting for transfers between devices, partner(): lax.ppermute(value, axis, [(i, i ^ flip) for i in range(lax.axis_size(axi...  11.1 us
    ppermute x2, starting transfers between devices, partner(): lax.ppermute(value, axis, [(i, i ^ flip) for i in range(lax.axis_size(axi...  8.58 us
    pallas_call x1, Pallas kernels, body(): pl.pallas_call(fused_kernel, grid=(cols // width,), in_specs=[tall(rows),...  3.62 us
    all_gather x1, blocking collectives, body(): codes = lax.all_gather(codes, 'c', axis=0, tiled=True)  2.4 us
    all_gather x1, blocking collectives, body(): full = lax.all_gather(arrived, 'c', axis=0, tiled=True)  2.36 us
  transfers between devices with their start and end apart: 4, of which 3 were waited for; matrix products, arithmetic and copies ran while one was open for 0% of the time, Pallas kernels for 0%

profile of v13, /device:TPU:6, one launch (start us, length us, event | category | flops | bytes accessed | tf_op | source)
XLA Modules:
  0.0 91.4 jit_solution(11354345472980601473)
XLA Ops:
  0.6 0.0 copy-start
  0.6 0.7 copy-done
  1.4 0.7 shard_map.86
  2.1 9.4 %all-to-all-start = ((bf16[16,16,512]{2,1,0:T(8,128)(2,1)}), bf16[16,16,512]{2,1,0:T(8,128)(2,1)S(1)}, u32[]{:S(2)}, u32[]{:S(2)}) async-start(bf16[16,16,512]{2,1,0:T(8,128)(2,1)} %shard_map.86), calls=%async_computation | async-start | bytes 524288 | tf_op jit(solution)/shard_map/all_to_all | solution.py:167
  11.4 3.6 %collective-permute-start = (bf16[8,1536]{1,0:T(8,128)(2,1)}, bf16[8,1536]{1,0:T(8,128)(2,1)S(1)}, u32[]{:S(2)}, u32[]{:S(2)}) collective-permute-start(bf16[8,1536]{1,0:T(8,128)(2,1)} %mine_ref.1), channel_id=1, source_target_pairs={{0,256},{256,0},{1,257},{257,1},{2,258},{258,2},{3,259},{259,3},{4... | collective-permute-start | bytes 73736 | tf_op jit(solution)/shard_map/ppermute | solution.py:18
  15.1 6.3 %collective-permute-done.other_ref = bf16[8,1536]{1,0:T(8,128)(2,1)S(1)} collective-permute-done((bf16[8,1536]{1,0:T(8,128)(2,1)}, bf16[8,1536]{1,0:T(8,128)(2,1)S(1)}, u32[]{:S(2)}, u32[]{:S(2)}) %collective-permute-start) | collective-permute-done | bytes 24608 | tf_op jit(solution)/shard_map/ppermute | solution.py:18
  21.4 0.0 all-to-all-done
  21.4 0.8 shard_map.87
  22.2 21.6 %all_to_all.20 = bf16[8,16,1536]{2,1,0:T(8,128)(2,1)S(1)} all-to-all(bf16[8,16,1536]{2,1,0:T(8,128)(2,1)S(1)} %shard_map.87), channel_id=1, replica_groups=mesh['yh'=2,'z'=8,'c'=2,'x'=4,'yl'=4] {'z'}, dimensions={0} | all-to-all | bytes 786432 | tf_op jit(solution)/shard_map/all_to_all | solution.py:167
  43.7 2.4 %all_gather.6.full_ref = bf16[256,1536]{1,0:T(8,128)(2,1)S(1)} all-gather(bf16[128,1536]{1,0:T(8,128)(2,1)S(1)} %bitcast.15), channel_id=1, replica_groups=mesh['yh'=2,'z'=8,'c'=2,'x'=4,'yl'=4] {'c'}, dimensions={0}, use_global_device_ids=true | all-gather | bytes 1179648 | tf_op jit(solution)/shard_map/all_gather | solution.py:176
  46.1 0.0 copy-done.1
  46.1 0.0 copy-done.2
  46.1 0.0 copy-done.3
  46.1 3.6 %shard_map.88 = (f32[128,1536]{1,0:T(8,128)S(1)}, f32[128,1536]{1,0:T(8,128)S(1)}, f32[256,512]{1,0:T(8,128)S(1)}) custom-call(bf16[512,1536]{1,0:T(8,128)(2,1)S(1)} %copy-done.1, bf16[512,1536]{1,0:T(8,128)(2,1)S(1)} %copy-done.2, s32[12,512]{1,0:T(8,128)S(1)} %bitcast.14, bf16[256,512]{1,0:T(8,128)(2,1)S(1)} %bitcast.12, bf16[512,256]{1,0:T(8,128)(2,1)} %coef_ref.1, ...), custom_call_target="tpu_custom_call" | custom-call | flops 1610612736 | bytes 4718592 | tf_op jit(solution)/shard_map/pallas_call | solution.py:181
  49.7 1.1 %shard_map.89 = (s16[256,640]{1,0:T(8,128)(2,1)}, s16[128,1664]{1,0:T(8,128)(2,1)S(1)}) custom-call(f32[256,512]{1,0:T(8,128)S(1)} %get-tuple-element.18.term_ref, f32[128,1536]{1,0:T(8,128)S(1)} %get-tuple-element.19.other_ref), custom_call_target="tpu_custom_call" | custom-call | tf_op jit(solution)/shard_map/pallas_call | solution.py:201
  50.8 2.4 %all_gather.7.both_ref = s16[256,1664]{1,0:T(8,128)(2,1)S(1)} all-gather(s16[128,1664]{1,0:T(8,128)(2,1)S(1)} %get-tuple-element.20), channel_id=1, replica_groups=mesh['yh'=2,'z'=8,'c'=2,'x'=4,'yl'=4] {'c'}, dimensions={0}, use_global_device_ids=true | all-gather | bytes 1277952 | tf_op jit(solution)/shard_map/all_gather | solution.py:204
  53.2 0.4 shard_map.90
  53.6 18.4 %all_to_all.21 = s16[8,16,1664]{2,1,0:T(8,128)(2,1)S(1)} all-to-all(s16[8,16,1664]{2,1,0:T(8,128)(2,1)S(1)} %bitcast.10), channel_id=1, replica_groups=mesh['yh'=2,'z'=8,'c'=2,'x'=4,'yl'=4] {'z'}, dimensions={0} | all-to-all | bytes 851968 | tf_op jit(solution)/shard_map/all_to_all | solution.py:167
  71.9 7.6 %all-to-all-start.3 = ((s16[16,16,640]{2,1,0:T(8,128)(2,1)}), s16[16,16,640]{2,1,0:T(8,128)(2,1)S(1)}, u32[]{:S(2)}, u32[]{:S(2)}) async-start(s16[16,16,640]{2,1,0:T(8,128)(2,1)} %bitcast.6), calls=%async_computation.3 | async-start | bytes 655360 | tf_op jit(solution)/shard_map/all_to_all | solution.py:167
  79.5 0.3 shard_map.91
  79.8 5.0 %collective-permute-start.1 = (s16[8,1664]{1,0:T(8,128)(2,1)S(1)}, s16[8,1664]{1,0:T(8,128)(2,1)S(1)}, u32[]{:S(2)}, u32[]{:S(2)}) collective-permute-start(s16[8,1664]{1,0:T(8,128)(2,1)S(1)} %get-tuple-element.25), channel_id=1, source_target_pairs={{0,256},{256,0},{1,257},{257,1},{2,258},{258,2},{3,259},{259,3},{4... | collective-permute-start | bytes 79880 | tf_op jit(solution)/shard_map/ppermute | solution.py:18
  84.8 4.8 %collective-permute-done.1.came_ref = s16[8,1664]{1,0:T(8,128)(2,1)S(1)} collective-permute-done((s16[8,1664]{1,0:T(8,128)(2,1)S(1)}, s16[8,1664]{1,0:T(8,128)(2,1)S(1)}, u32[]{:S(2)}, u32[]{:S(2)}) %collective-permute-start.1) | collective-permute-done | bytes 26656 | tf_op jit(solution)/shard_map/ppermute | solution.py:18
  89.6 1.0 %all-to-all-done.3 = s16[16,16,640]{2,1,0:T(8,128)(2,1)S(1)} async-done(((s16[16,16,640]{2,1,0:T(8,128)(2,1)}), s16[16,16,640]{2,1,0:T(8,128)(2,1)S(1)}, u32[]{:S(2)}, u32[]{:S(2)}) %all-to-all-start.3) | async-done | bytes 327712 | tf_op jit(solution)/shard_map/all_to_all | solution.py:167
  90.6 0.8 shard_map.92
  (3 shorter events, 0.0 us)
Async XLA Ops:
  0.6 0.7 copy-start
  1.3 44.7 %copy-start.1 = (bf16[512,1536]{1,0:T(8,128)(2,1)S(1)}, bf16[512,1536]{1,0:T(8,128)(2,1)}, u32[]{:S(2)}) copy-start(bf16[512,1536]{1,0:T(8,128)(2,1)} %trans_ref.1) | copy-start | bytes 4718596
  1.4 44.7 %copy-start.2 = (bf16[512,1536]{1,0:T(8,128)(2,1)S(1)}, bf16[512,1536]{1,0:T(8,128)(2,1)}, u32[]{:S(2)}) copy-start(bf16[512,1536]{1,0:T(8,128)(2,1)} %ivar_ref.1) | copy-start | bytes 4718596
  1.4 44.7 %copy-start.3 = (s32[512,12]{0,1:T(8,128)S(1)}, s32[512,12]{0,1:T(8,128)}, u32[]{:S(2)}) copy-start(s32[512,12]{0,1:T(8,128)} %param.9) | copy-start | bytes 73732
  2.1 19.3 %all-to-all-start = ((bf16[16,16,512]{2,1,0:T(8,128)(2,1)}), bf16[16,16,512]{2,1,0:T(8,128)(2,1)S(1)}, u32[]{:S(2)}, u32[]{:S(2)}) async-start(bf16[16,16,512]{2,1,0:T(8,128)(2,1)} %shard_map.86), calls=%async_computation | async-start | bytes 524288 | tf_op jit(solution)/shard_map/all_to_all | solution.py:167
  11.4 10.0 %collective-permute-start = (bf16[8,1536]{1,0:T(8,128)(2,1)}, bf16[8,1536]{1,0:T(8,128)(2,1)S(1)}, u32[]{:S(2)}, u32[]{:S(2)}) collective-permute-start(bf16[8,1536]{1,0:T(8,128)(2,1)} %mine_ref.1), channel_id=1, source_target_pairs={{0,256},{256,0},{1,257},{257,1},{2,258},{258,2},{3,259},{259,3},{4... | collective-permute-start | bytes 73736 | tf_op jit(solution)/shard_map/ppermute | solution.py:18
  71.9 18.7 %all-to-all-start.3 = ((s16[16,16,640]{2,1,0:T(8,128)(2,1)}), s16[16,16,640]{2,1,0:T(8,128)(2,1)S(1)}, u32[]{:S(2)}, u32[]{:S(2)}) async-start(s16[16,16,640]{2,1,0:T(8,128)(2,1)} %bitcast.6), calls=%async_computation.3 | async-start | bytes 655360 | tf_op jit(solution)/shard_map/all_to_all | solution.py:167
  79.8 9.8 %collective-permute-start.1 = (s16[8,1664]{1,0:T(8,128)(2,1)S(1)}, s16[8,1664]{1,0:T(8,128)(2,1)S(1)}, u32[]{:S(2)}, u32[]{:S(2)}) collective-permute-start(s16[8,1664]{1,0:T(8,128)(2,1)S(1)} %get-tuple-element.25), channel_id=1, source_target_pairs={{0,256},{256,0},{1,257},{257,1},{2,258},{258,2},{3,259},{259,3},{4... | collective-permute-start | bytes 79880 | tf_op jit(solution)/shard_map/ppermute | solution.py:18

commit v14 on v13

--- a/solution.py
+++ b/solution.py
@@ -28,7 +28,7 @@
 
 def fused_kernel(
     trans_ref, ivar_ref, mask_ref, tangent_ref, coef_ref, full_ref, basis_ref,
-    own_ref, other_ref, term_ref, coef_p_ref, coef_t_ref,
+    own_ref, other_codes_ref, term_codes_ref, coef_p_ref, coef_t_ref,
 ):
     step = pl.program_id(0)
 
@@ -62,20 +62,15 @@
 
     half = own_ref.shape[0]
     core = lax.axis_index("c")
-    for out, which in ((own_ref, core), (other_ref, 1 - core)):
-        rows = block_of(coef_t_ref, which, half)
-        out[...] = jnp.dot(rows, weighted, preferred_element_type=F32)
+    own_ref[...] = jnp.dot(
+        block_of(coef_t_ref, core, half), weighted, preferred_element_type=F32
+    )
+    other = jnp.dot(block_of(coef_t_ref, 1 - core, half), weighted, preferred_element_type=F32)
+    encode(other, other_codes_ref)
     term = lax.dot_general(
         basis_ref[...], weighted, (((1,), (1,)), ((), ())), preferred_element_type=F32
     )
-
-    @pl.when(step == 0)
-    def _():
-        term_ref[...] = term
-
-    @pl.when(step > 0)
-    def _():
-        term_ref[...] += term
+    encode(term, term_codes_ref)
 
 
 def encode(total, out_ref):
@@ -122,11 +117,6 @@
         out_ref[i] = pair
 
 
-def pack_kernel(term_ref, other_ref, term_codes_ref, other_codes_ref):
-    encode(term_ref[...], term_codes_ref)
-    encode(other_ref[...], other_codes_ref)
-
-
 def add_kernel(own_ref, both_ref, out_ref):
     n = own_ref.shape[0]
     came = pl.ds(pl.multiple_of((1 - lax.axis_index("c")) * n, n), n)
@@ -178,18 +168,18 @@
     width = cols
     whole = lambda *shape: pl.BlockSpec(shape, lambda i: (0,) * len(shape))
     tall = lambda n: pl.BlockSpec((n, width), lambda i: (0, i))
-    own, other, term = pl.pallas_call(
+    own, codes, terms = pl.pallas_call(
         fused_kernel,
         grid=(cols // width,),
         in_specs=[
             tall(rows), tall(rows), whole(cols // TILE, rows), whole(rank, rows),
             whole(rows, rank), tall(rank), tall(rank),
         ],
-        out_specs=[tall(half), tall(half), whole(rank, rows)],
+        out_specs=[tall(half), whole(half, cols + TILE), whole(rank, rows + TILE)],
         out_shape=[
             jax.ShapeDtypeStruct((half, cols), F32),
-            jax.ShapeDtypeStruct((half, cols), F32),
-            jax.ShapeDtypeStruct((rank, rows), F32),
+            jax.ShapeDtypeStruct((half, cols + TILE), I16),
+            jax.ShapeDtypeStruct((rank, rows + TILE), I16),
         ],
         scratch_shapes=[pltpu.VMEM((rows, rank), BF16), pltpu.VMEM((rank, rows), BF16)],
         compiler_params=pltpu.CompilerParams(vmem_limit_bytes=24 << 20),
@@ -198,9 +188,6 @@
         ),
     )(transmission, inverse_var, pixel_mask.T, tangent, in_hbm(coef), full, in_hbm(basis))
 
-    terms, codes = small(
-        pack_kernel, ((rank, rows + TILE), I16), ((half, cols + TILE), I16)
-    )(term, other)
     codes = lax.all_gather(codes, "c", axis=0, tiled=True)
     [codes] = small(add_kernel, ((half, cols + TILE), I16))(own, codes)
     codes = exchange(codes.reshape(8, 2 * mine, cols + TILE), "z").reshape(half, cols + TILE)

time: 92.7 us -> 92.7 us (level)
    pallas_call x1, Pallas kernels: 3.62 us -> 4.76 us  [body(): pl.pallas_call(fused_kernel, grid=(cols // width,), in_specs=[tall(rows),...]
    pallas_call x1 -> x0, Pallas kernels: 1.06 us -> none  [body(): small(pack_kernel, ((rank, rows + TILE), I16), ((half, cols + TILE), I16))]
where the time goes in v14:
time: 92.7 us; the launch traced here: 91.5 us
  blocking collectives  44.7 us (48%)
  starting transfers between devices  25.6 us (28%)
  waiting for transfers between devices  12.1 us (13%)
  Pallas kernels  7.71 us (8%)
    all_to_all x2, blocking collectives, body(): exchange = lambda value, axis: lax.all_to_all(value, axis, 0, 0, tiled=True)  39.9 us
    all_to_all x2, starting transfers between devices, body(): exchange = lambda value, axis: lax.all_to_all(value, axis, 0, 0, tiled=True)  17 us
    ppermute x2, waiting for transfers between devices, partner(): lax.ppermute(value, axis, [(i, i ^ flip) for i in range(lax.axis_size(axi...  11.1 us
    ppermute x2, starting transfers between devices, partner(): lax.ppermute(value, axis, [(i, i ^ flip) for i in range(lax.axis_size(axi...  8.58 us
    pallas_call x1, Pallas kernels, body(): pl.pallas_call(fused_kernel, grid=(cols // width,), in_specs=[tall(rows),...  4.76 us
    all_gather x1, blocking collectives, body(): codes = lax.all_gather(codes, 'c', axis=0, tiled=True)  2.4 us
    all_gather x1, blocking collectives, body(): full = lax.all_gather(arrived, 'c', axis=0, tiled=True)  2.36 us
  transfers between devices with their start and end apart: 4, of which 3 were waited for; matrix products, arithmetic and copies ran while one was open for 0% of the time, Pallas kernels for 0%

profile of v14, /device:TPU:6, one launch (start us, length us, event | category | flops | bytes accessed | tf_op | source)
XLA Modules:
  0.0 91.5 jit_solution(10830787641234252934)
XLA Ops:
  0.6 0.0 copy-start
  0.6 0.7 copy-done
  1.3 0.0 copy-start.1
  1.4 0.7 shard_map.86
  2.1 9.4 %all-to-all-start = ((bf16[16,16,512]{2,1,0:T(8,128)(2,1)}), bf16[16,16,512]{2,1,0:T(8,128)(2,1)S(1)}, u32[]{:S(2)}, u32[]{:S(2)}) async-start(bf16[16,16,512]{2,1,0:T(8,128)(2,1)} %shard_map.86), calls=%async_computation | async-start | bytes 524288 | tf_op jit(solution)/shard_map/all_to_all | solution.py:157
  11.5 3.6 %collective-permute-start = (bf16[8,1536]{1,0:T(8,128)(2,1)}, bf16[8,1536]{1,0:T(8,128)(2,1)S(1)}, u32[]{:S(2)}, u32[]{:S(2)}) collective-permute-start(bf16[8,1536]{1,0:T(8,128)(2,1)} %mine_ref.1), channel_id=1, source_target_pairs={{0,256},{256,0},{1,257},{257,1},{2,258},{258,2},{3,259},{259,3},{4... | collective-permute-start | bytes 73736 | tf_op jit(solution)/shard_map/ppermute | solution.py:18
  15.1 6.3 %collective-permute-done.other_ref = bf16[8,1536]{1,0:T(8,128)(2,1)S(1)} collective-permute-done((bf16[8,1536]{1,0:T(8,128)(2,1)}, bf16[8,1536]{1,0:T(8,128)(2,1)S(1)}, u32[]{:S(2)}, u32[]{:S(2)}) %collective-permute-start) | collective-permute-done | bytes 24608 | tf_op jit(solution)/shard_map/ppermute | solution.py:18
  21.4 0.0 all-to-all-done
  21.4 0.8 shard_map.87
  22.2 21.6 %all_to_all.20 = bf16[8,16,1536]{2,1,0:T(8,128)(2,1)S(1)} all-to-all(bf16[8,16,1536]{2,1,0:T(8,128)(2,1)S(1)} %shard_map.87), channel_id=1, replica_groups=mesh['yh'=2,'z'=8,'c'=2,'x'=4,'yl'=4] {'z'}, dimensions={0} | all-to-all | bytes 786432 | tf_op jit(solution)/shard_map/all_to_all | solution.py:157
  43.7 2.4 %all_gather.6.full_ref = bf16[256,1536]{1,0:T(8,128)(2,1)S(1)} all-gather(bf16[128,1536]{1,0:T(8,128)(2,1)S(1)} %bitcast.15), channel_id=1, replica_groups=mesh['yh'=2,'z'=8,'c'=2,'x'=4,'yl'=4] {'c'}, dimensions={0}, use_global_device_ids=true | all-gather | bytes 1179648 | tf_op jit(solution)/shard_map/all_gather | solution.py:166
  46.1 0.0 copy-done.1
  46.1 0.0 copy-done.2
  46.1 0.0 copy-done.3
  46.1 4.8 %shard_map.88 = (f32[128,1536]{1,0:T(8,128)S(1)}, s16[128,1664]{1,0:T(8,128)(2,1)S(1)}, s16[256,640]{1,0:T(8,128)(2,1)}) custom-call(bf16[512,1536]{1,0:T(8,128)(2,1)S(1)} %copy-done.1, bf16[512,1536]{1,0:T(8,128)(2,1)S(1)} %copy-done.2, s32[12,512]{1,0:T(8,128)S(1)} %bitcast.14, bf16[256,512]{1,0:T(8,128)(2,1)S(1)} %bitcast.12, bf16[512,256]{1,0:T(8,128)(2,1)} %coef_ref.1, ...), custom_call_target="tpu_custom_call" | custom-call | flops 1610612736 | bytes 4718592 | tf_op jit(solution)/shard_map/pallas_call | solution.py:171
  50.9 2.4 %all_gather.7.both_ref = s16[256,1664]{1,0:T(8,128)(2,1)S(1)} all-gather(s16[128,1664]{1,0:T(8,128)(2,1)S(1)} %get-tuple-element.16), channel_id=1, replica_groups=mesh['yh'=2,'z'=8,'c'=2,'x'=4,'yl'=4] {'c'}, dimensions={0}, use_global_device_ids=true | all-gather | bytes 1277952 | tf_op jit(solution)/shard_map/all_gather | solution.py:191
  53.3 0.4 shard_map.89
  53.6 18.4 %all_to_all.21 = s16[8,16,1664]{2,1,0:T(8,128)(2,1)S(1)} all-to-all(s16[8,16,1664]{2,1,0:T(8,128)(2,1)S(1)} %bitcast.10), channel_id=1, replica_groups=mesh['yh'=2,'z'=8,'c'=2,'x'=4,'yl'=4] {'z'}, dimensions={0} | all-to-all | bytes 851968 | tf_op jit(solution)/shard_map/all_to_all | solution.py:157
  72.0 7.6 %all-to-all-start.3 = ((s16[16,16,640]{2,1,0:T(8,128)(2,1)}), s16[16,16,640]{2,1,0:T(8,128)(2,1)S(1)}, u32[]{:S(2)}, u32[]{:S(2)}) async-start(s16[16,16,640]{2,1,0:T(8,128)(2,1)} %bitcast.6), calls=%async_computation.3 | async-start | bytes 655360 | tf_op jit(solution)/shard_map/all_to_all | solution.py:157
  79.6 0.3 shard_map.90
  79.9 5.0 %collective-permute-start.1 = (s16[8,1664]{1,0:T(8,128)(2,1)S(1)}, s16[8,1664]{1,0:T(8,128)(2,1)S(1)}, u32[]{:S(2)}, u32[]{:S(2)}) collective-permute-start(s16[8,1664]{1,0:T(8,128)(2,1)S(1)} %get-tuple-element.21), channel_id=1, source_target_pairs={{0,256},{256,0},{1,257},{257,1},{2,258},{258,2},{3,259},{259,3},{4... | collective-permute-start | bytes 79880 | tf_op jit(solution)/shard_map/ppermute | solution.py:18
  84.9 4.8 %collective-permute-done.1.came_ref = s16[8,1664]{1,0:T(8,128)(2,1)S(1)} collective-permute-done((s16[8,1664]{1,0:T(8,128)(2,1)S(1)}, s16[8,1664]{1,0:T(8,128)(2,1)S(1)}, u32[]{:S(2)}, u32[]{:S(2)}) %collective-permute-start.1) | collective-permute-done | bytes 26656 | tf_op jit(solution)/shard_map/ppermute | solution.py:18
  89.6 1.0 %all-to-all-done.3 = s16[16,16,640]{2,1,0:T(8,128)(2,1)S(1)} async-done(((s16[16,16,640]{2,1,0:T(8,128)(2,1)}), s16[16,16,640]{2,1,0:T(8,128)(2,1)S(1)}, u32[]{:S(2)}, u32[]{:S(2)}) %all-to-all-start.3) | async-done | bytes 327712 | tf_op jit(solution)/shard_map/all_to_all | solution.py:157
  90.7 0.8 shard_map.91
  (2 shorter events, 0.0 us)
Async XLA Ops:
  0.6 0.7 copy-start
  1.3 44.8 %copy-start.1 = (bf16[512,1536]{1,0:T(8,128)(2,1)S(1)}, bf16[512,1536]{1,0:T(8,128)(2,1)}, u32[]{:S(2)}) copy-start(bf16[512,1536]{1,0:T(8,128)(2,1)} %trans_ref.1) | copy-start | bytes 4718596
  1.4 44.8 %copy-start.2 = (bf16[512,1536]{1,0:T(8,128)(2,1)S(1)}, bf16[512,1536]{1,0:T(8,128)(2,1)}, u32[]{:S(2)}) copy-start(bf16[512,1536]{1,0:T(8,128)(2,1)} %ivar_ref.1) | copy-start | bytes 4718596
  1.4 44.8 %copy-start.3 = (s32[512,12]{0,1:T(8,128)S(1)}, s32[512,12]{0,1:T(8,128)}, u32[]{:S(2)}) copy-start(s32[512,12]{0,1:T(8,128)} %param.9) | copy-start | bytes 73732
  2.1 19.3 %all-to-all-start = ((bf16[16,16,512]{2,1,0:T(8,128)(2,1)}), bf16[16,16,512]{2,1,0:T(8,128)(2,1)S(1)}, u32[]{:S(2)}, u32[]{:S(2)}) async-start(bf16[16,16,512]{2,1,0:T(8,128)(2,1)} %shard_map.86), calls=%async_computation | async-start | bytes 524288 | tf_op jit(solution)/shard_map/all_to_all | solution.py:157
  11.5 10.0 %collective-permute-start = (bf16[8,1536]{1,0:T(8,128)(2,1)}, bf16[8,1536]{1,0:T(8,128)(2,1)S(1)}, u32[]{:S(2)}, u32[]{:S(2)}) collective-permute-start(bf16[8,1536]{1,0:T(8,128)(2,1)} %mine_ref.1), channel_id=1, source_target_pairs={{0,256},{256,0},{1,257},{257,1},{2,258},{258,2},{3,259},{259,3},{4... | collective-permute-start | bytes 73736 | tf_op jit(solution)/shard_map/ppermute | solution.py:18
  72.0 18.7 %all-to-all-start.3 = ((s16[16,16,640]{2,1,0:T(8,128)(2,1)}), s16[16,16,640]{2,1,0:T(8,128)(2,1)S(1)}, u32[]{:S(2)}, u32[]{:S(2)}) async-start(s16[16,16,640]{2,1,0:T(8,128)(2,1)} %bitcast.6), calls=%async_computation.3 | async-start | bytes 655360 | tf_op jit(solution)/shard_map/all_to_all | solution.py:157
  79.9 9.8 %collective-permute-start.1 = (s16[8,1664]{1,0:T(8,128)(2,1)S(1)}, s16[8,1664]{1,0:T(8,128)(2,1)S(1)}, u32[]{:S(2)}, u32[]{:S(2)}) collective-permute-start(s16[8,1664]{1,0:T(8,128)(2,1)S(1)} %get-tuple-element.21), channel_id=1, source_target_pairs={{0,256},{256,0},{1,257},{257,1},{2,258},{258,2},{3,259},{259,3},{4... | collective-permute-start | bytes 79880 | tf_op jit(solution)/shard_map/ppermute | solution.py:18
